TPU v7x, 32 devices: a whole 2x2x4 slice. The times are simulated.
32 devices in a mesh: slab: 8 (over z, y), chan: 4 (over x, core).
Axes of the slice: x: 2, y: 2, z: 4, core: 2. Of those that a mesh axis runs over, the one named last changes fastest.
Arguments:
- volume: bfloat16 [2, 32, 128, 32, 128], P(None, 'slab', 'chan'), may hold values from -6 to 6
- first_kernel: bfloat16 [3, 3, 3, 128, 128], P(None, None, None, None, 'chan'), may hold values from -0.109375 to 0.109375
- first_bias: float32 [128], P('chan'), may hold values from -3 to 3
- second_kernel: bfloat16 [3, 3, 3, 128, 128], P(None, None, None, 'chan'), may hold values from -0.109375 to 0.109375
- second_bias: float32 [128], P('chan'), may hold values from -3 to 3
Outputs:
- features_out: bfloat16 [2, 32, 128, 32, 128], P(None, 'slab', 'chan')
All inputs are finite; a program needn't handle non-finite values.
Results may differ from a plain program's by a relative error of at most 0.0046.
Values may be sent and summed in bfloat16 or wider, within the bound.
No kernel may reach another device: no remote copies, remote signals or barrier semaphores. Data moves between devices by JAX's collectives and lax.ppermute only.
A program may use at most 128 MiB of HBM per device.

v0:
```python
import jax
import jax.numpy as jnp
from jax import lax
from jax.sharding import PartitionSpec as P

layout_spec = ("NDCHW", "DHWIO", "NDCHW")


def padded(shard, sides, width):
    for axis, dim in sides:
        size, length = (lax.axis_size(axis), shard.shape[dim])
        up = [(i, (i + 1) % size) for i in range(size - 1)]
        down = [(j, i) for i, j in up]
        last = lax.slice_in_dim(shard, length - width, length, axis=dim)
        initial = lax.slice_in_dim(shard, 0, width, axis=dim)
        before = lax.ppermute(last, axis, up)
        after = lax.ppermute(initial, axis, down)
        shard = jnp.concatenate([before, shard, after], axis=dim)
    return shard


def convolve(values_in, kernel):
    return lax.conv_general_dilated(
        values_in,
        kernel,
        (1, 1, 1),
        ((0, 0), (1, 1), (1, 1)),
        dimension_numbers=layout_spec,
        preferred_element_type=jnp.float32,
    )


def activate(summed, bias_row):
    return jax.nn.relu(summed + bias_row[None, None, :, None, None]).astype(jnp.bfloat16)


def body(volume, first_kernel, first_bias, second_kernel, second_bias):
    gathered = lax.all_gather(volume, "chan", axis=2, tiled=True)
    rimmed = padded(gathered, (("slab", 1),), 1)
    first_sum = convolve(rimmed, first_kernel)
    hidden = activate(first_sum, first_bias)
    hidden_rim = padded(hidden, (("slab", 1),), 1)
    partial_value = convolve(hidden_rim, second_kernel)
    second_sum = lax.psum_scatter(partial_value, "chan", scatter_dimension=2, tiled=True)
    return activate(second_sum, second_bias)


def solution(mesh):
    return jax.shard_map(
        body,
        mesh=mesh,
        in_specs=(
            P(None, "slab", "chan", None, None),
            P(None, None, None, None, "chan"),
            P("chan"),
            P(None, None, None, "chan", None),
            P("chan"),
        ),
        out_specs=P(None, "slab", "chan", None, None),
        check_vma=False,
    )
```

profile of v0, /device:TPU:25, one launch (start us, length us, event | category | flops | bytes accessed | tf_op | source)
XLA Modules:
  0.0 597.5 jit_solution(8810597857634700409)
XLA Ops:
  6.5 3.6 copy.33
  10.2 59.8 %all-gather.2.cloned.1.call-done = bf16[2,4,128,32,128]{4,3,1,0,2:T(8,128)(2,1)} async-done(((bf16[2,4,32,32,128]{4,3,1,0,2:T(8,128)(2,1)}), bf16[2,4,128,32,128]{4,3,1,0,2:T(8,128)(2,1)}) %all-gather.2.cloned.1.call-update) | async-done | bytes 8388624 | tf_op jit(solution)/shard_map/all_gather | solution.py:38
  70.0 16.9 %copy.34 = bf16[2,4,128,32,128]{2,3,4,0,1:T(8,128)(2,1)} copy(bf16[2,4,128,32,128]{4,3,1,0,2:T(8,128)(2,1)} %all-gather.2.cloned.1.call-done) | data formatting | bytes 16777216 | tf_op jit(solution)/shard_map/all_gather | solution.py:38
  86.9 3.2 fusion.14
  90.1 3.2 collective-permute-start
  93.3 3.1 collective-permute-start.1
  96.4 43.6 %collective-permute-done = bf16[2,1,128,32,128]{2,3,4,0,1:T(8,128)(2,1)S(1)} collective-permute-done((bf16[2,1,128,32,128]{2,3,4,0,1:T(8,128)(2,1)S(1)}, bf16[2,1,128,32,128]{2,3,4,0,1:T(8,128)(2,1)S(1)}, u32[]{:S(2)}, u32[]{:S(2)}) %collective-permute-start) | collective-permute-done | bytes 2097184 | tf_op jit(solution)/shard_map/ppermute | solution.py:16
  140.0 45.5 %collective-permute-done.1 = bf16[2,1,128,32,128]{2,3,4,0,1:T(8,128)(2,1)S(1)} collective-permute-done((bf16[2,1,128,32,128]{2,3,4,0,1:T(8,128)(2,1)S(1)}, bf16[2,1,128,32,128]{2,3,4,0,1:T(8,128)(2,1)S(1)}, u32[]{:S(2)}, u32[]{:S(2)}) %collective-permute-start.1) | collective-permute-done | bytes 2097184 | tf_op jit(solution)/shard_map/ppermute | solution.py:17
  187.2 2.3 pad
  190.0 2.9 fusion.3
  192.9 82.8 %maximum_convert_fusion = bf16[4,32,16,17,32]{4,2,3,1,0:T(8,128)(2,1)S(1)} fusion(f32[32]{0:T(128)S(1)} %copy-done.5, pred[16,17]{0,1:T(8,128)(4,1)S(1)} %copy-done.6, bf16[3,3,3,128,32]{3,4,2,1,0:T(8,128)(2,1)} %param.6, bf16[6,128,32,2,8,19]{1,2,5,4,3,0:T(8,128)(2,1)S(1)} %fusion.3), kind=kOutput, calls=%fused_computation.4 | convolution fusion | flops 7544766464 | bytes 17392016 | tf_op jit(solution)/shard_map/conv_general_dilated | solution.py:23
  275.8 3.4 copy-done.3
  281.3 9.3 %copy.40 = bf16[4,32,16,17,32]{4,1,3,2,0:T(8,128)(2,1)} copy(bf16[4,32,16,17,32]{4,2,3,1,0:T(8,128)(2,1)} %copy-done.3) | data formatting | bytes 4456448 | tf_op jit(solution)/shard_map/convert_element_type | solution.py:34
  290.6 2.2 copy.38
  294.5 4.0 copy.39
  301.4 3.3 copy.42
  304.7 4.3 collective-permute-start.3
  308.9 8.0 %slice_bitcast_fusion.1 = bf16[2,4,32,32,128]{2,3,4,0,1:T(8,128)(2,1)} fusion(bf16[4,32,2,136,32]{4,1,3,2,0:T(8,128)(2,1)} %bitcast.35), kind=kLoop, calls=%fused_computation.16 | loop fusion | bytes 4194304 | tf_op jit(solution)/shard_map/convert_element_type | solution.py:34
  317.0 3.2 copy.43
  320.2 6.4 %collective-permute-done.3 = bf16[2,1,32,32,128]{4,3,2,1,0:T(8,128)(2,1)} collective-permute-done((bf16[2,1,32,32,128]{4,3,2,1,0:T(8,128)(2,1)}, bf16[2,1,32,32,128]{4,3,2,1,0:T(8,128)(2,1)}, u32[]{:S(2)}, u32[]{:S(2)}) %collective-permute-start.3) | collective-permute-done | bytes 524320 | tf_op jit(solution)/shard_map/ppermute | solution.py:17
  326.5 5.2 copy.44
  331.7 10.6 %maximum_bitcast_fusion.1 = bf16[6,32,32,2,128]{1,2,4,3,0:T(8,128)(2,1)} fusion(bf16[2,1,32,32,128]{2,3,4,0,1:T(8,128)(2,1)} %copy.44, bf16[2,4,32,32,128]{2,3,4,0,1:T(8,128)(2,1)} %slice_bitcast_fusion.1, bf16[2,1,32,32,128]{2,3,4,0,1:T(8,128)(2,1)S(1)} %copy.43), kind=kLoop, calls=%fused_computation.14 | loop fusion | flops 3145728 | bytes 6291456 | tf_op jit(solution)/shard_map/concatenate | solution.py:18
  342.3 16.6 %copy.50 = bf16[6,32,32,2,128]{2,1,4,3,0:T(8,128)(2,1)} copy(bf16[6,32,32,2,128]{1,2,4,3,0:T(8,128)(2,1)} %maximum_bitcast_fusion.1) | data formatting | bytes 6291456
  359.0 7.0 %pad.2.clone = bf16[6,32,32,2,136]{2,1,4,3,0:T(8,128)(2,1)S(1)} pad(bf16[6,32,32,2,128]{2,1,4,3,0:T(8,128)(2,1)} %copy.50, bf16[]{:T(256)} %constant.5), padding=0_0x0_0x0_0x0_0x1_7 | pad | bytes 6488066 | tf_op jit(solution)/shard_map/concatenate | solution.py:18
  366.4 7.3 %fusion.2 = bf16[6,32,32,2,8,19]{2,1,5,4,3,0:T(8,128)(2,1)} fusion(bf16[6,32,32,2,7,2]{2,1,5,4,3,0:T(8,128)(2,1)S(1)} %slice.32, bf16[6,32,32,2,8,17]{2,1,5,4,3,0:T(8,128)(2,1)S(1)} %bitcast.32), kind=kLoop, calls=%fused_computation.6 | loop fusion | flops 11206656 | bytes 7421952 | tf_op jit(solution)/shard_map/conv_general_dilated | solution.py:23
  373.7 21.0 %copy.46 = bf16[6,32,32,2,8,19]{1,4,3,5,2,0:T(8,128)(2,1)} copy(bf16[6,32,32,2,8,19]{2,1,5,4,3,0:T(8,128)(2,1)} %fusion.2) | data formatting | bytes 7471104 | tf_op jit(solution)/shard_map/conv_general_dilated | solution.py:23
  394.7 31.6 %broadcast_select_fusion = f32[4,32,16,17,128]{4,2,3,1,0:T(8,128)S(1)} fusion(pred[16,17]{0,1:T(8,128)(4,1)S(1)} %copy-done.6, bf16[3,3,3,32,128]{4,3,2,1,0:T(8,128)(2,1)S(1)} %copy-done, bf16[6,32,32,2,8,19]{1,4,3,5,2,0:T(8,128)(2,1)} %copy.46), kind=kOutput, calls=%fused_computation.15 | convolution fusion | flops 7544766464 | bytes 21782800 | tf_op jit(solution)/shard_map/conv_general_dilated | solution.py:23
  426.3 6.2 %copy.47 = f32[4,32,16,17,128]{4,1,3,2,0:T(8,128)S(1)} copy(f32[4,32,16,17,128]{4,2,3,1,0:T(8,128)S(1)} %broadcast_select_fusion) | data formatting | bytes 35651584 | tf_op jit(solution)/shard_map/conv_general_dilated | solution.py:23
  432.5 6.2 %slice_bitcast_fusion = f32[2,4,128,32,128]{2,3,4,0,1:T(8,128)} fusion(f32[4,32,2,136,128]{4,1,3,2,0:T(8,128)S(1)} %bitcast.30), kind=kLoop, calls=%fused_computation.5 | loop fusion | bytes 33554432 | tf_op jit(solution)/shard_map/conv_general_dilated | solution.py:23
  438.7 20.9 %copy.48 = f32[2,4,128,32,128]{4,3,1,0,2:T(8,128)} copy(f32[2,4,128,32,128]{2,3,4,0,1:T(8,128)} %slice_bitcast_fusion) | data formatting | bytes 33554432 | tf_op jit(solution)/shard_map/conv_general_dilated | solution.py:23
  459.7 126.2 %reduce-scatter.2.cloned.1.call-done = f32[2,4,32,32,128]{4,3,1,0,2:T(8,128)} async-done(((f32[2,4,128,32,128]{4,3,1,0,2:T(8,128)}), f32[2,4,32,32,128]{4,3,1,0,2:T(8,128)}) %reduce-scatter.2.cloned.1.call-update) | async-done | bytes 4194320 | tf_op jit(solution)/shard_map/reduce_scatter | solution.py:44
  585.9 2.9 maximum_convert_fusion.1
  (27 shorter events, 11.0 us)
Async XLA Ops:
  6.5 388.2 %copy-start = (bf16[3,3,3,32,128]{4,3,2,1,0:T(8,128)(2,1)S(1)}, bf16[3,3,3,32,128]{4,3,2,1,0:T(8,128)(2,1)}, u32[]{:S(2)}) copy-start(bf16[3,3,3,32,128]{4,3,2,1,0:T(8,128)(2,1)} %param.8) | copy-start | bytes 663556
  6.5 63.5 %all-gather.2.cloned.1.call-start = ((), (), s32[]{:S(2)}) async-start(), calls=%async_computation.1 | async-start | bytes 10485760 | tf_op jit(solution)/shard_map/all_gather | solution.py:38
  10.2 575.7 %reduce-scatter.2.cloned.1.call-start = ((), (), s32[]{:S(2)}) async-start(), calls=%async_computation.2 | async-start | bytes 20971520 | tf_op jit(solution)/shard_map/reduce_scatter | solution.py:44
  86.9 98.6 %copy-start.2 = (bf16[2,4,128,32,128]{2,3,4,0,1:T(8,128)(2,1)S(1)}, bf16[2,4,128,32,128]{2,3,4,0,1:T(8,128)(2,1)}, u32[]{:S(2)}) copy-start(bf16[2,4,128,32,128]{2,3,4,0,1:T(8,128)(2,1)} %copy.34) | copy-start | bytes 25165828
  90.1 49.9 %collective-permute-start = (bf16[2,1,128,32,128]{2,3,4,0,1:T(8,128)(2,1)S(1)}, bf16[2,1,128,32,128]{2,3,4,0,1:T(8,128)(2,1)S(1)}, u32[]{:S(2)}, u32[]{:S(2)}) collective-permute-start(bf16[2,1,128,32,128]{2,3,4,0,1:T(8,128)(2,1)S(1)} %get-tuple-element.7), channel_id=1, source_target_pairs={{0,4},{4,8},{8,12},{12,16},{16,20},{20,24},{24,28},{1,5},{5,9},{9,... | collective-permute-start | bytes 6291464 | tf_op jit(solution)/shard_map/ppermute | solution.py:16
  93.3 92.2 %collective-permute-start.1 = (bf16[2,1,128,32,128]{2,3,4,0,1:T(8,128)(2,1)S(1)}, bf16[2,1,128,32,128]{2,3,4,0,1:T(8,128)(2,1)S(1)}, u32[]{:S(2)}, u32[]{:S(2)}) collective-permute-start(bf16[2,1,128,32,128]{2,3,4,0,1:T(8,128)(2,1)S(1)} %get-tuple-element.8), channel_id=1, source_target_pairs={{4,0},{8,4},{12,8},{16,12},{20,16},{24,20},{28,24},{5,1},{9,5},{13... | collective-permute-start | bytes 6291464 | tf_op jit(solution)/shard_map/ppermute | solution.py:17
  189.9 3.0 copy-start.5
  189.9 3.0 copy-start.6
  275.7 3.5 copy-start.3
  298.5 18.4 %collective-permute-start.2 = (bf16[2,1,32,32,128]{4,3,2,1,0:T(8,128)(2,1)S(1)}, bf16[2,1,32,32,128]{4,3,2,1,0:T(8,128)(2,1)S(1)}, u32[]{:S(2)}, u32[]{:S(2)}) collective-permute-start(bf16[2,1,32,32,128]{4,3,2,1,0:T(8,128)(2,1)S(1)} %copy.39), channel_id=1, source_target_pairs={{0,4},{4,8},{8,12},{12,16},{16,20},{20,24},{24,28},{1,5},{5,9},{9,... | collective-permute-start | bytes 1572872 | tf_op jit(solution)/shard_map/ppermute | solution.py:16
  304.7 21.8 %collective-permute-start.3 = (bf16[2,1,32,32,128]{4,3,2,1,0:T(8,128)(2,1)}, bf16[2,1,32,32,128]{4,3,2,1,0:T(8,128)(2,1)}, u32[]{:S(2)}, u32[]{:S(2)}) collective-permute-start(bf16[2,1,32,32,128]{4,3,2,1,0:T(8,128)(2,1)} %copy.42), channel_id=1, source_target_pairs={{4,0},{8,4},{12,8},{16,12},{20,16},{24,20},{28,24},{5,1},{9,5},{13... | collective-permute-start | bytes 1572872 | tf_op jit(solution)/shard_map/ppermute | solution.py:17
  459.7 126.2 %copy-start.4 = (f32[32]{0:T(128)S(1)}, f32[32]{0:T(128)}, u32[]{:S(2)}) copy-start(f32[32]{0:T(128)} %param.9) | copy-start | bytes 388
  459.7 130.8 %copy-start.1 = (bf16[3,3,3,32,128]{4,3,2,1,0:T(8,128)(2,1)S(1)}, bf16[3,3,3,32,128]{4,3,2,1,0:T(8,128)(2,1)}, u32[]{:S(2)}) copy-start(bf16[3,3,3,32,128]{4,3,2,1,0:T(8,128)(2,1)} %param.8) | copy-start | bytes 663556
Sparse Core Ops, SparseCore 0:
  10.3 59.6 all-gather.1
  459.8 126.0 reduce-scatter.1
where the time goes:
time: 599 us; the launch traced here: 598 us
  waiting for transfers between devices  281 us (47%)
  local copies, waits for them, and re-layouts  150 us (25%)
  matrix products  114 us (19%)
  other arithmetic  25.3 us (4%)
  between operations  13.8 us (2%)
  starting transfers between devices  12.5 us (2%)
    reduce_scatter x1, waiting for transfers between devices, body(): lax.psum_scatter(partial_value, 'chan', scatter_dimension=2, tiled=True)  126 us
    conv_general_dilated x2, matrix products, convolve(): lax.conv_general_dilated(values_in, kernel, (1, 1, 1), ((0, 0), (1, 1), (...  114 us
    all_gather x1, waiting for transfers between devices, body(): gathered = lax.all_gather(volume, 'chan', axis=2, tiled=True)  59.8 us
    conv_general_dilated x6, local copies, waits for them, and re-layouts, convolve(): lax.conv_general_dilated(values_in, kernel, (1, 1, 1), ((0, 0), (1, 1), (...  55.2 us
    ppermute x2, waiting for transfers between devices, padded(): after = lax.ppermute(initial, axis, down)  51.8 us
    ppermute x2, waiting for transfers between devices, padded(): before = lax.ppermute(last, axis, up)  43.6 us
    convert_element_type x6, local copies, waits for them, and re-layouts, activate(): jax.nn.relu(summed + bias_row[None, None, :, None, None])  24 us
    unnamed x16, local copies, waits for them, and re-layouts  23.7 us
  transfers between devices with their start and end apart: 6, of which 5 were waited for; matrix products, arithmetic and copies ran while one was open for 3% of the time, Pallas kernels for 0%

commit v1 on v0

v1 whole, which is shorter than its diff:
```python
import functools

import jax
import jax.numpy as jnp
from jax import lax
from jax.experimental import pallas as pl
from jax.experimental.pallas import tpu as pltpu
from jax.sharding import PartitionSpec as P

BF = jnp.bfloat16
VMEM_LIMIT = 48 * 2**20


def chan_swap(value, k):
    return lax.ppermute(value, "chan", [(i, i ^ k) for i in range(4)])


def slab_up(value):
    size = lax.axis_size("slab")
    return lax.ppermute(value, "slab", [(i, i + 1) for i in range(size - 1)])


def slab_down(value):
    size = lax.axis_size("slab")
    return lax.ppermute(value, "slab", [(i + 1, i) for i in range(size - 1)])


def rows(value, axis, start, count):
    return lax.dynamic_slice_in_dim(value, start, count, axis=axis)


def conv_rows(x, w, bias, depth, count, store):
    chans, width = x.shape[2], x.shape[3]
    lane = lax.broadcasted_iota(jnp.int32, (chans, width), 1)

    def step(j, _):
        for z in range(0, depth, 2):
            cols = [
                jnp.concatenate([x[z + u + a, j + c] for a in range(3) for c in range(3)], axis=0)
                for u in range(2)
            ]
            lhs = jnp.concatenate([w[k] for k in range(9)], axis=1)
            acc = jnp.dot(lhs, jnp.concatenate(cols, axis=1), preferred_element_type=jnp.float32)
            for u in range(2):
                part = acc[:, u * width : (u + 1) * width]
                before = jnp.where(lane == 0, 0.0, pltpu.roll(part[:chans], 1, 1))
                after = jnp.where(lane == width - 1, 0.0, pltpu.roll(part[2 * chans :], width - 1, 1))
                total = before + part[chans : 2 * chans] + after
                store(z + u, j, jnp.maximum(total + bias[...], 0.0).astype(BF))
        return 0

    lax.fori_loop(0, count, step, 0)


def run_copies(pairs, sems):
    copies = [pltpu.make_async_copy(s, d, sems.at[i]) for i, (s, d) in enumerate(pairs)]
    for copy in copies:
        copy.start()
    return copies


def first_kernel_body(chunk, count, own, *refs):
    if chunk == 0:
        new, old, w, bias = refs[:4], None, refs[4], refs[5]
        out_lo, out_mid, out_hi, x, sems = refs[6:]
    else:
        new, old, w, bias = refs[:4], refs[4:8], refs[8], refs[9]
        out_lo, out_mid, out_hi, x, sems = refs[10:]
    me = lax.axis_index("chan")
    b, c = me // 2, me % 2
    depth = own.shape[1]
    thick = own.shape[2]
    unit = own.shape[3]

    def pieces(four, have, own_at, x_at, skip, n, dst):
        xr, sr, lo, hi = four
        to = pl.ds(dst, n)
        inner = pl.ds(1, depth)
        out = [
            (own.at[b, :, pl.ds(own_at + skip, n)], x.at[inner, to, pl.ds(0, unit)]),
            (xr.at[:, pl.ds(x_at + skip, n)], x.at[inner, to, pl.ds(unit, unit)]),
        ]
        for k in range(2):
            out.append((sr.at[k, :, pl.ds(skip, n)], x.at[inner, to, pl.ds((2 + k) * unit, unit)]))
        for k in range(4):
            out.append((lo.at[k, pl.ds(skip, n)], x.at[0, to, pl.ds(k * unit, unit)]))
            out.append((hi.at[k, pl.ds(skip, n)], x.at[depth + 1, to, pl.ds(k * unit, unit)]))
        return out

    half = thick // 2
    n0 = half // 2 + 2
    if chunk == 0:
        pairs = pieces(new, n0, c * (thick - n0), c * n0, 0, n0, 1 - c)
        edge = jnp.where(c == 0, 0, n0)
    else:
        n1 = half // 2
        lead = n1 - 4
        pairs = pieces(new, n1, n0 + c * lead, c * lead, 0, n1, 2 - 2 * c)
        pairs += pieces(old, 2, c * (thick - n0), c * n0, (1 - c) * (n0 - 2), 2, c * n1)
        edge = None
    copies = run_copies(pairs, sems)
    if edge is not None:
        for z in range(depth + 2):
            x[z, edge] = jnp.zeros(x.shape[2:], BF)
    for copy in copies:
        copy.wait()

    def store(z, j, value):
        if z == 0:
            out_lo[j] = value
        elif z == depth - 1:
            out_hi[j] = value
        else:
            out_mid[z - 1, j] = value

    conv_rows(x, w, bias, depth, count, store)


def second_kernel_body(chunk, count, *refs):
    if chunk == 0:
        new, old, w, bias = refs[:5], None, refs[5], refs[6]
        outs, x, sems = refs[7:11], refs[11], refs[12]
    else:
        new, old, w, bias = refs[:5], refs[5:10], refs[10], refs[11]
        outs, x, sems = refs[12:16], refs[16], refs[17]
    c = lax.axis_index("chan") % 2
    depth = x.shape[0] - 2
    unit = outs[0].shape[2]

    def pieces(five, skip, n, dst):
        below, low, mid, high, above = five
        src, to = pl.ds(skip, n), pl.ds(dst, n)
        return [
            (below.at[src], x.at[0, to]),
            (low.at[src], x.at[1, to]),
            (mid.at[:, src], x.at[pl.ds(2, depth - 2), to]),
            (high.at[src], x.at[depth, to]),
            (above.at[src], x.at[depth + 1, to]),
        ]

    n0 = new[0].shape[0]
    if chunk == 0:
        pairs = pieces(new, 0, n0, 1 - c)
        edge = jnp.where(c == 0, 0, n0)
    else:
        h0 = old[0].shape[0]
        pairs = pieces(new, 0, n0, 2 - 2 * c)
        pairs += pieces(old, (1 - c) * (h0 - 2), 2, c * n0)
        edge = None
    copies = run_copies(pairs, sems)
    if edge is not None:
        for z in range(depth + 2):
            x[z, edge] = jnp.zeros(x.shape[2:], BF)
    for copy in copies:
        copy.wait()

    def store(z, j, value):
        for k in range(4):
            outs[k][z, j] = value[k * unit : (k + 1) * unit]

    conv_rows(x, w, bias, depth, count, store)


def call(body, count, depth, out_shapes, n_copies, chans, width, operands):
    any_spec = pl.BlockSpec(memory_space=pl.ANY)
    vmem = pl.BlockSpec(memory_space=pltpu.VMEM)
    flops = 2 * depth * count * width * 27 * chans * chans
    return pl.pallas_call(
        body,
        out_shape=[jax.ShapeDtypeStruct(s, BF) for s in out_shapes],
        in_specs=[any_spec] * (len(operands) - 2) + [vmem, vmem],
        out_specs=[vmem] * len(out_shapes),
        scratch_shapes=[
            pltpu.VMEM((depth + 2, count + 2, chans, width), BF),
            pltpu.SemaphoreType.DMA((n_copies,)),
        ],
        cost_estimate=pl.CostEstimate(flops=3 * flops, bytes_accessed=2**21, transcendentals=0),
        compiler_params=pltpu.CompilerParams(vmem_limit_bytes=VMEM_LIMIT),
    )(*operands)


def body(volume, first_kernel, first_bias, second_kernel, second_bias):
    _, depth, unit, thick, width = volume.shape
    chans = 4 * unit
    half = thick // 2
    n0, n1 = half // 2 + 2, half // 2
    lead = n1 - 4
    me = lax.axis_index("chan")
    b, c = me // 2, me % 2
    order = [me, me ^ 2, me ^ 1, me ^ 3]

    xt = jnp.transpose(volume, (0, 1, 3, 2, 4))
    away = lax.dynamic_index_in_dim(xt, 1 - b, 0, keepdims=False)
    home = lax.dynamic_index_in_dim(xt, b, 0, keepdims=False)
    xr0 = chan_swap(jnp.concatenate([away[:, :n0], away[:, thick - n0 :]], axis=1), 2)
    xr1 = chan_swap(away[:, n0 : thick - n0], 2)

    def reorder(value, axis):
        return jnp.concatenate([lax.dynamic_slice_in_dim(value, k * unit, unit, axis=axis) for k in order], axis=axis)

    w1 = jnp.transpose(reorder(first_kernel, 3), (0, 1, 2, 4, 3)).reshape(27, unit, chans)
    w2 = reorder(second_kernel, 4).reshape(27, unit, chans)
    mine = jnp.stack([w1, w2])
    pair = jnp.stack([mine, chan_swap(mine, 2)])
    four = jnp.concatenate([pair, chan_swap(pair, 1)])
    four = jnp.stack(
        [jnp.concatenate([four[m, ..., (j ^ m) * unit : ((j ^ m) + 1) * unit] for j in range(4)], axis=-1) for m in range(4)]
    )
    full1 = jnp.transpose(four[:, 0], (1, 0, 2, 3)).reshape(9, 3 * chans, chans)
    full2 = jnp.transpose(four[:, 1], (1, 3, 0, 2)).reshape(9, 3 * chans, chans)
    biases = jnp.stack([first_bias, second_bias])
    biases = jnp.concatenate([biases, chan_swap(biases, 2)], axis=1)
    spread = jnp.concatenate([biases, chan_swap(biases, 1)], axis=1)
    bias1 = jnp.broadcast_to(spread[0][:, None], (chans, width))
    bias2 = jnp.broadcast_to(spread[1][:, None], (chans, width))

    def gathered(xr, n, own_at, x_at):
        o = 1 - c
        sr = chan_swap(jnp.stack([rows(home, 1, own_at(o), n), rows(xr, 1, x_at(o), n)]), 1)
        mine_own, mine_x = rows(home, 1, own_at(c), n), rows(xr, 1, x_at(c), n)

        def layer(z):
            return jnp.concatenate([mine_own[z][None], mine_x[z][None], sr[:, z]])

        return xr, sr, slab_up(layer(depth - 1)), slab_down(layer(0))

    in0 = gathered(xr0, n0, lambda k: k * (thick - n0), lambda k: k * n0)
    in1 = gathered(xr1, n1, lambda k: n0 + k * lead, lambda k: k * lead)

    def hidden_shapes(n):
        return [(n, chans, width), (depth - 2, n, chans, width), (n, chans, width)]

    h0, h1 = n0 - 1, n1
    low0, mid0, high0 = call(
        functools.partial(first_kernel_body, 0, h0), h0, depth, hidden_shapes(h0), 12, chans, width,
        (xt, *in0, full1, bias1),
    )
    hid0 = (slab_up(high0), low0, mid0, high0, slab_down(low0))
    low1, mid1, high1 = call(
        functools.partial(first_kernel_body, 1, h1), h1, depth, hidden_shapes(h1), 24, chans, width,
        (xt, *in1, *in0, full1, bias1),
    )
    hid1 = (slab_up(high1), low1, mid1, high1, slab_down(low1))

    blocks = [(depth, n1, unit, width)] * 4
    got = []
    for chunk, hid in ((0, hid0), (1, hid1 + hid0)):
        outs = call(
            functools.partial(second_kernel_body, chunk, n1), n1, depth, blocks, 5 + 5 * chunk, chans, width,
            (*hid, full2, bias2),
        )
        got.append([outs[0], chan_swap(outs[1], 2), chan_swap(outs[2], 1), chan_swap(outs[3], 3)])

    def halves(first, second):
        as0 = jnp.concatenate([first[0], first[1], second[1], second[0]], axis=1)
        as1 = jnp.concatenate([second[0], second[1], first[1], first[0]], axis=1)
        return jnp.where(c == 0, as0, as1)

    at_home = halves([g[0] for g in got], [g[2] for g in got])
    abroad = halves([g[1] for g in got], [g[3] for g in got])
    out = jnp.where(b == 0, jnp.stack([at_home, abroad]), jnp.stack([abroad, at_home]))
    return jnp.transpose(out, (0, 1, 3, 2, 4))


def solution(mesh):
    return jax.shard_map(
        body,
        mesh=mesh,
        in_specs=(
            P(None, "slab", "chan", None, None),
            P(None, None, None, None, "chan"),
            P("chan"),
            P(None, None, None, "chan", None),
            P("chan"),
        ),
        out_specs=P(None, "slab", "chan", None, None),
        check_vma=False,
    )
```

time: 599 us -> 168 us (0.28)
  waiting for transfers between devices: 281 us -> 57.5 us
  local copies, waits for them, and re-layouts: 150 us -> 33.6 us
  matrix products: 114 us -> 0 us
  Pallas kernels: 0 us -> 31.3 us
  starting transfers between devices: 12.5 us -> 33.6 us
  other arithmetic: 25.3 us -> 10.7 us
  between operations: 13.8 us -> 0.62 us
    reduce_scatter x1 -> x0, waiting for transfers between devices: 126 us -> none  [body(): lax.psum_scatter(partial_value, 'chan', scatter_dimension=2, tiled=True)]
    conv_general_dilated x2 -> x0, matrix products: 114 us -> none  [convolve(): lax.conv_general_dilated(values_in, kernel, (1, 1, 1), ((0, 0), (1, 1), (...]
    all_gather x1 -> x0, waiting for transfers between devices: 59.8 us -> none  [body(): gathered = lax.all_gather(volume, 'chan', axis=2, tiled=True)]
    conv_general_dilated x6 -> x0, local copies, waits for them, and re-layouts: 55.2 us -> none  [convolve(): lax.conv_general_dilated(values_in, kernel, (1, 1, 1), ((0, 0), (1, 1), (...]
    ppermute x4 -> x22, waiting for transfers between devices: 95.4 us -> 57.5 us  [the longest x14 37.9 us: chan_swap(): return lax.ppermute(value, 'chan', [(i, i ^ k) for i in range(4)])]
    pallas_call x0 -> x4, Pallas kernels: none -> 31.3 us  [call(): pl.pallas_call(body, out_shape=[jax.ShapeDtypeStruct(s, BF) for s in out_...]
    convert_element_type x6 -> x0, local copies, waits for them, and re-layouts: 24 us -> none  [activate(): jax.nn.relu(summed + bias_row[None, None, :, None, None])]
    ppermute x4 -> x22, starting transfers between devices: 12.5 us -> 33.6 us  [the longest x4 13.9 us: slab_down(): return lax.ppermute(value, 'slab', [(i + 1, i) for i in range(size - 1)])]
  transfers between devices with their start and end apart: 6 -> 22, of which waited for: 5 -> 7; matrix products, arithmetic and copies ran while one was open for 3% -> 19% of each run, Pallas kernels for 0% -> 14%
where the time goes in v1:
time: 168 us; the launch traced here: 167 us
  waiting for transfers between devices  57.5 us (34%)
  local copies, waits for them, and re-layouts  33.6 us (20%)
  starting transfers between devices  33.6 us (20%)
  Pallas kernels  31.3 us (19%)
  other arithmetic  10.7 us (6%)
    ppermute x14, waiting for transfers between devices, chan_swap(): return lax.ppermute(value, 'chan', [(i, i ^ k) for i in range(4)])  37.9 us
    pallas_call x4, Pallas kernels, call(): pl.pallas_call(body, out_shape=[jax.ShapeDtypeStruct(s, BF) for s in out_...  31.3 us
    ppermute x4, waiting for transfers between devices, slab_down(): return lax.ppermute(value, 'slab', [(i + 1, i) for i in range(size - 1)])  19.5 us
    ppermute x4, starting transfers between devices, slab_down(): return lax.ppermute(value, 'slab', [(i + 1, i) for i in range(size - 1)])  13.9 us
    ppermute x4, starting transfers between devices, slab_up(): return lax.ppermute(value, 'slab', [(i, i + 1) for i in range(size - 1)])  10.1 us
    unnamed x45, local copies, waits for them, and re-layouts  9.76 us
    ppermute x14, starting transfers between devices, chan_swap(): return lax.ppermute(value, 'chan', [(i, i ^ k) for i in range(4)])  9.59 us
    squeeze x3, local copies, waits for them, and re-layouts, body(): four[m, ..., (j ^ m) * unit:((j ^ m) + 1) * unit]  5.94 us
  transfers between devices with their start and end apart: 22, of which 7 were waited for; matrix products, arithmetic and copies ran while one was open for 19% of the time, Pallas kernels for 14%

profile of v1, /device:TPU:25, one launch (start us, length us, event | category | flops | bytes accessed | tf_op | source)
XLA Modules:
  0.0 167.2 jit_solution(5645574258004491785)
XLA Ops:
  0.0 1.6 constant_dynamic-slice_fusion.11
  4.8 2.4 %copy.44 = bf16[2,4,32,32,128]{4,2,3,1,0:T(8,128)(2,1)S(1)} copy(bf16[2,4,32,32,128]{4,3,2,1,0:T(8,128)(2,1)} %param.5) | data formatting | bytes 4194304 | tf_op args[0]
  10.9 3.1 %slice_bitcast_fusion.17 = (bf16[2,27,32,32]{3,2,1,0:T(8,128)(2,1)}, bf16[2,27,32,32]{3,2,1,0:T(8,128)(2,1)}, bf16[2,27,32,32]{3,2,1,0:T(8,128)(2,1)}, bf16[2,27,32,32]{3,2,1,0:T(8,128)(2,1)}) fusion(bf16[1,2,27,32,128]{4,3,2,1,0:T(8,128)(2,1)} %get-tuple-element.61), kind=kLoop, calls=%fused_computation.27 | loop fusion | bytes 884736 | tf_op jit(solution)/shard_map/squeeze | solution.py:207
  15.9 2.2 %constant_dynamic-slice_fusion.13 = bf16[1,4,32,10,128]{4,3,2,1,0:T(8,128)(2,1)} fusion(bf16[2,4,32,32,128]{4,3,2,1,0:T(8,128)(2,1)} %param.5, s32[]{:T(128)S(6)} %select_n.108, s32[]{:T(128)S(6)} %select_n.110), kind=kLoop, calls=%fused_computation.66 | loop fusion | bytes 655368 | tf_op jit(solution)/shard_map/dynamic-slice.8
  18.7 18.6 %collective-permute-done.6 = f32[2,32]{1,0:T(2,128)S(1)} collective-permute-done((f32[2,32]{1,0:T(2,128)S(1)}, f32[2,32]{1,0:T(2,128)S(1)}, u32[]{:S(2)}, u32[]{:S(2)}) %collective-permute-start.6) | collective-permute-done | bytes 288 | tf_op jit(solution)/shard_map/ppermute | solution.py:15
  37.9 1.6 collective-permute-start.7
  43.9 2.0 %slice_bitcast_fusion.13 = (bf16[2,27,32,32]{3,2,1,0:T(8,128)(2,1)S(1)}, bf16[2,27,32,32]{3,2,1,0:T(8,128)(2,1)S(1)}, bf16[2,27,32,32]{3,2,1,0:T(8,128)(2,1)S(1)}, bf16[2,27,32,32]{3,2,1,0:T(8,128)(2,1)S(1)}) fusion(bf16[1,2,27,32,128]{4,3,2,1,0:T(8,128)(2,1)} %bitcast.20), kind=kLoop, calls=%fused_computation.23 | loop fusion | bytes 884736 | tf_op jit(solution)/shard_map/squeeze | solution.py:207
  45.9 1.2 pad_maximum_fusion.1
  49.2 3.1 %collective-permute-start.12 = (bf16[4,8,32,128]{3,2,1,0:T(8,128)(2,1)S(1)}, bf16[4,8,32,128]{3,2,1,0:T(8,128)(2,1)S(1)}, u32[]{:S(2)}, u32[]{:S(2)}) collective-permute-start(bf16[4,8,32,128]{3,2,1,0:T(8,128)(2,1)S(1)} %pad_maximum_fusion.8), channel_id=1, source_target_pairs={{0,4},{4,8},{8,12},{12,16},{16,20},{20,24},{24,28},{1,5},{5,9},{9,... | collective-permute-start | bytes 786440 | tf_op jit(solution)/shard_map/ppermute | solution.py:20
  52.4 3.0 %collective-permute-start.13 = (bf16[4,8,32,128]{3,2,1,0:T(8,128)(2,1)S(1)}, bf16[4,8,32,128]{3,2,1,0:T(8,128)(2,1)S(1)}, u32[]{:S(2)}, u32[]{:S(2)}) collective-permute-start(bf16[4,8,32,128]{3,2,1,0:T(8,128)(2,1)S(1)} %pad_maximum_fusion.9), channel_id=1, source_target_pairs={{4,0},{8,4},{12,8},{16,12},{20,16},{24,20},{28,24},{5,1},{9,5},{13... | collective-permute-start | bytes 786440 | tf_op jit(solution)/shard_map/ppermute | solution.py:25
  55.6 2.1 %collective-permute-start.3 = (bf16[4,10,32,128]{3,2,1,0:T(8,128)(2,1)S(1)}, bf16[4,10,32,128]{3,2,1,0:T(8,128)(2,1)S(1)}, u32[]{:S(2)}, u32[]{:S(2)}) collective-permute-start(bf16[4,10,32,128]{3,2,1,0:T(8,128)(2,1)S(1)} %pad_maximum_fusion.7), channel_id=1, source_target_pairs={{4,0},{8,4},{12,8},{16,12},{20,16},{24,20},{28,24},{5,1},{9,5},{13... | collective-permute-start | bytes 983048 | tf_op jit(solution)/shard_map/ppermute | solution.py:25
  57.8 3.2 %collective-permute-start.2 = (bf16[4,10,32,128]{3,2,1,0:T(8,128)(2,1)S(1)}, bf16[4,10,32,128]{3,2,1,0:T(8,128)(2,1)S(1)}, u32[]{:S(2)}, u32[]{:S(2)}) collective-permute-start(bf16[4,10,32,128]{3,2,1,0:T(8,128)(2,1)S(1)} %pad_maximum_fusion.6), channel_id=1, source_target_pairs={{0,4},{4,8},{8,12},{12,16},{16,20},{20,24},{24,28},{1,5},{5,9},{9,... | collective-permute-start | bytes 983048 | tf_op jit(solution)/shard_map/ppermute | solution.py:20
  63.6 16.3 %collective-permute-done.3.refs_3_.refs_7_ = bf16[4,10,32,128]{3,2,1,0:T(8,128)(2,1)S(1)} collective-permute-done((bf16[4,10,32,128]{3,2,1,0:T(8,128)(2,1)S(1)}, bf16[4,10,32,128]{3,2,1,0:T(8,128)(2,1)S(1)}, u32[]{:S(2)}, u32[]{:S(2)}) %collective-permute-start.3) | collective-permute-done | bytes 327712 | tf_op jit(solution)/shard_map/ppermute | solution.py:25
  80.0 8.1 %shard_map.55 = (bf16[9,128,128]{2,1,0:T(8,128)(2,1)S(1)}, bf16[2,9,128,128]{3,2,1,0:T(8,128)(2,1)S(1)}, bf16[9,128,128]{2,1,0:T(8,128)(2,1)}) custom-call(bf16[2,4,32,32,128]{4,3,2,1,0:T(8,128)(2,1)S(1)} %bitcast.110, bf16[4,20,32,128]{3,2,1,0:T(8,128)(2,1)S(1)} %collective-permute-done.refs_0_.refs_4_, ...), custom_call_target="tpu_custom_call" | custom-call | flops 12230590464 | bytes 2097152 | tf_op jit(solution)/shard_map/pallas_call | solution.py:168
  88.9 1.9 %collective-permute-start.8 = (bf16[9,128,128]{2,1,0:T(8,128)(2,1)}, bf16[9,128,128]{2,1,0:T(8,128)(2,1)S(1)}, u32[]{:S(2)}, u32[]{:S(2)}) collective-permute-start(bf16[9,128,128]{2,1,0:T(8,128)(2,1)} %get-tuple-element.19.refs_3_.refs_8_), channel_id=1, source_target_pairs={{0,4},{4,8},{8,12},{12,16},{16,20},{20,24},{24,28},{1,5},{5,9},{9,... | collective-permute-start | bytes 884744 | tf_op jit(solution)/shard_map/ppermute | solution.py:20
  90.8 4.3 %collective-permute-start.9 = (bf16[9,128,128]{2,1,0:T(8,128)(2,1)S(1)}, bf16[9,128,128]{2,1,0:T(8,128)(2,1)S(1)}, u32[]{:S(2)}, u32[]{:S(2)}) collective-permute-start(bf16[9,128,128]{2,1,0:T(8,128)(2,1)S(1)} %get-tuple-element.20.refs_1_.refs_6_), channel_id=1, source_target_pairs={{4,0},{8,4},{12,8},{16,12},{20,16},{24,20},{28,24},{5,1},{9,5},{13... | collective-permute-start | bytes 884744 | tf_op jit(solution)/shard_map/ppermute | solution.py:25
  95.1 7.5 %shard_map.57 = (bf16[8,128,128]{2,1,0:T(8,128)(2,1)S(1)}, bf16[2,8,128,128]{3,2,1,0:T(8,128)(2,1)S(1)}, bf16[8,128,128]{2,1,0:T(8,128)(2,1)S(1)}) custom-call(bf16[2,4,32,32,128]{4,3,2,1,0:T(8,128)(2,1)} %bitcast.111, bf16[4,12,32,128]{3,2,1,0:T(8,128)(2,1)S(1)} %collective-permute-done.10.refs_0_, bf16[2,4,8,32,128]{4,3,2,1,0:T(8,128)(2,1)S(1)} %copy.32.refs_1_, ...), custom_call_target="tpu_custom_call" | custom-call | flops 10871635968 | bytes 2097152 | tf_op jit(solution)/shard_map/pallas_call | solution.py:168
  103.4 1.9 %collective-permute-start.14 = (bf16[8,128,128]{2,1,0:T(8,128)(2,1)S(1)}, bf16[8,128,128]{2,1,0:T(8,128)(2,1)S(1)}, u32[]{:S(2)}, u32[]{:S(2)}) collective-permute-start(bf16[8,128,128]{2,1,0:T(8,128)(2,1)S(1)} %get-tuple-element.23.refs_3_), channel_id=1, source_target_pairs={{0,4},{4,8},{8,12},{12,16},{16,20},{20,24},{24,28},{1,5},{5,9},{9,... | collective-permute-start | bytes 786440 | tf_op jit(solution)/shard_map/ppermute | solution.py:20
  105.3 4.4 %collective-permute-start.15 = (bf16[8,128,128]{2,1,0:T(8,128)(2,1)S(1)}, bf16[8,128,128]{2,1,0:T(8,128)(2,1)S(1)}, u32[]{:S(2)}, u32[]{:S(2)}) collective-permute-start(bf16[8,128,128]{2,1,0:T(8,128)(2,1)S(1)} %get-tuple-element.24.refs_1_), channel_id=1, source_target_pairs={{4,0},{8,4},{12,8},{16,12},{20,16},{24,20},{28,24},{5,1},{9,5},{13... | collective-permute-start | bytes 786440 | tf_op jit(solution)/shard_map/ppermute | solution.py:25
  109.8 1.4 copy.28
  111.2 3.2 %reshape.233 = bf16[9,384,128]{1,0,2:T(8,128)(2,1)} reshape(bf16[27,128,4,32]{1,0,3,2:T(8,128)(2,1)} %copy.28) | data formatting | bytes 1769472 | tf_op jit(solution)/shard_map/reshape | solution.py:210
  114.4 2.4 %copy.29.refs_5_.refs_10_ = bf16[9,384,128]{2,1,0:T(8,128)(2,1)S(1)} copy(bf16[9,384,128]{1,0,2:T(8,128)(2,1)} %reshape.233) | data formatting | bytes 1769472 | tf_op jit(solution)/shard_map/reshape | solution.py:210
  116.8 3.2 %collective-permute-done.15.refs_4_ = bf16[8,128,128]{2,1,0:T(8,128)(2,1)S(1)} collective-permute-done((bf16[8,128,128]{2,1,0:T(8,128)(2,1)S(1)}, bf16[8,128,128]{2,1,0:T(8,128)(2,1)S(1)}, u32[]{:S(2)}, u32[]{:S(2)}) %collective-permute-start.15) | collective-permute-done | bytes 262176 | tf_op jit(solution)/shard_map/ppermute | solution.py:25
  123.2 7.6 %shard_map.58 = (bf16[4,8,32,128]{3,2,1,0:T(8,128)(2,1)S(1)}, bf16[4,8,32,128]{3,2,1,0:T(8,128)(2,1)S(1)}, bf16[4,8,32,128]{3,2,1,0:T(8,128)(2,1)S(1)}, bf16[4,8,32,128]{3,2,1,0:T(8,128)(2,1)S(1)}) custom-call(bf16[8,128,128]{2,1,0:T(8,128)(2,1)S(1)} %collective-permute-done.14.refs_0_, bf16[8,128,128]{2,1,0:T(8,128)(2,1)S(1)} %get-tuple-element.24.refs_1_, ...), custom_call_target="tpu_custom_call" | custom-call | flops 10871635968 | bytes 2097152 | tf_op jit(solution)/shard_map/pallas_call | solution.py:168
  131.3 8.1 %shard_map.56 = (bf16[4,8,32,128]{3,2,1,0:T(8,128)(2,1)S(1)}, bf16[4,8,32,128]{3,2,1,0:T(8,128)(2,1)S(1)}, bf16[4,8,32,128]{3,2,1,0:T(8,128)(2,1)}, bf16[4,8,32,128]{3,2,1,0:T(8,128)(2,1)S(1)}) custom-call(bf16[9,128,128]{2,1,0:T(8,128)(2,1)S(1)} %collective-permute-done.8.refs_0_.refs_5_, bf16[9,128,128]{2,1,0:T(8,128)(2,1)S(1)} %get-tuple-element.20.refs_1_.refs_6_, ...), custom_call_target="tpu_custom_call" | custom-call | flops 10871635968 | bytes 2097152 | tf_op jit(solution)/shard_map/pallas_call | solution.py:168
  139.6 1.3 collective-permute-start.19
  143.9 1.3 maximum_select_fusion.1
  145.2 1.9 %collective-permute-done.19 = bf16[4,8,32,128]{3,2,1,0:T(8,128)(2,1)S(1)} collective-permute-done((bf16[4,8,32,128]{3,2,1,0:T(8,128)(2,1)S(1)}, bf16[4,8,32,128]{3,2,1,0:T(8,128)(2,1)S(1)}, u32[]{:S(2)}, u32[]{:S(2)}) %collective-permute-start.19) | collective-permute-done | bytes 262176 | tf_op jit(solution)/shard_map/ppermute | solution.py:15
  147.1 7.1 %collective-permute-done.20 = bf16[4,8,32,128]{3,2,1,0:T(8,128)(2,1)S(1)} collective-permute-done((bf16[4,8,32,128]{3,2,1,0:T(8,128)(2,1)S(1)}, bf16[4,8,32,128]{3,2,1,0:T(8,128)(2,1)S(1)}, u32[]{:S(2)}, u32[]{:S(2)}) %collective-permute-start.20) | collective-permute-done | bytes 262176 | tf_op jit(solution)/shard_map/ppermute | solution.py:15
  154.2 4.2 %collective-permute-done.18 = bf16[4,8,32,128]{3,2,1,0:T(8,128)(2,1)S(1)} collective-permute-done((bf16[4,8,32,128]{3,2,1,0:T(8,128)(2,1)S(1)}, bf16[4,8,32,128]{3,2,1,0:T(8,128)(2,1)S(1)}, u32[]{:S(2)}, u32[]{:S(2)}) %collective-permute-start.18) | collective-permute-done | bytes 262176 | tf_op jit(solution)/shard_map/ppermute | solution.py:15
  158.3 6.2 %collective-permute-done.21 = bf16[4,8,32,128]{3,2,1,0:T(8,128)(2,1)S(1)} collective-permute-done((bf16[4,8,32,128]{3,2,1,0:T(8,128)(2,1)S(1)}, bf16[4,8,32,128]{3,2,1,0:T(8,128)(2,1)S(1)}, u32[]{:S(2)}, u32[]{:S(2)}) %collective-permute-start.21) | collective-permute-done | bytes 262176 | tf_op jit(solution)/shard_map/ppermute | solution.py:15
  165.1 2.1 %copy.35 = bf16[2,4,32,32,128]{4,3,2,1,0:T(8,128)(2,1)} copy(bf16[2,4,32,32,128]{4,2,3,1,0:T(8,128)(2,1)S(1)} %fusion) | data formatting | bytes 4194304 | tf_op jit(solution)/shard_map/transpose | solution.py:262
  (112 shorter events, 28.1 us)
Async XLA Ops:
  3.6 40.3 %collective-permute-start.4 = (bf16[2,27,32,128]{3,2,1,0:T(8,128)(2,1)}, bf16[2,27,32,128]{3,2,1,0:T(8,128)(2,1)}, u32[]{:S(2)}, u32[]{:S(2)}) collective-permute-start(bf16[2,27,32,128]{3,2,1,0:T(8,128)(2,1)} %get-tuple-element.62), channel_id=1, source_target_pairs={{0,2},{1,3},{2,0},{3,1},{4,6},{5,7},{6,4},{7,5},{8,10},{9,11},{10,... | collective-permute-start | bytes 1327112 | tf_op jit(solution)/shard_map/ppermute | solution.py:15
  7.2 72.8 %copy-start = (bf16[2,4,32,32,128]{4,2,3,1,0:T(8,128)(2,1)}, bf16[2,4,32,32,128]{4,2,3,1,0:T(8,128)(2,1)S(1)}, u32[]{:S(2)}) copy-start(bf16[2,4,32,32,128]{4,2,3,1,0:T(8,128)(2,1)S(1)} %copy.44) | copy-start | bytes 6291460
  7.3 3.3 %copy-start.17 = (f32[32]{0:T(128)S(1)}, f32[32]{0:T(128)}, u32[]{:S(2)}) copy-start(f32[32]{0:T(128)} %param.9) | copy-start | bytes 388
  7.3 3.2 %copy-start.18 = (f32[32]{0:T(128)S(1)}, f32[32]{0:T(128)}, u32[]{:S(2)}) copy-start(f32[32]{0:T(128)} %param.7) | copy-start | bytes 388
  8.1 34.6 %collective-permute-start.10 = (bf16[4,12,32,128]{3,2,1,0:T(8,128)(2,1)}, bf16[4,12,32,128]{3,2,1,0:T(8,128)(2,1)S(1)}, u32[]{:S(2)}, u32[]{:S(2)}) collective-permute-start(bf16[4,12,32,128]{3,2,1,0:T(8,128)(2,1)} %slice.180), channel_id=1, source_target_pairs={{0,2},{1,3},{2,0},{3,1},{4,6},{5,7},{6,4},{7,5},{8,10},{9,11},{10,... | collective-permute-start | bytes 1179656 | tf_op jit(solution)/shard_map/ppermute | solution.py:15
  9.3 38.3 %collective-permute-start = (bf16[4,20,32,128]{3,2,1,0:T(8,128)(2,1)}, bf16[4,20,32,128]{3,2,1,0:T(8,128)(2,1)S(1)}, u32[]{:S(2)}, u32[]{:S(2)}) collective-permute-start(bf16[4,20,32,128]{3,2,1,0:T(8,128)(2,1)} %pad_maximum_fusion.2), channel_id=1, source_target_pairs={{0,2},{1,3},{2,0},{3,1},{4,6},{5,7},{6,4},{7,5},{8,10},{9,11},{10,... | collective-permute-start | bytes 1966088 | tf_op jit(solution)/shard_map/ppermute | solution.py:15
  10.6 26.7 %collective-permute-start.6 = (f32[2,32]{1,0:T(2,128)S(1)}, f32[2,32]{1,0:T(2,128)S(1)}, u32[]{:S(2)}, u32[]{:S(2)}) collective-permute-start(f32[2,32]{1,0:T(2,128)S(1)} %pad_maximum_fusion.12), channel_id=1, source_target_pairs={{0,2},{1,3},{2,0},{3,1},{4,6},{5,7},{6,4},{7,5},{8,10},{9,11},{10,... | collective-permute-start | bytes 776 | tf_op jit(solution)/shard_map/ppermute | solution.py:15
  37.3 3.0 %copy-start.19 = (f32[2,32]{1,0:T(2,128)}, f32[2,32]{1,0:T(2,128)S(1)}, u32[]{:S(2)}) copy-start(f32[2,32]{1,0:T(2,128)S(1)} %collective-permute-done.6) | copy-start | bytes 772
  37.9 3.5 %collective-permute-start.7 = (f32[2,64]{1,0:T(2,128)}, f32[2,64]{1,0:T(2,128)}, u32[]{:S(2)}, u32[]{:S(2)}) collective-permute-start(f32[2,64]{1,0:T(2,128)} %pad_maximum_fusion.13), channel_id=1, source_target_pairs={{0,1},{1,0},{2,3},{3,2},{4,5},{5,4},{6,7},{7,6},{8,9},{9,8},{10,11... | collective-permute-start | bytes 1544 | tf_op jit(solution)/shard_map/ppermute | solution.py:15
  43.7 2.1 %copy-start.7 = (bf16[1,2,27,32,128]{4,3,2,1,0:T(8,128)(2,1)S(1)}, bf16[1,2,27,32,128]{4,3,2,1,0:T(8,128)(2,1)}, u32[]{:S(2)}) copy-start(bf16[1,2,27,32,128]{4,3,2,1,0:T(8,128)(2,1)} %get-tuple-element.61) | copy-start | bytes 1327108
  43.7 5.4 %collective-permute-start.11 = (bf16[2,4,8,32,128]{4,3,2,0,1:T(8,128)(2,1)S(1)}, bf16[2,4,8,32,128]{4,3,2,0,1:T(8,128)(2,1)S(1)}, u32[]{:S(2)}, u32[]{:S(2)}) collective-permute-start(bf16[2,4,8,32,128]{4,3,2,0,1:T(8,128)(2,1)S(1)} %pad_maximum_fusion.4), channel_id=1, source_target_pairs={{0,1},{1,0},{2,3},{3,2},{4,5},{5,4},{6,7},{7,6},{8,9},{9,8},{10,11... | collective-permute-start | bytes 1572872 | tf_op jit(solution)/shard_map/ppermute | solution.py:15
  45.9 2.0 %copy-start.9 = (bf16[2,27,32,32]{3,2,1,0:T(8,128)(2,1)S(1)}, bf16[2,27,32,32]{3,2,1,0:T(8,128)(2,1)}, u32[]{:S(2)}) copy-start(bf16[2,27,32,32]{3,2,1,0:T(8,128)(2,1)} %get-tuple-element.53) | copy-start | bytes 331780
  47.1 13.8 %collective-permute-start.5 = (bf16[2,2,27,32,128]{4,3,2,1,0:T(8,128)(2,1)S(1)}, bf16[2,2,27,32,128]{4,3,2,1,0:T(8,128)(2,1)S(1)}, u32[]{:S(2)}, u32[]{:S(2)}) collective-permute-start(bf16[2,2,27,32,128]{4,3,2,1,0:T(8,128)(2,1)S(1)} %pad_maximum_fusion.1), channel_id=1, source_target_pairs={{0,1},{1,0},{2,3},{3,2},{4,5},{5,4},{6,7},{7,6},{8,9},{9,8},{10,11... | collective-permute-start | bytes 2654216 | tf_op jit(solution)/shard_map/ppermute | solution.py:15
  47.8 7.7 %collective-permute-start.1 = (bf16[2,4,10,32,128]{4,3,2,0,1:T(8,128)(2,1)S(1)}, bf16[2,4,10,32,128]{4,3,2,0,1:T(8,128)(2,1)S(1)}, u32[]{:S(2)}, u32[]{:S(2)}) collective-permute-start(bf16[2,4,10,32,128]{4,3,2,0,1:T(8,128)(2,1)S(1)} %pad_maximum_fusion.3), channel_id=1, source_target_pairs={{0,1},{1,0},{2,3},{3,2},{4,5},{5,4},{6,7},{7,6},{8,9},{9,8},{10,11... | collective-permute-start | bytes 1966088 | tf_op jit(solution)/shard_map/ppermute | solution.py:15
  47.9 4.4 %copy-start.15 = (bf16[1,8,32,128]{3,2,1,0:T(8,128)(2,1)S(1)}, bf16[1,8,32,128]{3,2,1,0:T(8,128)(2,1)}, u32[]{:S(2)}) copy-start(bf16[1,8,32,128]{3,2,1,0:T(8,128)(2,1)} %get-tuple-element.67) | copy-start | bytes 196612
  49.1 6.5 %copy-start.13 = (bf16[1,10,32,128]{3,2,1,0:T(8,128)(2,1)S(1)}, bf16[1,10,32,128]{3,2,1,0:T(8,128)(2,1)}, u32[]{:S(2)}) copy-start(bf16[1,10,32,128]{3,2,1,0:T(8,128)(2,1)} %get-tuple-element.65) | copy-start | bytes 245764
  49.2 45.9 %collective-permute-start.12 = (bf16[4,8,32,128]{3,2,1,0:T(8,128)(2,1)S(1)}, bf16[4,8,32,128]{3,2,1,0:T(8,128)(2,1)S(1)}, u32[]{:S(2)}, u32[]{:S(2)}) collective-permute-start(bf16[4,8,32,128]{3,2,1,0:T(8,128)(2,1)S(1)} %pad_maximum_fusion.8), channel_id=1, source_target_pairs={{0,4},{4,8},{8,12},{12,16},{16,20},{20,24},{24,28},{1,5},{5,9},{9,... | collective-permute-start | bytes 786440 | tf_op jit(solution)/shard_map/ppermute | solution.py:20
  52.4 42.7 %collective-permute-start.13 = (bf16[4,8,32,128]{3,2,1,0:T(8,128)(2,1)S(1)}, bf16[4,8,32,128]{3,2,1,0:T(8,128)(2,1)S(1)}, u32[]{:S(2)}, u32[]{:S(2)}) collective-permute-start(bf16[4,8,32,128]{3,2,1,0:T(8,128)(2,1)S(1)} %pad_maximum_fusion.9), channel_id=1, source_target_pairs={{4,0},{8,4},{12,8},{16,12},{20,16},{24,20},{28,24},{5,1},{9,5},{13... | collective-permute-start | bytes 786440 | tf_op jit(solution)/shard_map/ppermute | solution.py:25
  55.6 24.3 %collective-permute-start.3 = (bf16[4,10,32,128]{3,2,1,0:T(8,128)(2,1)S(1)}, bf16[4,10,32,128]{3,2,1,0:T(8,128)(2,1)S(1)}, u32[]{:S(2)}, u32[]{:S(2)}) collective-permute-start(bf16[4,10,32,128]{3,2,1,0:T(8,128)(2,1)S(1)} %pad_maximum_fusion.7), channel_id=1, source_target_pairs={{4,0},{8,4},{12,8},{16,12},{20,16},{24,20},{28,24},{5,1},{9,5},{13... | collective-permute-start | bytes 983048 | tf_op jit(solution)/shard_map/ppermute | solution.py:25
  57.8 22.1 %collective-permute-start.2 = (bf16[4,10,32,128]{3,2,1,0:T(8,128)(2,1)S(1)}, bf16[4,10,32,128]{3,2,1,0:T(8,128)(2,1)S(1)}, u32[]{:S(2)}, u32[]{:S(2)}) collective-permute-start(bf16[4,10,32,128]{3,2,1,0:T(8,128)(2,1)S(1)} %pad_maximum_fusion.6), channel_id=1, source_target_pairs={{0,4},{4,8},{8,12},{12,16},{16,20},{20,24},{24,28},{1,5},{5,9},{9,... | collective-permute-start | bytes 983048 | tf_op jit(solution)/shard_map/ppermute | solution.py:20
  88.9 31.2 %collective-permute-start.8 = (bf16[9,128,128]{2,1,0:T(8,128)(2,1)}, bf16[9,128,128]{2,1,0:T(8,128)(2,1)S(1)}, u32[]{:S(2)}, u32[]{:S(2)}) collective-permute-start(bf16[9,128,128]{2,1,0:T(8,128)(2,1)} %get-tuple-element.19.refs_3_.refs_8_), channel_id=1, source_target_pairs={{0,4},{4,8},{8,12},{12,16},{16,20},{20,24},{24,28},{1,5},{5,9},{9,... | collective-permute-start | bytes 884744 | tf_op jit(solution)/shard_map/ppermute | solution.py:20
  90.8 29.3 %collective-permute-start.9 = (bf16[9,128,128]{2,1,0:T(8,128)(2,1)S(1)}, bf16[9,128,128]{2,1,0:T(8,128)(2,1)S(1)}, u32[]{:S(2)}, u32[]{:S(2)}) collective-permute-start(bf16[9,128,128]{2,1,0:T(8,128)(2,1)S(1)} %get-tuple-element.20.refs_1_.refs_6_), channel_id=1, source_target_pairs={{4,0},{8,4},{12,8},{16,12},{20,16},{24,20},{28,24},{5,1},{9,5},{13... | collective-permute-start | bytes 884744 | tf_op jit(solution)/shard_map/ppermute | solution.py:25
  103.4 11.0 %copy-start.1 = (bf16[8,128,128]{2,1,0:T(8,128)(2,1)}, bf16[8,128,128]{2,1,0:T(8,128)(2,1)S(1)}, u32[]{:S(2)}) copy-start(bf16[8,128,128]{2,1,0:T(8,128)(2,1)S(1)} %get-tuple-element.23.refs_3_) | copy-start | bytes 786436
  103.4 13.4 %collective-permute-start.14 = (bf16[8,128,128]{2,1,0:T(8,128)(2,1)S(1)}, bf16[8,128,128]{2,1,0:T(8,128)(2,1)S(1)}, u32[]{:S(2)}, u32[]{:S(2)}) collective-permute-start(bf16[8,128,128]{2,1,0:T(8,128)(2,1)S(1)} %get-tuple-element.23.refs_3_), channel_id=1, source_target_pairs={{0,4},{4,8},{8,12},{12,16},{16,20},{20,24},{24,28},{1,5},{5,9},{9,... | collective-permute-start | bytes 786440 | tf_op jit(solution)/shard_map/ppermute | solution.py:20
  105.3 14.7 %collective-permute-start.15 = (bf16[8,128,128]{2,1,0:T(8,128)(2,1)S(1)}, bf16[8,128,128]{2,1,0:T(8,128)(2,1)S(1)}, u32[]{:S(2)}, u32[]{:S(2)}) collective-permute-start(bf16[8,128,128]{2,1,0:T(8,128)(2,1)S(1)} %get-tuple-element.24.refs_1_), channel_id=1, source_target_pairs={{4,0},{8,4},{12,8},{16,12},{20,16},{24,20},{28,24},{5,1},{9,5},{13... | collective-permute-start | bytes 786440 | tf_op jit(solution)/shard_map/ppermute | solution.py:25
  111.2 8.9 %copy-start.20 = (f32[128]{0:T(128)S(1)}, f32[128]{0:T(128)}, u32[]{:S(2)}) copy-start(f32[128]{0:T(128)} %get-tuple-element.77) | copy-start | bytes 1540
  130.8 12.1 %collective-permute-start.16 = (bf16[4,8,32,128]{3,2,1,0:T(8,128)(2,1)S(1)}, bf16[4,8,32,128]{3,2,1,0:T(8,128)(2,1)S(1)}, u32[]{:S(2)}, u32[]{:S(2)}) collective-permute-start(bf16[4,8,32,128]{3,2,1,0:T(8,128)(2,1)S(1)} %get-tuple-element.27), channel_id=1, source_target_pairs={{0,1},{1,0},{2,3},{3,2},{4,5},{5,4},{6,7},{7,6},{8,9},{9,8},{10,11... | collective-permute-start | bytes 786440 | tf_op jit(solution)/shard_map/ppermute | solution.py:15
  139.5 4.5 %collective-permute-start.17 = (bf16[4,8,32,128]{3,2,1,0:T(8,128)(2,1)}, bf16[4,8,32,128]{3,2,1,0:T(8,128)(2,1)S(1)}, u32[]{:S(2)}, u32[]{:S(2)}) collective-permute-start(bf16[4,8,32,128]{3,2,1,0:T(8,128)(2,1)} %get-tuple-element.28), channel_id=1, source_target_pairs={{0,1},{1,0},{2,3},{3,2},{4,5},{5,4},{6,7},{7,6},{8,9},{9,8},{10,11... | collective-permute-start | bytes 786440 | tf_op jit(solution)/shard_map/ppermute | solution.py:15
  139.6 7.5 %collective-permute-start.19 = (bf16[4,8,32,128]{3,2,1,0:T(8,128)(2,1)S(1)}, bf16[4,8,32,128]{3,2,1,0:T(8,128)(2,1)S(1)}, u32[]{:S(2)}, u32[]{:S(2)}) collective-permute-start(bf16[4,8,32,128]{3,2,1,0:T(8,128)(2,1)S(1)} %get-tuple-element.30), channel_id=1, source_target_pairs={{0,2},{1,3},{2,0},{3,1},{4,6},{5,7},{6,4},{7,5},{8,10},{9,11},{10,... | collective-permute-start | bytes 786440 | tf_op jit(solution)/shard_map/ppermute | solution.py:15
  140.8 13.3 %collective-permute-start.20 = (bf16[4,8,32,128]{3,2,1,0:T(8,128)(2,1)S(1)}, bf16[4,8,32,128]{3,2,1,0:T(8,128)(2,1)S(1)}, u32[]{:S(2)}, u32[]{:S(2)}) collective-permute-start(bf16[4,8,32,128]{3,2,1,0:T(8,128)(2,1)S(1)} %get-tuple-element.31), channel_id=1, source_target_pairs={{0,3},{1,2},{2,1},{3,0},{4,7},{5,6},{6,5},{7,4},{8,11},{9,10},{10,... | collective-permute-start | bytes 786440 | tf_op jit(solution)/shard_map/ppermute | solution.py:15
  141.7 16.6 %collective-permute-start.18 = (bf16[4,8,32,128]{3,2,1,0:T(8,128)(2,1)S(1)}, bf16[4,8,32,128]{3,2,1,0:T(8,128)(2,1)S(1)}, u32[]{:S(2)}, u32[]{:S(2)}) collective-permute-start(bf16[4,8,32,128]{3,2,1,0:T(8,128)(2,1)S(1)} %get-tuple-element.29), channel_id=1, source_target_pairs={{0,2},{1,3},{2,0},{3,1},{4,6},{5,7},{6,4},{7,5},{8,10},{9,11},{10,... | collective-permute-start | bytes 786440 | tf_op jit(solution)/shard_map/ppermute | solution.py:15
  143.6 20.9 %collective-permute-start.21 = (bf16[4,8,32,128]{3,2,1,0:T(8,128)(2,1)S(1)}, bf16[4,8,32,128]{3,2,1,0:T(8,128)(2,1)S(1)}, u32[]{:S(2)}, u32[]{:S(2)}) collective-permute-start(bf16[4,8,32,128]{3,2,1,0:T(8,128)(2,1)S(1)} %get-tuple-element.32), channel_id=1, source_target_pairs={{0,3},{1,2},{2,1},{3,0},{4,7},{5,6},{6,5},{7,4},{8,11},{9,10},{10,... | collective-permute-start | bytes 786440 | tf_op jit(solution)/shard_map/ppermute | solution.py:15
  (11 other events, 14.3 us)

commit v2 on v0

v2 whole, which is shorter than its diff:
```python
import functools

import jax
import jax.numpy as jnp
from jax import lax
from jax.experimental import pallas as pl
from jax.experimental.pallas import tpu as pltpu
from jax.sharding import PartitionSpec as P

BF = jnp.bfloat16
VMEM_LIMIT = 48 * 2**20
PARTS = 2


def chan_swap(value, k):
    return lax.ppermute(value, "chan", [(i, i ^ k) for i in range(4)])


def slab_swap(value, odd):
    size = lax.axis_size("slab")
    pairs = [(i, i + 1) for i in range(odd, size - 1, 2)]
    return lax.ppermute(value, "slab", pairs + [(j, i) for i, j in pairs])


def after(value, *earlier):
    return lax.optimization_barrier((value, earlier))[0]


def position():
    me = lax.axis_index("chan")
    return me, me // 2, me % 2, 1 - lax.axis_index("slab") % 2


def layer_at(r, depth, even):
    return jnp.where(even == 1, depth - 1 - r, r)


def conv_rows(x, w, bias, depth, count, even, store):
    chans, width = x.shape[2], x.shape[3]
    lane = lax.broadcasted_iota(jnp.int32, (chans, width), 1)

    def step(j, _):
        for r in range(0, depth, 2):
            cols = [
                jnp.concatenate(
                    [x[layer_at(r + u, depth, even) + a, j + c] for a in range(3) for c in range(3)], axis=0
                )
                for u in range(2)
            ]
            lhs = jnp.concatenate([w[3 * k : 3 * k + 3].reshape(3 * chans, chans) for k in range(9)], axis=1)
            acc = jnp.dot(lhs, jnp.concatenate(cols, axis=1), preferred_element_type=jnp.float32)
            for u in range(2):
                part = acc[:, u * width : (u + 1) * width]
                before = jnp.where(lane == 0, 0.0, pltpu.roll(part[:chans], 1, 1))
                later = jnp.where(lane == width - 1, 0.0, pltpu.roll(part[2 * chans :], width - 1, 1))
                total = before + part[chans : 2 * chans] + later
                store(r + u, j, jnp.maximum(total + bias[...], 0.0).astype(BF))
        return 0

    lax.fori_loop(0, count, step, 0)


def run_copies(pairs, sems, meanwhile):
    copies = [pltpu.make_async_copy(s, d, sems.at[i]) for i, (s, d) in enumerate(pairs)]
    for copy in copies:
        copy.start()
    meanwhile()
    for copy in copies:
        copy.wait()


def clear_edge(x, c, old):
    def clear():
        if not old:
            for z in range(x.shape[0]):
                x[z, jnp.where(c == 0, 0, x.shape[1] - 1)] = jnp.zeros(x.shape[2:], BF)

    return clear


def places(old, new, c):
    n = new[0].shape[1]
    if not old:
        return [(new, 0, n, 1 - c)]
    m = old[0].shape[1]
    return [(new, 0, n, 2 - 2 * c), (old, (1 - c) * (m - 2), 2, c * n)]


def first_kernel_body(count, has_old, *refs):
    new, refs = refs[:6], refs[6:]
    old, refs = (refs[:6], refs[6:]) if has_old else (None, refs)
    weights, bias, (out_a, out_mid, out_b, x, w, sems) = refs[:4], refs[4], refs[5:]
    me, _, c, even = position()
    depth, unit = new[0].shape[0], new[0].shape[2]
    pairs = []
    for k in range(4):
        pairs.append((weights[k].at[0], w.at[:, pl.ds(k * unit, unit)]))
    for arrays, start, n, dst in places(old, new, c):
        src, to = pl.ds(start, n), pl.ds(dst, n)
        for k in range(4):
            chan = pl.ds(pl.multiple_of((me ^ k) * unit, unit), unit)
            pairs.append((arrays[k].at[:, src], x.at[pl.ds(1, depth), to, chan]))
            pairs.append((arrays[4].at[k, src], x.at[1 + layer_at(-1, depth, even), to, chan]))
            pairs.append((arrays[5].at[k, src], x.at[1 + layer_at(depth, depth, even), to, chan]))
    run_copies(pairs, sems, clear_edge(x, c, old))

    def store(r, j, value):
        if r == 0:
            out_a[0, j] = value
        elif r == depth - 1:
            out_b[0, j] = value
        else:
            out_mid[r - 1, j] = value

    conv_rows(x, w, bias, depth, count, even, store)


def second_kernel_body(count, has_old, *refs):
    new, refs = refs[:5], refs[5:]
    old, refs = (refs[:5], refs[5:]) if has_old else (None, refs)
    w, bias, outs, (x, sems) = refs[0], refs[1], refs[2:6], refs[6:]
    _, _, c, even = position()
    depth, unit = x.shape[0] - 2, outs[0].shape[2]
    pairs = []
    for arrays, start, n, dst in places(old, new, c):
        src, to = pl.ds(start, n), pl.ds(dst, n)
        r = -1
        for part in arrays:
            for k in range(part.shape[0]):
                pairs.append((part.at[k, src], x.at[1 + layer_at(r, depth, even), to]))
                r += 1
    run_copies(pairs, sems, clear_edge(x, c, old))

    def store(r, j, value):
        for k in range(4):
            outs[k][layer_at(r, depth, even), j] = value[k * unit : (k + 1) * unit]

    conv_rows(x, w, bias, depth, count, even, store)


def weights_kernel_body(*refs):
    pieces, (out, w, sems) = refs[:4], refs[4:]
    me = lax.axis_index("chan")
    unit = pieces[0].shape[2]
    run_copies([(pieces[k].at[1], w.at[:, pl.ds(k * unit, unit)]) for k in range(4)], sems, lambda: None)

    def step(i, _):
        turned = jnp.transpose(w[i])
        for q in range(4):
            out[i, pl.ds(pl.multiple_of((me ^ q) * unit, unit), unit)] = turned[q * unit : (q + 1) * unit]
        return 0

    lax.fori_loop(0, w.shape[0], step, 0, unroll=3)


def call(body, outs, any_operands, vmem_operands, scratch, n_copies, flops):
    any_spec = pl.BlockSpec(memory_space=pl.ANY)
    vmem = pl.BlockSpec(memory_space=pltpu.VMEM)
    return pl.pallas_call(
        body,
        out_shape=[jax.ShapeDtypeStruct(s, BF) for s in outs],
        in_specs=[any_spec] * len(any_operands) + [vmem] * len(vmem_operands),
        out_specs=[vmem] * len(outs),
        scratch_shapes=[*(pltpu.VMEM(s, BF) for s in scratch), pltpu.SemaphoreType.DMA((n_copies,))],
        cost_estimate=pl.CostEstimate(flops=flops, bytes_accessed=2**21, transcendentals=0),
        compiler_params=pltpu.CompilerParams(vmem_limit_bytes=VMEM_LIMIT),
    )(*any_operands, *vmem_operands)


def body(volume, first_kernel, first_bias, second_kernel, second_bias):
    _, depth, unit, thick, width = volume.shape
    chans = 4 * unit
    half = thick // 2
    _, b, c, even = position()
    ends = [half * k // PARTS for k in range(PARTS + 1)]
    in_ends = [0] + [e + 2 for e in ends[1:]]
    hidden_ends = [0] + [e + 1 for e in ends[1:]]

    def cut(chunk, k):
        first, last = in_ends[chunk], in_ends[chunk + 1]
        start = jnp.where(c ^ (k & 1) == 0, first, thick - last)
        zero = jnp.int32(0)
        part = lax.dynamic_slice(
            volume, (b ^ (k >> 1), zero, zero, start, zero), (1, depth, unit, last - first, width)
        )
        return jnp.transpose(part[0], (0, 2, 1, 3))

    def outer(value, r):
        return lax.dynamic_index_in_dim(value, layer_at(r, depth, even), 0, keepdims=False)

    received = []
    got = None
    weights = None
    for chunk in range(PARTS):
        sent = [cut(chunk, k) for k in (2, 3, 1)]
        if got is not None:
            sent = after(sent, got)
        got = [chan_swap(v, k) for v, k in zip(sent, (2, 3, 1))]
        v = [cut(chunk, 0), got[2], got[0], got[1]]
        side = [slab_swap(jnp.stack([outer(p, r) for p in v]), odd) for odd, r in ((0, 0), (1, depth - 1))]
        received.append((*v, *side))
        if chunk == 0:
            w1 = jnp.transpose(first_kernel, (0, 1, 2, 4, 3)).reshape(27, unit, chans)
            mine = jnp.stack([w1, second_kernel.reshape(27, unit, chans)])
            across = chan_swap(after(mine, got), 2)
            weights = (mine, chan_swap(mine, 1), across, chan_swap(across, 1))

    biases = jnp.stack([first_bias, second_bias])
    biases = jnp.concatenate([biases, chan_swap(biases, 1)], axis=1)
    biases = jnp.concatenate([biases, chan_swap(biases, 2)], axis=1)
    bias1, bias2 = (jnp.broadcast_to(v[:, None], (chans, width)) for v in biases)
    full2 = call(weights_kernel_body, [(27, chans, chans)], weights, (), [(27, chans, chans)], 4, 10**9)[0]

    unit_flops = 3 * 2 * depth * width * 27 * chans * chans
    hidden = []
    for chunk in range(PARTS):
        n = hidden_ends[chunk + 1] - hidden_ends[chunk]
        operands = received[chunk] + (received[chunk - 1] if chunk else ())
        edge_a, mid, edge_b = call(
            functools.partial(first_kernel_body, n, chunk > 0),
            [(1, n, chans, width), (depth - 2, n, chans, width), (1, n, chans, width)],
            (*operands, *weights), (bias1,),
            [(depth + 2, n + 2, chans, width), (27, chans, chans)],
            4 + 12 * (1 + (chunk > 0)), unit_flops * n,
        )
        hidden.append((slab_swap(edge_a, 0), edge_a, mid, edge_b, slab_swap(edge_b, 1)))

    done = []
    for chunk in range(PARTS):
        n = ends[chunk + 1] - ends[chunk]
        operands = hidden[chunk] + (hidden[chunk - 1] if chunk else ())
        outs = call(
            functools.partial(second_kernel_body, n, chunk > 0),
            [(depth, n, unit, width)] * 4,
            operands, (full2, bias2),
            [(depth + 2, n + 2, chans, width)],
            (depth + 2) * (1 + (chunk > 0)), unit_flops * n,
        )
        done.append([outs[0], *(chan_swap(outs[k], k) for k in (1, 2, 3))])

    def halves(near, far):
        lower = jnp.concatenate(near + far[::-1], axis=1)
        upper = jnp.concatenate(far + near[::-1], axis=1)
        return jnp.where(c == 0, lower, upper)

    home = halves([d[0] for d in done], [d[1] for d in done])
    away = halves([d[2] for d in done], [d[3] for d in done])
    out = jnp.where(b == 0, jnp.stack([home, away]), jnp.stack([away, home]))
    return jnp.transpose(out, (0, 1, 3, 2, 4))


def solution(mesh):
    return jax.shard_map(
        body,
        mesh=mesh,
        in_specs=(
            P(None, "slab", "chan", None, None),
            P(None, None, None, None, "chan"),
            P("chan"),
            P(None, None, None, "chan", None),
            P("chan"),
        ),
        out_specs=P(None, "slab", "chan", None, None),
        check_vma=False,
    )
```

time: 599 us -> 128 us (0.21)
  waiting for transfers between devices: 281 us -> 55 us
  local copies, waits for them, and re-layouts: 150 us -> 9.53 us
  matrix products: 114 us -> 0 us
  Pallas kernels: 0 us -> 30.2 us
  other arithmetic: 25.3 us -> 2.88 us
  starting transfers between devices: 12.5 us -> 29.1 us
  between operations: 13.8 us -> 0.43 us
    reduce_scatter x1 -> x0, waiting for transfers between devices: 126 us -> none  [body(): lax.psum_scatter(partial_value, 'chan', scatter_dimension=2, tiled=True)]
    conv_general_dilated x2 -> x0, matrix products: 114 us -> none  [convolve(): lax.conv_general_dilated(values_in, kernel, (1, 1, 1), ((0, 0), (1, 1), (...]
    all_gather x1 -> x0, waiting for transfers between devices: 59.8 us -> none  [body(): gathered = lax.all_gather(volume, 'chan', axis=2, tiled=True)]
    conv_general_dilated x6 -> x0, local copies, waits for them, and re-layouts: 55.2 us -> none  [convolve(): lax.conv_general_dilated(values_in, kernel, (1, 1, 1), ((0, 0), (1, 1), (...]
    ppermute x4 -> x25, waiting for transfers between devices: 95.4 us -> 55 us  [the longest x17 45.4 us: chan_swap(): return lax.ppermute(value, 'chan', [(i, i ^ k) for i in range(4)])]
    pallas_call x0 -> x5, Pallas kernels: none -> 30.2 us  [call(): pl.pallas_call(body, out_shape=[jax.ShapeDtypeStruct(s, BF) for s in outs...]
    convert_element_type x6 -> x0, local copies, waits for them, and re-layouts: 24 us -> none  [activate(): jax.nn.relu(summed + bias_row[None, None, :, None, None])]
    unnamed x16 -> x6, local copies, waits for them, and re-layouts: 23.7 us -> 0.01 us
  transfers between devices with their start and end apart: 6 -> 25, of which waited for: 5 -> 9; matrix products, arithmetic and copies ran while one was open for 3% -> 7% of each run, Pallas kernels for 0% -> 18%
where the time goes in v2:
time: 128 us; the launch traced here: 127 us
  waiting for transfers between devices  55 us (43%)
  Pallas kernels  30.2 us (24%)
  starting transfers between devices  29.1 us (23%)
  local copies, waits for them, and re-layouts  9.53 us (7%)
  other arithmetic  2.88 us (2%)
    ppermute x17, waiting for transfers between devices, chan_swap(): return lax.ppermute(value, 'chan', [(i, i ^ k) for i in range(4)])  45.4 us
    pallas_call x5, Pallas kernels, call(): pl.pallas_call(body, out_shape=[jax.ShapeDtypeStruct(s, BF) for s in outs...  30.2 us
    ppermute x8, starting transfers between devices, slab_swap(): return lax.ppermute(value, 'slab', pairs + [(j, i) for i, j in pairs])  15.3 us
    ppermute x17, starting transfers between devices, chan_swap(): return lax.ppermute(value, 'chan', [(i, i ^ k) for i in range(4)])  13.8 us
    ppermute x8, waiting for transfers between devices, slab_swap(): return lax.ppermute(value, 'slab', pairs + [(j, i) for i, j in pairs])  9.62 us
    dynamic_slice x8, local copies, waits for them, and re-layouts, cut(): lax.dynamic_slice(volume, (b ^ k >> 1, zero, zero, start, zero), (1, dept...  4.87 us
  transfers between devices with their start and end apart: 25, of which 9 were waited for; matrix products, arithmetic and copies ran while one was open for 7% of the time, Pallas kernels for 18%

profile of v2, /device:TPU:25, one launch (start us, length us, event | category | flops | bytes accessed | tf_op | source)
XLA Modules:
  0.0 127.2 jit_solution(8825582714057903076)
XLA Ops:
  1.4 1.1 pad_maximum_fusion.refs_6_.refs_0_.refs_12_
  2.6 2.5 %constant_dynamic-slice_fusion.20 = (bf16[1,4,32,10,128]{4,3,2,1,0:T(8,128)(2,1)S(1)}, bf16[1,4,32,10,128]{4,3,2,1,0:T(8,128)(2,1)S(1)}, bf16[1,4,32,10,128]{4,3...) fusion(bf16[2,4,32,32,128]{4,3,2,1,0:T(8,128)(2,1)} %param.5, s32[]{:T(128)S(6)} %select_n.141, s32[]{:T(128)S(6)} %select_n.140, ...), kind=kLoop, calls=%fused_computation.41 | loop fusion | bytes 2621456 | tf_op jit(solution)/shard_map/dynamic_slice | solution.py:183
  5.8 1.3 %collective-permute-start.1 = (bf16[4,10,32,128]{3,2,1,0:T(8,128)(2,1)S(1)}, bf16[4,10,32,128]{3,2,1,0:T(8,128)(2,1)S(1)}, u32[]{:S(2)}, u32[]{:S(2)}) collective-permute-start(bf16[4,10,32,128]{3,2,1,0:T(8,128)(2,1)S(1)} %bitcast.86), channel_id=1, source_target_pairs={{0,2},{1,3},{2,0},{3,1},{4,6},{5,7},{6,4},{7,5},{8,10},{9,11},{10,... | collective-permute-start | bytes 983048 | tf_op jit(solution)/shard_map/ppermute | solution.py:16
  7.7 1.9 %constant_dynamic-slice_fusion.8 = (bf16[1,4,32,8,128]{4,3,2,1,0:T(8,128)(2,1)S(1)}, bf16[1,4,32,8,128]{4,3,2,1,0:T(8,128)(2,1)S(1)}, bf16[1,4,32,8,128]{4,3,2,1,0:T(8,128)(2,1)S(1)}, bf16[1,4,32,8,128]{4,3,2,1,0:T(8,128)(2,1)S(1)}) fusion(bf16[2,4,32,32,128]{4,3,2,1,0:T(8,128)(2,1)} %param.5, s32[]{:T(128)S(6)} %select_n.138, s32[]{:T(128)S(6)} %select_n.150, ...), kind=kLoop, calls=%fused_computation.29 | loop fusion | bytes 2097168 | tf_op jit(solution)/shard_map/dynamic_slice | solution.py:183
  9.7 1.1 constant_dynamic-slice_fusion.15
  10.8 1.0 constant_dynamic-slice_fusion.3
  12.0 1.2 collective-permute-start.9
  13.5 8.7 %collective-permute-done.9 = f32[2,64]{1,0:T(2,128)S(1)} collective-permute-done((f32[2,64]{1,0:T(2,128)S(1)}, f32[2,64]{1,0:T(2,128)S(1)}, u32[]{:S(2)}, u32[]{:S(2)}) %collective-permute-start.9) | collective-permute-done | bytes 544 | tf_op jit(solution)/shard_map/ppermute | solution.py:16
  23.2 1.2 collective-permute-start.13
  24.9 1.2 collective-permute-start.6
  26.3 1.3 %collective-permute-start.3 = (bf16[4,10,32,128]{3,2,1,0:T(8,128)(2,1)S(1)}, bf16[4,10,32,128]{3,2,1,0:T(8,128)(2,1)S(1)}, u32[]{:S(2)}, u32[]{:S(2)}) collective-permute-start(bf16[4,10,32,128]{3,2,1,0:T(8,128)(2,1)S(1)} %pad_maximum_fusion.1), channel_id=1, source_target_pairs={{0,4},{8,12},{16,20},{24,28},{4,0},{12,8},{20,16},{28,24},{1,5},{9... | collective-permute-start | bytes 983048 | tf_op jit(solution)/shard_map/ppermute | solution.py:22
  27.6 3.5 %collective-permute-done.13.refs_2_ = bf16[4,8,32,128]{3,2,1,0:T(8,128)(2,1)S(1)} collective-permute-done((bf16[4,8,32,128]{3,2,1,0:T(8,128)(2,1)S(1)}, bf16[4,8,32,128]{3,2,1,0:T(8,128)(2,1)S(1)}, u32[]{:S(2)}, u32[]{:S(2)}) %collective-permute-start.13) | collective-permute-done | bytes 262176 | tf_op jit(solution)/shard_map/ppermute | solution.py:16
  31.1 3.0 %collective-permute-start.4 = (bf16[4,10,32,128]{3,2,1,0:T(8,128)(2,1)S(1)}, bf16[4,10,32,128]{3,2,1,0:T(8,128)(2,1)S(1)}, u32[]{:S(2)}, u32[]{:S(2)}) collective-permute-start(bf16[4,10,32,128]{3,2,1,0:T(8,128)(2,1)S(1)} %pad_maximum_fusion.2), channel_id=1, source_target_pairs={{4,8},{12,16},{20,24},{8,4},{16,12},{24,20},{5,9},{13,17},{21,25},... | collective-permute-start | bytes 983048 | tf_op jit(solution)/shard_map/ppermute | solution.py:22
  34.1 12.1 %collective-permute-done.6.refs_8_.refs_2_.refs_14_ = bf16[2,27,32,128]{3,2,1,0:T(8,128)(2,1)S(1)} collective-permute-done((bf16[2,27,32,128]{3,2,1,0:T(8,128)(2,1)S(1)}, bf16[2,27,32,128]{3,2,1,0:T(8,128)(2,1)S(1)}, u32[]{:S(2)}, u32[]{:S(2)}) %collective-permute-start.6) | collective-permute-done | bytes 442400 | tf_op jit(solution)/shard_map/ppermute | solution.py:16
  47.1 1.3 %collective-permute-start.15 = (bf16[4,8,32,128]{3,2,1,0:T(8,128)(2,1)S(1)}, bf16[4,8,32,128]{3,2,1,0:T(8,128)(2,1)S(1)}, u32[]{:S(2)}, u32[]{:S(2)}) collective-permute-start(bf16[4,8,32,128]{3,2,1,0:T(8,128)(2,1)S(1)} %pad_maximum_fusion.3), channel_id=1, source_target_pairs={{0,4},{8,12},{16,20},{24,28},{4,0},{12,8},{20,16},{28,24},{1,5},{9... | collective-permute-start | bytes 786440 | tf_op jit(solution)/shard_map/ppermute | solution.py:22
  48.5 2.0 %collective-permute-start.16 = (bf16[4,8,32,128]{3,2,1,0:T(8,128)(2,1)S(1)}, bf16[4,8,32,128]{3,2,1,0:T(8,128)(2,1)S(1)}, u32[]{:S(2)}, u32[]{:S(2)}) collective-permute-start(bf16[4,8,32,128]{3,2,1,0:T(8,128)(2,1)S(1)} %pad_maximum_fusion.4), channel_id=1, source_target_pairs={{4,8},{12,16},{20,24},{8,4},{16,12},{24,20},{5,9},{13,17},{21,25},... | collective-permute-start | bytes 786440 | tf_op jit(solution)/shard_map/ppermute | solution.py:22
  50.6 7.6 %shard_map.55 = (bf16[1,9,128,128]{3,2,1,0:T(8,128)(2,1)S(1)}, bf16[2,9,128,128]{3,2,1,0:T(8,128)(2,1)S(1)}, bf16[1,9,128,128]{3,2,1,0:T(8,128)(2,1)S(1)}) custom-call(bf16[4,10,32,128]{3,2,1,0:T(8,128)(2,1)S(1)} %bitcast.78, bf16[4,10,32,128]{3,2,1,0:T(8,128)(2,1)S(1)} %collective-permute-done.refs_1_.refs_7_, ...), custom_call_target="tpu_custom_call" | custom-call | flops 12230590464 | bytes 2097152 | tf_op jit(solution)/shard_map/pallas_call | solution.py:159
  58.3 4.2 %collective-permute-start.11 = (bf16[1,9,128,128]{3,2,1,0:T(8,128)(2,1)S(1)}, bf16[1,9,128,128]{3,2,1,0:T(8,128)(2,1)S(1)}, u32[]{:S(2)}, u32[]{:S(2)}) collective-permute-start(bf16[1,9,128,128]{3,2,1,0:T(8,128)(2,1)S(1)} %get-tuple-element.26.refs_3_.refs_8_), channel_id=1, source_target_pairs={{4,8},{12,16},{20,24},{8,4},{16,12},{24,20},{5,9},{13,17},{21,25},... | collective-permute-start | bytes 884744 | tf_op jit(solution)/shard_map/ppermute | solution.py:22
  62.5 7.8 %shard_map.58 = (bf16[1,8,128,128]{3,2,1,0:T(8,128)(2,1)S(1)}, bf16[2,8,128,128]{3,2,1,0:T(8,128)(2,1)}, bf16[1,8,128,128]{3,2,1,0:T(8,128)(2,1)S(1)}) custom-call(bf16[4,8,32,128]{3,2,1,0:T(8,128)(2,1)S(1)} %bitcast.82, bf16[4,8,32,128]{3,2,1,0:T(8,128)(2,1)S(1)} %collective-permute-done.12.refs_1_, ...), custom_call_target="tpu_custom_call" | custom-call | flops 10871635968 | bytes 2097152 | tf_op jit(solution)/shard_map/pallas_call | solution.py:159
  70.4 3.3 %collective-permute-start.18 = (bf16[1,8,128,128]{3,2,1,0:T(8,128)(2,1)S(1)}, bf16[1,8,128,128]{3,2,1,0:T(8,128)(2,1)S(1)}, u32[]{:S(2)}, u32[]{:S(2)}) collective-permute-start(bf16[1,8,128,128]{3,2,1,0:T(8,128)(2,1)S(1)} %get-tuple-element.33.refs_3_), channel_id=1, source_target_pairs={{4,8},{12,16},{20,24},{8,4},{16,12},{24,20},{5,9},{13,17},{21,25},... | collective-permute-start | bytes 786440 | tf_op jit(solution)/shard_map/ppermute | solution.py:22
  73.8 1.0 shard_map.56.refs_5_.refs_10_
  74.7 9.6 %collective-permute-done.17.refs_0_ = bf16[1,8,128,128]{3,2,1,0:T(8,128)(2,1)S(1)} collective-permute-done((bf16[1,8,128,128]{3,2,1,0:T(8,128)(2,1)S(1)}, bf16[1,8,128,128]{3,2,1,0:T(8,128)(2,1)S(1)}, u32[]{:S(2)}, u32[]{:S(2)}) %collective-permute-start.17) | collective-permute-done | bytes 262176 | tf_op jit(solution)/shard_map/ppermute | solution.py:22
  84.4 7.1 %shard_map.59 = (bf16[4,8,32,128]{3,2,1,0:T(8,128)(2,1)S(1)}, bf16[4,8,32,128]{3,2,1,0:T(8,128)(2,1)S(1)}, bf16[4,8,32,128]{3,2,1,0:T(8,128)(2,1)S(1)}, bf16[4,8,32,128]{3,2,1,0:T(8,128)(2,1)S(1)}) custom-call(bf16[1,8,128,128]{3,2,1,0:T(8,128)(2,1)S(1)} %collective-permute-done.17.refs_0_, bf16[1,8,128,128]{3,2,1,0:T(8,128)(2,1)S(1)} %get-tuple-element.31.refs_1_, ...), custom_call_target="tpu_custom_call" | custom-call | flops 10871635968 | bytes 2097152 | tf_op jit(solution)/shard_map/pallas_call | solution.py:159
  91.5 1.1 collective-permute-start.19
  92.6 6.7 %shard_map.57 = (bf16[4,8,32,128]{3,2,1,0:T(8,128)(2,1)S(1)}, bf16[4,8,32,128]{3,2,1,0:T(8,128)(2,1)S(1)}, bf16[4,8,32,128]{3,2,1,0:T(8,128)(2,1)S(1)}, bf16[4,8,32,128]{3,2,1,0:T(8,128)(2,1)S(1)}) custom-call(bf16[1,9,128,128]{3,2,1,0:T(8,128)(2,1)S(1)} %collective-permute-done.10.refs_0_.refs_5_, ...), custom_call_target="tpu_custom_call" | custom-call | flops 10871635968 | bytes 2097152 | tf_op jit(solution)/shard_map/pallas_call | solution.py:159
  99.5 1.2 collective-permute-start.22
  101.6 1.2 collective-permute-start.21
  103.4 3.6 %collective-permute-done.22 = bf16[4,8,32,128]{3,2,1,0:T(8,128)(2,1)S(1)} collective-permute-done((bf16[4,8,32,128]{3,2,1,0:T(8,128)(2,1)S(1)}, bf16[4,8,32,128]{3,2,1,0:T(8,128)(2,1)S(1)}, u32[]{:S(2)}, u32[]{:S(2)}) %collective-permute-start.22) | collective-permute-done | bytes 262176 | tf_op jit(solution)/shard_map/ppermute | solution.py:16
  107.0 7.1 %collective-permute-done.23 = bf16[4,8,32,128]{3,2,1,0:T(8,128)(2,1)S(1)} collective-permute-done((bf16[4,8,32,128]{3,2,1,0:T(8,128)(2,1)S(1)}, bf16[4,8,32,128]{3,2,1,0:T(8,128)(2,1)S(1)}, u32[]{:S(2)}, u32[]{:S(2)}) %collective-permute-start.23) | collective-permute-done | bytes 262176 | tf_op jit(solution)/shard_map/ppermute | solution.py:16
  114.1 4.2 %collective-permute-done.21 = bf16[4,8,32,128]{3,2,1,0:T(8,128)(2,1)S(1)} collective-permute-done((bf16[4,8,32,128]{3,2,1,0:T(8,128)(2,1)S(1)}, bf16[4,8,32,128]{3,2,1,0:T(8,128)(2,1)S(1)}, u32[]{:S(2)}, u32[]{:S(2)}) %collective-permute-start.21) | collective-permute-done | bytes 262176 | tf_op jit(solution)/shard_map/ppermute | solution.py:16
  118.2 6.2 %collective-permute-done.24 = bf16[4,8,32,128]{3,2,1,0:T(8,128)(2,1)S(1)} collective-permute-done((bf16[4,8,32,128]{3,2,1,0:T(8,128)(2,1)S(1)}, bf16[4,8,32,128]{3,2,1,0:T(8,128)(2,1)S(1)}, u32[]{:S(2)}, u32[]{:S(2)}) %collective-permute-start.24) | collective-permute-done | bytes 262176 | tf_op jit(solution)/shard_map/ppermute | solution.py:16
  125.0 2.1 %copy.18 = bf16[2,4,32,32,128]{4,3,2,1,0:T(8,128)(2,1)} copy(bf16[2,4,32,32,128]{4,2,3,1,0:T(8,128)(2,1)S(1)} %fusion) | data formatting | bytes 4194304 | tf_op jit(solution)/shard_map/transpose | solution.py:249
  (65 shorter events, 8.2 us)
Async XLA Ops:
  0.7 11.2 %collective-permute-start.8 = (f32[2,32]{1,0:T(2,128)S(1)}, f32[2,32]{1,0:T(2,128)S(1)}, u32[]{:S(2)}, u32[]{:S(2)}) collective-permute-start(f32[2,32]{1,0:T(2,128)S(1)} %pad_maximum_fusion.5), channel_id=1, source_target_pairs={{0,1},{1,0},{2,3},{3,2},{4,5},{5,4},{6,7},{7,6},{8,9},{9,8},{10,11... | collective-permute-start | bytes 776 | tf_op jit(solution)/shard_map/ppermute | solution.py:16
  2.4 46.0 %collective-permute-start.5 = (bf16[2,27,32,128]{3,2,1,0:T(8,128)(2,1)S(1)}, bf16[2,27,32,128]{3,2,1,0:T(8,128)(2,1)S(1)}, u32[]{:S(2)}, u32[]{:S(2)}) collective-permute-start(bf16[2,27,32,128]{3,2,1,0:T(8,128)(2,1)S(1)} %pad_maximum_fusion.refs_6_.refs_0_.refs_12_), channel_id=1, source_target_pairs={{0,1},{1,0},{2,3},{3,2},{4,5},{5,4},{6,7},{7,6},{8,9},{9,8},{10,11... | collective-permute-start | bytes 1327112 | tf_op jit(solution)/shard_map/ppermute | solution.py:16
  5.2 17.1 %collective-permute-start = (bf16[4,10,32,128]{3,2,1,0:T(8,128)(2,1)S(1)}, bf16[4,10,32,128]{3,2,1,0:T(8,128)(2,1)S(1)}, u32[]{:S(2)}, u32[]{:S(2)}) collective-permute-start(bf16[4,10,32,128]{3,2,1,0:T(8,128)(2,1)S(1)} %bitcast.85), channel_id=1, source_target_pairs={{0,1},{1,0},{2,3},{3,2},{4,5},{5,4},{6,7},{7,6},{8,9},{9,8},{10,11... | collective-permute-start | bytes 983048 | tf_op jit(solution)/shard_map/ppermute | solution.py:16
  5.8 16.5 %collective-permute-start.1 = (bf16[4,10,32,128]{3,2,1,0:T(8,128)(2,1)S(1)}, bf16[4,10,32,128]{3,2,1,0:T(8,128)(2,1)S(1)}, u32[]{:S(2)}, u32[]{:S(2)}) collective-permute-start(bf16[4,10,32,128]{3,2,1,0:T(8,128)(2,1)S(1)} %bitcast.86), channel_id=1, source_target_pairs={{0,2},{1,3},{2,0},{3,1},{4,6},{5,7},{6,4},{7,5},{8,10},{9,11},{10,... | collective-permute-start | bytes 983048 | tf_op jit(solution)/shard_map/ppermute | solution.py:16
  7.2 15.2 %collective-permute-start.2 = (bf16[4,10,32,128]{3,2,1,0:T(8,128)(2,1)S(1)}, bf16[4,10,32,128]{3,2,1,0:T(8,128)(2,1)S(1)}, u32[]{:S(2)}, u32[]{:S(2)}) collective-permute-start(bf16[4,10,32,128]{3,2,1,0:T(8,128)(2,1)S(1)} %bitcast.87), channel_id=1, source_target_pairs={{0,3},{1,2},{2,1},{3,0},{4,7},{5,6},{6,5},{7,4},{8,11},{9,10},{10,... | collective-permute-start | bytes 983048 | tf_op jit(solution)/shard_map/ppermute | solution.py:16
  7.7 4.2 %copy-start.1 = (f32[32]{0:T(128)S(1)}, f32[32]{0:T(128)}, u32[]{:S(2)}) copy-start(f32[32]{0:T(128)} %param.9) | copy-start | bytes 388
  7.7 4.2 %copy-start.2 = (f32[32]{0:T(128)S(1)}, f32[32]{0:T(128)}, u32[]{:S(2)}) copy-start(f32[32]{0:T(128)} %param.7) | copy-start | bytes 388
  12.0 10.2 %collective-permute-start.9 = (f32[2,64]{1,0:T(2,128)S(1)}, f32[2,64]{1,0:T(2,128)S(1)}, u32[]{:S(2)}, u32[]{:S(2)}) collective-permute-start(f32[2,64]{1,0:T(2,128)S(1)} %pad_maximum_fusion.6), channel_id=1, source_target_pairs={{0,2},{1,3},{2,0},{3,1},{4,6},{5,7},{6,4},{7,5},{8,10},{9,11},{10,... | collective-permute-start | bytes 1544 | tf_op jit(solution)/shard_map/ppermute | solution.py:16
  22.4 4.0 %collective-permute-start.12 = (bf16[4,8,32,128]{3,2,1,0:T(8,128)(2,1)S(1)}, bf16[4,8,32,128]{3,2,1,0:T(8,128)(2,1)S(1)}, u32[]{:S(2)}, u32[]{:S(2)}) collective-permute-start(bf16[4,8,32,128]{3,2,1,0:T(8,128)(2,1)S(1)} %get-tuple-element.28), channel_id=1, source_target_pairs={{0,1},{1,0},{2,3},{3,2},{4,5},{5,4},{6,7},{7,6},{8,9},{9,8},{10,11... | collective-permute-start | bytes 786440 | tf_op jit(solution)/shard_map/ppermute | solution.py:16
  23.2 7.9 %collective-permute-start.13 = (bf16[4,8,32,128]{3,2,1,0:T(8,128)(2,1)S(1)}, bf16[4,8,32,128]{3,2,1,0:T(8,128)(2,1)S(1)}, u32[]{:S(2)}, u32[]{:S(2)}) collective-permute-start(bf16[4,8,32,128]{3,2,1,0:T(8,128)(2,1)S(1)} %bitcast.94), channel_id=1, source_target_pairs={{0,2},{1,3},{2,0},{3,1},{4,6},{5,7},{6,4},{7,5},{8,10},{9,11},{10,... | collective-permute-start | bytes 786440 | tf_op jit(solution)/shard_map/ppermute | solution.py:16
  24.4 22.6 %collective-permute-start.14 = (bf16[4,8,32,128]{3,2,1,0:T(8,128)(2,1)S(1)}, bf16[4,8,32,128]{3,2,1,0:T(8,128)(2,1)S(1)}, u32[]{:S(2)}, u32[]{:S(2)}) collective-permute-start(bf16[4,8,32,128]{3,2,1,0:T(8,128)(2,1)S(1)} %get-tuple-element.30), channel_id=1, source_target_pairs={{0,3},{1,2},{2,1},{3,0},{4,7},{5,6},{6,5},{7,4},{8,11},{9,10},{10,... | collective-permute-start | bytes 786440 | tf_op jit(solution)/shard_map/ppermute | solution.py:16
  24.9 21.3 %collective-permute-start.6 = (bf16[2,27,32,128]{3,2,1,0:T(8,128)(2,1)S(1)}, bf16[2,27,32,128]{3,2,1,0:T(8,128)(2,1)S(1)}, u32[]{:S(2)}, u32[]{:S(2)}) collective-permute-start(bf16[2,27,32,128]{3,2,1,0:T(8,128)(2,1)S(1)} %pad_maximum_fusion.refs_6_.refs_0_.refs_12_), channel_id=1, source_target_pairs={{0,2},{1,3},{2,0},{3,1},{4,6},{5,7},{6,4},{7,5},{8,10},{9,11},{10,... | collective-permute-start | bytes 1327112 | tf_op jit(solution)/shard_map/ppermute | solution.py:16
  26.3 24.2 %collective-permute-start.3 = (bf16[4,10,32,128]{3,2,1,0:T(8,128)(2,1)S(1)}, bf16[4,10,32,128]{3,2,1,0:T(8,128)(2,1)S(1)}, u32[]{:S(2)}, u32[]{:S(2)}) collective-permute-start(bf16[4,10,32,128]{3,2,1,0:T(8,128)(2,1)S(1)} %pad_maximum_fusion.1), channel_id=1, source_target_pairs={{0,4},{8,12},{16,20},{24,28},{4,0},{12,8},{20,16},{28,24},{1,5},{9... | collective-permute-start | bytes 983048 | tf_op jit(solution)/shard_map/ppermute | solution.py:22
  31.1 19.4 %collective-permute-start.4 = (bf16[4,10,32,128]{3,2,1,0:T(8,128)(2,1)S(1)}, bf16[4,10,32,128]{3,2,1,0:T(8,128)(2,1)S(1)}, u32[]{:S(2)}, u32[]{:S(2)}) collective-permute-start(bf16[4,10,32,128]{3,2,1,0:T(8,128)(2,1)S(1)} %pad_maximum_fusion.2), channel_id=1, source_target_pairs={{4,8},{12,16},{20,24},{8,4},{16,12},{24,20},{5,9},{13,17},{21,25},... | collective-permute-start | bytes 983048 | tf_op jit(solution)/shard_map/ppermute | solution.py:22
  46.2 4.4 %collective-permute-start.7 = (bf16[2,27,32,128]{3,2,1,0:T(8,128)(2,1)S(1)}, bf16[2,27,32,128]{3,2,1,0:T(8,128)(2,1)S(1)}, u32[]{:S(2)}, u32[]{:S(2)}) collective-permute-start(bf16[2,27,32,128]{3,2,1,0:T(8,128)(2,1)S(1)} %collective-permute-done.6.refs_8_.refs_2_.refs_14_), channel_id=1, source_target_pairs={{0,1},{1,0},{2,3},{3,2},{4,5},{5,4},{6,7},{7,6},{8,9},{9,8},{10,11... | collective-permute-start | bytes 1327112 | tf_op jit(solution)/shard_map/ppermute | solution.py:16
  47.1 15.3 %collective-permute-start.15 = (bf16[4,8,32,128]{3,2,1,0:T(8,128)(2,1)S(1)}, bf16[4,8,32,128]{3,2,1,0:T(8,128)(2,1)S(1)}, u32[]{:S(2)}, u32[]{:S(2)}) collective-permute-start(bf16[4,8,32,128]{3,2,1,0:T(8,128)(2,1)S(1)} %pad_maximum_fusion.3), channel_id=1, source_target_pairs={{0,4},{8,12},{16,20},{24,28},{4,0},{12,8},{20,16},{28,24},{1,5},{9... | collective-permute-start | bytes 786440 | tf_op jit(solution)/shard_map/ppermute | solution.py:22
  48.5 14.0 %collective-permute-start.16 = (bf16[4,8,32,128]{3,2,1,0:T(8,128)(2,1)S(1)}, bf16[4,8,32,128]{3,2,1,0:T(8,128)(2,1)S(1)}, u32[]{:S(2)}, u32[]{:S(2)}) collective-permute-start(bf16[4,8,32,128]{3,2,1,0:T(8,128)(2,1)S(1)} %pad_maximum_fusion.4), channel_id=1, source_target_pairs={{4,8},{12,16},{20,24},{8,4},{16,12},{24,20},{5,9},{13,17},{21,25},... | collective-permute-start | bytes 786440 | tf_op jit(solution)/shard_map/ppermute | solution.py:22
  58.2 26.1 %collective-permute-start.10 = (bf16[1,9,128,128]{3,2,1,0:T(8,128)(2,1)S(1)}, bf16[1,9,128,128]{3,2,1,0:T(8,128)(2,1)S(1)}, u32[]{:S(2)}, u32[]{:S(2)}) collective-permute-start(bf16[1,9,128,128]{3,2,1,0:T(8,128)(2,1)S(1)} %get-tuple-element.24.refs_1_.refs_6_), channel_id=1, source_target_pairs={{0,4},{8,12},{16,20},{24,28},{4,0},{12,8},{20,16},{28,24},{1,5},{9... | collective-permute-start | bytes 884744 | tf_op jit(solution)/shard_map/ppermute | solution.py:22
  58.3 26.0 %collective-permute-start.11 = (bf16[1,9,128,128]{3,2,1,0:T(8,128)(2,1)S(1)}, bf16[1,9,128,128]{3,2,1,0:T(8,128)(2,1)S(1)}, u32[]{:S(2)}, u32[]{:S(2)}) collective-permute-start(bf16[1,9,128,128]{3,2,1,0:T(8,128)(2,1)S(1)} %get-tuple-element.26.refs_3_.refs_8_), channel_id=1, source_target_pairs={{4,8},{12,16},{20,24},{8,4},{16,12},{24,20},{5,9},{13,17},{21,25},... | collective-permute-start | bytes 884744 | tf_op jit(solution)/shard_map/ppermute | solution.py:22
  70.3 14.1 %copy-start = (bf16[2,8,128,128]{3,2,1,0:T(8,128)(2,1)S(1)}, bf16[2,8,128,128]{3,2,1,0:T(8,128)(2,1)}, u32[]{:S(2)}) copy-start(bf16[2,8,128,128]{3,2,1,0:T(8,128)(2,1)} %get-tuple-element.32.refs_2_) | copy-start | bytes 1572868
  70.3 14.0 %collective-permute-start.17 = (bf16[1,8,128,128]{3,2,1,0:T(8,128)(2,1)S(1)}, bf16[1,8,128,128]{3,2,1,0:T(8,128)(2,1)S(1)}, u32[]{:S(2)}, u32[]{:S(2)}) collective-permute-start(bf16[1,8,128,128]{3,2,1,0:T(8,128)(2,1)S(1)} %get-tuple-element.31.refs_1_), channel_id=1, source_target_pairs={{0,4},{8,12},{16,20},{24,28},{4,0},{12,8},{20,16},{28,24},{1,5},{9... | collective-permute-start | bytes 786440 | tf_op jit(solution)/shard_map/ppermute | solution.py:22
  70.4 13.9 %collective-permute-start.18 = (bf16[1,8,128,128]{3,2,1,0:T(8,128)(2,1)S(1)}, bf16[1,8,128,128]{3,2,1,0:T(8,128)(2,1)S(1)}, u32[]{:S(2)}, u32[]{:S(2)}) collective-permute-start(bf16[1,8,128,128]{3,2,1,0:T(8,128)(2,1)S(1)} %get-tuple-element.33.refs_3_), channel_id=1, source_target_pairs={{4,8},{12,16},{20,24},{8,4},{16,12},{24,20},{5,9},{13,17},{21,25},... | collective-permute-start | bytes 786440 | tf_op jit(solution)/shard_map/ppermute | solution.py:22
  91.5 11.3 %collective-permute-start.19 = (bf16[4,8,32,128]{3,2,1,0:T(8,128)(2,1)S(1)}, bf16[4,8,32,128]{3,2,1,0:T(8,128)(2,1)S(1)}, u32[]{:S(2)}, u32[]{:S(2)}) collective-permute-start(bf16[4,8,32,128]{3,2,1,0:T(8,128)(2,1)S(1)} %get-tuple-element.35), channel_id=1, source_target_pairs={{0,1},{1,0},{2,3},{3,2},{4,5},{5,4},{6,7},{7,6},{8,9},{9,8},{10,11... | collective-permute-start | bytes 786440 | tf_op jit(solution)/shard_map/ppermute | solution.py:16
  99.4 3.7 %collective-permute-start.20 = (bf16[4,8,32,128]{3,2,1,0:T(8,128)(2,1)S(1)}, bf16[4,8,32,128]{3,2,1,0:T(8,128)(2,1)S(1)}, u32[]{:S(2)}, u32[]{:S(2)}) collective-permute-start(bf16[4,8,32,128]{3,2,1,0:T(8,128)(2,1)S(1)} %get-tuple-element.36), channel_id=1, source_target_pairs={{0,1},{1,0},{2,3},{3,2},{4,5},{5,4},{6,7},{7,6},{8,9},{9,8},{10,11... | collective-permute-start | bytes 786440 | tf_op jit(solution)/shard_map/ppermute | solution.py:16
  99.5 7.5 %collective-permute-start.22 = (bf16[4,8,32,128]{3,2,1,0:T(8,128)(2,1)S(1)}, bf16[4,8,32,128]{3,2,1,0:T(8,128)(2,1)S(1)}, u32[]{:S(2)}, u32[]{:S(2)}) collective-permute-start(bf16[4,8,32,128]{3,2,1,0:T(8,128)(2,1)S(1)} %get-tuple-element.38), channel_id=1, source_target_pairs={{0,2},{1,3},{2,0},{3,1},{4,6},{5,7},{6,4},{7,5},{8,10},{9,11},{10,... | collective-permute-start | bytes 786440 | tf_op jit(solution)/shard_map/ppermute | solution.py:16
  100.8 13.3 %collective-permute-start.23 = (bf16[4,8,32,128]{3,2,1,0:T(8,128)(2,1)S(1)}, bf16[4,8,32,128]{3,2,1,0:T(8,128)(2,1)S(1)}, u32[]{:S(2)}, u32[]{:S(2)}) collective-permute-start(bf16[4,8,32,128]{3,2,1,0:T(8,128)(2,1)S(1)} %get-tuple-element.39), channel_id=1, source_target_pairs={{0,3},{1,2},{2,1},{3,0},{4,7},{5,6},{6,5},{7,4},{8,11},{9,10},{10,... | collective-permute-start | bytes 786440 | tf_op jit(solution)/shard_map/ppermute | solution.py:16
  101.6 16.6 %collective-permute-start.21 = (bf16[4,8,32,128]{3,2,1,0:T(8,128)(2,1)S(1)}, bf16[4,8,32,128]{3,2,1,0:T(8,128)(2,1)S(1)}, u32[]{:S(2)}, u32[]{:S(2)}) collective-permute-start(bf16[4,8,32,128]{3,2,1,0:T(8,128)(2,1)S(1)} %get-tuple-element.37), channel_id=1, source_target_pairs={{0,2},{1,3},{2,0},{3,1},{4,6},{5,7},{6,4},{7,5},{8,10},{9,11},{10,... | collective-permute-start | bytes 786440 | tf_op jit(solution)/shard_map/ppermute | solution.py:16
  102.8 21.6 %collective-permute-start.24 = (bf16[4,8,32,128]{3,2,1,0:T(8,128)(2,1)S(1)}, bf16[4,8,32,128]{3,2,1,0:T(8,128)(2,1)S(1)}, u32[]{:S(2)}, u32[]{:S(2)}) collective-permute-start(bf16[4,8,32,128]{3,2,1,0:T(8,128)(2,1)S(1)} %get-tuple-element.40), channel_id=1, source_target_pairs={{0,3},{1,2},{2,1},{3,0},{4,7},{5,6},{6,5},{7,4},{8,11},{9,10},{10,... | collective-permute-start | bytes 786440 | tf_op jit(solution)/shard_map/ppermute | solution.py:16

commit v3 on v0

v3 whole, which is shorter than its diff:
```python
import functools

import jax
import jax.numpy as jnp
from jax import lax
from jax.experimental import pallas as pl
from jax.experimental.pallas import tpu as pltpu
from jax.sharding import PartitionSpec as P

BF = jnp.bfloat16
VMEM_LIMIT = 48 * 2**20
CUTS = (9, 21, 32)
UNROLL = 3


def chan_swap(value, k):
    return lax.ppermute(value, "chan", [(i, i ^ k) for i in range(4)])


def slab_swap(value):
    size = lax.axis_size("slab")
    pairs = [(4 * s + i + 1, 4 * (s + 1) + i) for s in range(size - 1) for i in (0, 2)]
    return lax.ppermute(value, ("slab", "chan"), pairs + [(j, i) for i, j in pairs])


def after(value, *earlier):
    return lax.optimization_barrier((value, earlier))[0]


def conv_rows(x, w, bias, first, second, count, store):
    chans, width = x.shape[2], x.shape[3]
    lane = lax.broadcasted_iota(jnp.int32, (chans, width), 1)

    def step(j, _):
        cols = [
            jnp.concatenate([x[z + a, j + c] for a in range(3) for c in range(3)], axis=0) for z in (first, second)
        ]
        lhs = jnp.concatenate([w[3 * k : 3 * k + 3].reshape(3 * chans, chans) for k in range(9)], axis=1)
        acc = jnp.dot(lhs, jnp.concatenate(cols, axis=1), preferred_element_type=jnp.float32)
        for u in range(2):
            part = acc[:, u * width : (u + 1) * width]
            before = jnp.where(lane == 0, 0.0, pltpu.roll(part[:chans], 1, 1))
            later = jnp.where(lane == width - 1, 0.0, pltpu.roll(part[2 * chans :], width - 1, 1))
            total = before + part[chans : 2 * chans] + later
            store(u, j, jnp.maximum(total + bias[...], 0.0).astype(BF))
        return 0

    lax.fori_loop(0, count, step, 0, unroll=UNROLL)


def start_copies(pairs, sems, first=0):
    copies = [pltpu.make_async_copy(s, d, sems.at[first + i]) for i, (s, d) in enumerate(pairs)]
    for copy in copies:
        copy.start()
    return copies


def place(block, unit):
    return pl.ds(pl.multiple_of(block * unit, unit), unit)


def spans(new, old, axis):
    n = new[0].shape[axis]
    if old is None:
        return [(new, 0, n, 1)]
    return [(new, 0, n, 2), (old, old[0].shape[axis] - 2, 2, 0)]


def clear_edges(x, has_old, last):
    edges = ([] if has_old else [0]) + ([x.shape[1] - 1] if last else [])
    for row in edges:
        for z in range(x.shape[0]):
            x[z, row] = jnp.zeros(x.shape[2:], BF)


def first_kernel_body(has_old, last, *refs):
    new, refs = refs[:4], refs[4:]
    old, refs = (refs[:4], refs[4:]) if has_old else (None, refs)
    (w_own, w_x, w_s), bias, (out_slab, out_sib, x, w, sems) = refs[:3], refs[3], refs[4:]
    me = lax.axis_index("chan")
    c = me % 2
    unit = w_own.shape[1]
    pairs = [
        (block, w.at[:, place(me ^ k, unit)]) for k, block in enumerate((w_own, w_s.at[0], w_x, w_s.at[1]))
    ]
    for (own, xr, sr, side), start, rows, dst in spans(new, old, 1):
        src, to = pl.ds(start, rows), pl.ds(dst, rows)
        three = pl.ds(c, 3)
        for k, block in enumerate((own.at[three, src], sr.at[0, :, src], xr.at[three, src], sr.at[1, :, src])):
            pairs.append((block, x.at[pl.ds(1 - c, 3), to, place(me ^ k, unit)]))
            pairs.append((side.at[k, src], x.at[3 * c, to, place(me ^ 1 ^ k, unit)]))
    copies = start_copies(pairs, sems)
    clear_edges(x, has_old, last)
    for copy in copies:
        copy.wait()

    def store(u, j, value):
        (out_slab, out_sib)[u][j] = value

    conv_rows(x, w, bias, c, 1 - c, out_slab.shape[0], store)


def second_kernel_body(has_old, last, *refs):
    new, refs = refs[:4], refs[4:]
    old, refs = (refs[:4], refs[4:]) if has_old else (None, refs)
    w, bias, outs, (h, sems) = refs[0], refs[1], refs[2:-2], refs[-2:]
    if len(outs) == 3:
        outs = (outs[0], outs[1], outs[2].at[0], outs[2].at[1])
    c = lax.axis_index("chan") % 2
    unit = outs[0].shape[2]
    pairs = []
    for arrays, start, rows, dst in spans(new, old, 0):
        for part, z in zip(arrays, (3 * c, 1 + c, 2 - c, 3 - 3 * c)):
            pairs.append((part.at[pl.ds(start, rows)], h.at[z, pl.ds(dst, rows)]))
    copies = start_copies(pairs, sems)
    clear_edges(h, has_old, last)
    for copy in copies:
        copy.wait()

    def store(u, j, value):
        for k in range(4):
            outs[k][u, j] = value[k * unit : (k + 1) * unit]

    conv_rows(h, w, bias, 0, 1, outs[0].shape[1], store)


def weights_kernel_body(*refs):
    (own, across, shared), (out, w, sems) = refs[:3], refs[3:]
    pieces = (own, shared.at[0], across, shared.at[1])
    me = lax.axis_index("chan")
    unit = own.shape[1]
    for copy in start_copies([(pieces[k], w.at[:, place(me ^ k, unit)]) for k in range(4)], sems):
        copy.wait()

    def step(i, _):
        turned = jnp.transpose(w[i])
        for q in range(4):
            out[i, place(me ^ q, unit)] = turned[q * unit : (q + 1) * unit]
        return 0

    lax.fori_loop(0, w.shape[0], step, 0, unroll=3)


def call(body, outs, any_operands, vmem_operands, scratch, n_copies, flops):
    any_spec = pl.BlockSpec(memory_space=pl.ANY)
    vmem = pl.BlockSpec(memory_space=pltpu.VMEM)
    return pl.pallas_call(
        body,
        out_shape=[jax.ShapeDtypeStruct(s, BF) for s in outs],
        in_specs=[any_spec] * len(any_operands) + [vmem] * len(vmem_operands),
        out_specs=[vmem] * len(outs),
        scratch_shapes=[*(pltpu.VMEM(s, BF) for s in scratch), pltpu.SemaphoreType.DMA((n_copies,))],
        cost_estimate=pl.CostEstimate(flops=flops, bytes_accessed=2**21, transcendentals=0),
        compiler_params=pltpu.CompilerParams(vmem_limit_bytes=VMEM_LIMIT),
    )(*any_operands, *vmem_operands)


def body(volume, first_kernel, first_bias, second_kernel, second_bias):
    _, depth, unit, thick, width = volume.shape
    chans = 4 * unit
    me = lax.axis_index("chan")
    b, c = me // 2, me % 2
    ends = [0] + [thick * k // CUTS[-1] for k in CUTS]
    parts = len(CUTS)
    in_ends = [0] + [e + 2 for e in ends[1:-1]] + [thick]
    hidden_ends = [0] + [e + 1 for e in ends[1:-1]] + [thick]

    def cut(chunk, batch):
        part = lax.dynamic_index_in_dim(volume, batch, 0, keepdims=False)
        return jnp.transpose(part[:, :, in_ends[chunk] : in_ends[chunk + 1]], (0, 2, 1, 3))

    def layer(value, z):
        return lax.dynamic_index_in_dim(value, z, 0, keepdims=False)

    def share(own, xr):
        three = [lax.dynamic_slice_in_dim(v, 1 - c, 3) for v in (own, xr)]
        sr = chan_swap(jnp.stack(three), 1)
        edge = jnp.stack([layer(own, 3 * c), layer(sr[0], 2 * c), layer(xr, 3 * c), layer(sr[1], 2 * c)])
        return (own, xr, sr, slab_swap(edge)), edge

    def weight_pieces(own, earlier):
        across = chan_swap(after(own, earlier), 2)
        return (own, across, chan_swap(jnp.stack([own, across]), 1))

    sent = cut(0, 1 - b)
    xr = chan_swap(sent, 2)
    (volume, w1, w2, biases), _ = lax.optimization_barrier(
        ((volume, first_kernel, second_kernel, (first_bias, second_bias)), sent)
    )
    biases = jnp.stack(biases)
    biases = jnp.concatenate([biases, chan_swap(biases, 1)], axis=1)
    biases = jnp.concatenate([biases, chan_swap(biases, 2)], axis=1)
    w1 = jnp.transpose(w1, (0, 1, 2, 4, 3)).reshape(27, unit, chans)
    w2 = w2.reshape(27, unit, chans)
    xr, biases = lax.optimization_barrier((xr, biases))
    received, edges = [], []
    for chunk in range(parts):
        arrays, edge = share(cut(chunk, b), xr)
        received.append(arrays)
        edges.append(edge)
        if chunk == 0:
            first = weight_pieces(w1, edge)
        if chunk < parts - 1:
            xr = chan_swap(after(cut(chunk + 1, 1 - b), xr, edge), 2)
    second = weight_pieces(w2, xr)

    order = [jnp.concatenate([layer(v.reshape(4, unit), me ^ q) for q in range(4)]) for v in biases[:1]] + [biases[1]]
    bias1, bias2 = (jnp.broadcast_to(v[:, None], (chans, width)) for v in order)
    full2 = call(weights_kernel_body, [(27, chans, chans)], second, (), [(27, chans, chans)], 4, 10**9)[0]

    unit_flops = 2 * 4 * width * 27 * chans * chans
    hidden = []
    for chunk in range(parts):
        n = hidden_ends[chunk + 1] - hidden_ends[chunk]
        operands = received[chunk] + (received[chunk - 1] if chunk else ())
        operands = after(operands, edges[chunk + 1 : chunk + 2])
        to_slab, to_sib = call(
            functools.partial(first_kernel_body, chunk > 0, chunk == parts - 1),
            [(n, chans, width)] * 2, (*operands, *first), (bias1,),
            [(4, n + 2, chans, width), (27, chans, chans)],
            4 + 8 * (1 + (chunk > 0)), unit_flops * n,
        )
        hidden.append((slab_swap(to_slab), to_slab, to_sib, chan_swap(to_sib, 1)))

    own, other, sibling, diagonal = [], [], [], []
    for chunk in range(parts):
        n = ends[chunk + 1] - ends[chunk]
        operands = hidden[chunk] + (hidden[chunk - 1] if chunk else ())
        operands = after(operands, [h[1] for h in hidden[chunk + 1 : chunk + 2]])
        last = chunk == parts - 1
        block = (2, n, unit, width)
        outs = call(
            functools.partial(second_kernel_body, chunk > 0, last),
            [block] * 4 if last else [block, block, (2, *block)], operands, (full2, bias2),
            [(4, n + 2, chans, width)], 4 * (1 + (chunk > 0)), unit_flops * n,
        )
        own.append(outs[0])
        if last:
            x, s, d = (chan_swap(outs[k], k) for k in (2, 1, 3))
        else:
            got = chan_swap(outs[2], 2)
            x = got[0]
            s, d = chan_swap(jnp.stack([outs[1], got[1]]), 1)
        other.append(x)
        sibling.append(s)
        diagonal.append(d)

    def layers(near, far):
        near, far = jnp.concatenate(near, axis=1), jnp.concatenate(far, axis=1)
        return jnp.where(c == 0, jnp.concatenate([near, far]), jnp.concatenate([far, near]))

    home = layers(own, sibling)
    away = layers(other, diagonal)
    out = jnp.where(b == 0, jnp.stack([home, away]), jnp.stack([away, home]))
    return jnp.transpose(out, (0, 1, 3, 2, 4))


def solution(mesh):
    return jax.shard_map(
        body,
        mesh=mesh,
        in_specs=(
            P(None, "slab", "chan", None, None),
            P(None, None, None, None, "chan"),
            P("chan"),
            P(None, None, None, "chan", None),
            P("chan"),
        ),
        out_specs=P(None, "slab", "chan", None, None),
        check_vma=False,
    )
```

time: 599 us -> 112 us (0.19)
  waiting for transfers between devices: 281 us -> 30.8 us
  local copies, waits for them, and re-layouts: 150 us -> 16.1 us
  matrix products: 114 us -> 0 us
  Pallas kernels: 0 us -> 27.9 us
  other arithmetic: 25.3 us -> 3.15 us
  starting transfers between devices: 12.5 us -> 33.1 us
  between operations: 13.8 us -> 0.58 us
    reduce_scatter x1 -> x0, waiting for transfers between devices: 126 us -> none  [body(): lax.psum_scatter(partial_value, 'chan', scatter_dimension=2, tiled=True)]
    conv_general_dilated x2 -> x0, matrix products: 114 us -> none  [convolve(): lax.conv_general_dilated(values_in, kernel, (1, 1, 1), ((0, 0), (1, 1), (...]
    ppermute x4 -> x28, waiting for transfers between devices: 95.4 us -> 30.8 us  [the longest x22 24.5 us: chan_swap(): return lax.ppermute(value, 'chan', [(i, i ^ k) for i in range(4)])]
    all_gather x1 -> x0, waiting for transfers between devices: 59.8 us -> none  [body(): gathered = lax.all_gather(volume, 'chan', axis=2, tiled=True)]
    conv_general_dilated x6 -> x0, local copies, waits for them, and re-layouts: 55.2 us -> none  [convolve(): lax.conv_general_dilated(values_in, kernel, (1, 1, 1), ((0, 0), (1, 1), (...]
    pallas_call x0 -> x7, Pallas kernels: none -> 27.9 us  [call(): pl.pallas_call(body, out_shape=[jax.ShapeDtypeStruct(s, BF) for s in outs...]
    convert_element_type x6 -> x0, local copies, waits for them, and re-layouts: 24 us -> none  [activate(): jax.nn.relu(summed + bias_row[None, None, :, None, None])]
    unnamed x16 -> x14, local copies, waits for them, and re-layouts: 23.7 us -> 0.03 us
  transfers between devices with their start and end apart: 6 -> 28, of which waited for: 5 -> 9; matrix products, arithmetic and copies ran while one was open for 3% -> 12% of each run, Pallas kernels for 0% -> 25%
where the time goes in v3:
time: 112 us
  starting transfers between devices  33.1 us (30%)
  waiting for transfers between devices  30.8 us (28%)
  Pallas kernels  27.9 us (25%)
  local copies, waits for them, and re-layouts  16.1 us (14%)
  other arithmetic  3.15 us (3%)
    pallas_call x7, Pallas kernels, call(): pl.pallas_call(body, out_shape=[jax.ShapeDtypeStruct(s, BF) for s in outs...  27.9 us
    ppermute x22, waiting for transfers between devices, chan_swap(): return lax.ppermute(value, 'chan', [(i, i ^ k) for i in range(4)])  24.5 us
    ppermute x22, starting transfers between devices, chan_swap(): return lax.ppermute(value, 'chan', [(i, i ^ k) for i in range(4)])  18 us
    ppermute x6, starting transfers between devices, slab_swap(): lax.ppermute(value, ('slab', 'chan'), pairs + [(j, i) for i, j in pairs])  15.1 us
    ppermute x6, waiting for transfers between devices, slab_swap(): lax.ppermute(value, ('slab', 'chan'), pairs + [(j, i) for i, j in pairs])  6.32 us
    dynamic_slice x5, local copies, waits for them, and re-layouts, cut(): part = lax.dynamic_index_in_dim(volume, batch, 0, keepdims=False)  5.56 us
    transpose x5, local copies, waits for them, and re-layouts, cut(): jnp.transpose(part[:, :, in_ends[chunk]:in_ends[chunk + 1]], (0, 2, 1, 3))  4.71 us
  transfers between devices with their start and end apart: 28, of which 9 were waited for; matrix products, arithmetic and copies ran while one was open for 12% of the time, Pallas kernels for 25%

profile of v3, /device:TPU:25, one launch (start us, length us, event | category | flops | bytes accessed | tf_op | source)
XLA Modules:
  0.0 111.6 jit_solution(2777196779653442758)
XLA Ops:
  0.0 1.3 %constant_dynamic-slice_fusion.9 = bf16[1,4,32,32,128]{4,3,2,1,0:T(8,128)(2,1)S(1)} fusion(bf16[2,4,32,32,128]{4,3,2,1,0:T(8,128)(2,1)} %param.5, s32[]{:T(128)S(6)} %select_n.103), kind=kLoop, calls=%fused_computation.54 | loop fusion | bytes 2097156 | tf_op jit(solution)/shard_map/jit(dynamic_index_in_dim)/dynamic_slice | solution.py:169
  1.8 1.3 %collective-permute-start = (bf16[4,11,32,128]{3,2,1,0:T(8,128)(2,1)S(1)}, bf16[4,11,32,128]{3,2,1,0:T(8,128)(2,1)S(1)}, u32[]{:S(2)}, u32[]{:S(2)}) collective-permute-start(bf16[4,11,32,128]{3,2,1,0:T(8,128)(2,1)S(1)} %slice_bitcast_fusion.1), channel_id=1, source_target_pairs={{0,2},{1,3},{2,0},{3,1},{4,6},{5,7},{6,4},{7,5},{8,10},{9,11},{10,... | collective-permute-start | bytes 1081352 | tf_op jit(solution)/shard_map/ppermute | solution.py:17
  4.1 2.0 %constant_dynamic-slice_fusion.6 = (bf16[1,4,32,32,128]{4,3,2,1,0:T(8,128)(2,1)S(1)}, bf16[1,4,32,32,128]{4,3,2,1,0:T(8,128)(2,1)S(1)}) fusion(bf16[2,4,32,32,128]{4,3,2,1,0:T(8,128)(2,1)} %param.5, s32[]{:T(128)S(6)} %select_n.103, s32[]{:T(128)S(6)} %select_n.104), kind=kLoop, calls=%fused_computation.51 | loop fusion | bytes 4194312 | tf_op jit(solution)/shard_map/jit(dynamic_index_in_dim)/dynamic_slice | solution.py:169
  6.1 1.4 %copy.14 = bf16[1,4,32,32,128]{4,2,3,1,0:T(8,128)(2,1)} copy(bf16[1,4,32,32,128]{4,3,2,1,0:T(8,128)(2,1)S(1)} %get-tuple-element.140) | data formatting | bytes 2097152 | tf_op jit(solution)/shard_map/jit(dynamic_index_in_dim)/dynamic_slice | solution.py:169
  9.4 2.1 %collective-permute-done.2 = f32[2,64]{1,0:T(2,128)S(1)} collective-permute-done((f32[2,64]{1,0:T(2,128)S(1)}, f32[2,64]{1,0:T(2,128)S(1)}, u32[]{:S(2)}, u32[]{:S(2)}) %collective-permute-start.2) | collective-permute-done | bytes 544 | tf_op jit(solution)/shard_map/ppermute | solution.py:17
  11.7 1.3 %collective-permute-start.3 = (bf16[2,3,11,32,128]{4,3,2,1,0:T(8,128)(2,1)S(1)}, bf16[2,3,11,32,128]{4,3,2,1,0:T(8,128)(2,1)S(1)}, u32[]{:S(2)}, u32[]{:S(2)}) collective-permute-start(bf16[2,3,11,32,128]{4,3,2,1,0:T(8,128)(2,1)S(1)} %pad_maximum_fusion.1), channel_id=1, source_target_pairs={{0,1},{1,0},{2,3},{3,2},{4,5},{5,4},{6,7},{7,6},{8,9},{9,8},{10,11... | collective-permute-start | bytes 1622024 | tf_op jit(solution)/shard_map/ppermute | solution.py:17
  18.8 7.9 %collective-permute-done.5.refs_1_.refs_5_ = bf16[4,12,32,128]{3,2,1,0:T(8,128)(2,1)S(1)} collective-permute-done((bf16[4,12,32,128]{3,2,1,0:T(8,128)(2,1)}, bf16[4,12,32,128]{3,2,1,0:T(8,128)(2,1)S(1)}, u32[]{:S(2)}, u32[]{:S(2)}) %collective-permute-start.5) | collective-permute-done | bytes 393248 | tf_op jit(solution)/shard_map/ppermute | solution.py:17
  28.4 1.7 %slice_bitcast_fusion.2 = bf16[4,9,32,128]{3,2,1,0:T(8,128)(2,1)} fusion(bf16[4,32,32,128]{3,1,2,0:T(8,128)(2,1)} %bitcast.115), kind=kLoop, calls=%fused_computation.21 | loop fusion | bytes 589824 | tf_op jit(solution)/shard_map/transpose | solution.py:170
  31.5 3.2 %collective-permute-start.4 = (bf16[4,11,32,128]{3,2,1,0:T(8,128)(2,1)}, bf16[4,11,32,128]{3,2,1,0:T(8,128)(2,1)S(1)}, u32[]{:S(2)}, u32[]{:S(2)}) collective-permute-start(bf16[4,11,32,128]{3,2,1,0:T(8,128)(2,1)} %pad_maximum_fusion.7), channel_id=1, source_target_pairs={{1,4},{3,6},{5,8},{7,10},{9,12},{11,14},{13,16},{15,18},{17,20},{1... | collective-permute-start | bytes 1081352 | tf_op jit(solution)/shard_map/ppermute | solution.py:23
  36.5 5.0 %collective-permute-done.7.refs_5_.refs_9_ = bf16[27,32,128]{2,1,0:T(8,128)(2,1)S(1)} collective-permute-done((bf16[27,32,128]{2,1,0:T(8,128)(2,1)S(1)}, bf16[27,32,128]{2,1,0:T(8,128)(2,1)S(1)}, u32[]{:S(2)}, u32[]{:S(2)}) %collective-permute-start.7) | collective-permute-done | bytes 221216 | tf_op jit(solution)/shard_map/ppermute | solution.py:17
  41.6 1.9 %collective-permute-start.8 = (bf16[2,27,32,128]{3,2,1,0:T(8,128)(2,1)S(1)}, bf16[2,27,32,128]{3,2,1,0:T(8,128)(2,1)S(1)}, u32[]{:S(2)}, u32[]{:S(2)}) collective-permute-start(bf16[2,27,32,128]{3,2,1,0:T(8,128)(2,1)S(1)} %pad_maximum_fusion.2), channel_id=1, source_target_pairs={{0,1},{1,0},{2,3},{3,2},{4,5},{5,4},{6,7},{7,6},{8,9},{9,8},{10,11... | collective-permute-start | bytes 1327112 | tf_op jit(solution)/shard_map/ppermute | solution.py:17
  43.6 2.3 %collective-permute-start.11 = (bf16[4,12,32,128]{3,2,1,0:T(8,128)(2,1)S(1)}, bf16[4,12,32,128]{3,2,1,0:T(8,128)(2,1)S(1)}, u32[]{:S(2)}, u32[]{:S(2)}) collective-permute-start(bf16[4,12,32,128]{3,2,1,0:T(8,128)(2,1)S(1)} %pad_maximum_fusion.5), channel_id=1, source_target_pairs={{1,4},{3,6},{5,8},{7,10},{9,12},{11,14},{13,16},{15,18},{17,20},{1... | collective-permute-start | bytes 1179656 | tf_op jit(solution)/shard_map/ppermute | solution.py:23
  45.8 2.0 %collective-permute-done.12.refs_1_ = bf16[4,9,32,128]{3,2,1,0:T(8,128)(2,1)S(1)} collective-permute-done((bf16[4,9,32,128]{3,2,1,0:T(8,128)(2,1)S(1)}, bf16[4,9,32,128]{3,2,1,0:T(8,128)(2,1)S(1)}, u32[]{:S(2)}, u32[]{:S(2)}) %collective-permute-start.12) | collective-permute-done | bytes 294944 | tf_op jit(solution)/shard_map/ppermute | solution.py:17
  49.1 1.5 %collective-permute-start.13 = (bf16[2,3,9,32,128]{4,3,2,1,0:T(8,128)(2,1)S(1)}, bf16[2,3,9,32,128]{4,3,2,1,0:T(8,128)(2,1)S(1)}, u32[]{:S(2)}, u32[]{:S(2)}) collective-permute-start(bf16[2,3,9,32,128]{4,3,2,1,0:T(8,128)(2,1)S(1)} %pad_maximum_fusion.3), channel_id=1, source_target_pairs={{0,1},{1,0},{2,3},{3,2},{4,5},{5,4},{6,7},{7,6},{8,9},{9,8},{10,11... | collective-permute-start | bytes 1327112 | tf_op jit(solution)/shard_map/ppermute | solution.py:17
  50.7 4.0 %shard_map.55 = (bf16[10,128,128]{2,1,0:T(8,128)(2,1)S(1)}, bf16[10,128,128]{2,1,0:T(8,128)(2,1)S(1)}) custom-call(bf16[4,11,32,128]{3,2,1,0:T(8,128)(2,1)S(1)} %get-tuple-element.77.refs_0_.refs_4_, bf16[4,11,32,128]{3,2,1,0:T(8,128)(2,1)S(1)} %collective-permute-done.refs_1_.refs_5_, ...), custom_call_target="tpu_custom_call" | custom-call | flops 4529848320 | bytes 2097152 | tf_op jit(solution)/shard_map/pallas_call | solution.py:147
  54.7 1.9 %collective-permute-start.9 = (bf16[10,128,128]{2,1,0:T(8,128)(2,1)S(1)}, bf16[10,128,128]{2,1,0:T(8,128)(2,1)S(1)}, u32[]{:S(2)}, u32[]{:S(2)}) collective-permute-start(bf16[10,128,128]{2,1,0:T(8,128)(2,1)S(1)} %get-tuple-element.97.refs_1_.refs_5_), channel_id=1, source_target_pairs={{1,4},{3,6},{5,8},{7,10},{9,12},{11,14},{13,16},{15,18},{17,20},{1... | collective-permute-start | bytes 983048 | tf_op jit(solution)/shard_map/ppermute | solution.py:23
  56.6 1.3 %collective-permute-start.10 = (bf16[10,128,128]{2,1,0:T(8,128)(2,1)S(1)}, bf16[10,128,128]{2,1,0:T(8,128)(2,1)S(1)}, u32[]{:S(2)}, u32[]{:S(2)}) collective-permute-start(bf16[10,128,128]{2,1,0:T(8,128)(2,1)S(1)} %get-tuple-element.98.refs_2_.refs_6_), channel_id=1, source_target_pairs={{0,1},{1,0},{2,3},{3,2},{4,5},{5,4},{6,7},{7,6},{8,9},{9,8},{10,11... | collective-permute-start | bytes 983048 | tf_op jit(solution)/shard_map/ppermute | solution.py:17
  58.2 2.9 %collective-permute-start.18 = (bf16[4,9,32,128]{3,2,1,0:T(8,128)(2,1)S(1)}, bf16[4,9,32,128]{3,2,1,0:T(8,128)(2,1)S(1)}, u32[]{:S(2)}, u32[]{:S(2)}) collective-permute-start(bf16[4,9,32,128]{3,2,1,0:T(8,128)(2,1)S(1)} %pad_maximum_fusion.8), channel_id=1, source_target_pairs={{1,4},{3,6},{5,8},{7,10},{9,12},{11,14},{13,16},{15,18},{17,20},{1... | collective-permute-start | bytes 884744 | tf_op jit(solution)/shard_map/ppermute | solution.py:23
  61.1 4.7 %shard_map.56 = (bf16[12,128,128]{2,1,0:T(8,128)(2,1)S(1)}, bf16[12,128,128]{2,1,0:T(8,128)(2,1)S(1)}) custom-call(bf16[4,12,32,128]{3,2,1,0:T(8,128)(2,1)S(1)} %get-tuple-element.87.refs_0_.refs_4_, bf16[4,12,32,128]{3,2,1,0:T(8,128)(2,1)S(1)} %collective-permute-done.5.refs_1_.refs_5_, ...), custom_call_target="tpu_custom_call" | custom-call | flops 5435817984 | bytes 2097152 | tf_op jit(solution)/shard_map/pallas_call | solution.py:147
  65.8 2.7 %collective-permute-start.16 = (bf16[12,128,128]{2,1,0:T(8,128)(2,1)S(1)}, bf16[12,128,128]{2,1,0:T(8,128)(2,1)S(1)}, u32[]{:S(2)}, u32[]{:S(2)}) collective-permute-start(bf16[12,128,128]{2,1,0:T(8,128)(2,1)S(1)} %get-tuple-element.114.refs_1_.refs_5_), channel_id=1, source_target_pairs={{1,4},{3,6},{5,8},{7,10},{9,12},{11,14},{13,16},{15,18},{17,20},{1... | collective-permute-start | bytes 1179656 | tf_op jit(solution)/shard_map/ppermute | solution.py:23
  71.0 3.6 %shard_map.58 = (bf16[2,9,32,128]{3,2,1,0:T(8,128)(2,1)S(1)}, bf16[2,9,32,128]{3,2,1,0:T(8,128)(2,1)S(1)}, bf16[2,2,9,32,128]{4,3,2,1,0:T(8,128)(2,1)S(1)}) custom-call(bf16[10,128,128]{2,1,0:T(8,128)(2,1)S(1)} %collective-permute-done.9.refs_0_.refs_4_, bf16[10,128,128]{2,1,0:T(8,128)(2,1)S(1)} %get-tuple-element.97.refs_1_.refs_5_, ...), custom_call_target="tpu_custom_call" | custom-call | flops 4076863488 | bytes 2097152 | tf_op jit(solution)/shard_map/pallas_call | solution.py:147
  75.0 2.1 %collective-permute-done.18.refs_3_ = bf16[4,9,32,128]{3,2,1,0:T(8,128)(2,1)S(1)} collective-permute-done((bf16[4,9,32,128]{3,2,1,0:T(8,128)(2,1)S(1)}, bf16[4,9,32,128]{3,2,1,0:T(8,128)(2,1)S(1)}, u32[]{:S(2)}, u32[]{:S(2)}) %collective-permute-start.18) | collective-permute-done | bytes 294944 | tf_op jit(solution)/shard_map/ppermute | solution.py:23
  77.1 4.2 %shard_map.59 = (bf16[10,128,128]{2,1,0:T(8,128)(2,1)S(1)}, bf16[10,128,128]{2,1,0:T(8,128)(2,1)S(1)}) custom-call(bf16[4,9,32,128]{3,2,1,0:T(8,128)(2,1)S(1)} %get-tuple-element.104.refs_0_, bf16[4,9,32,128]{3,2,1,0:T(8,128)(2,1)S(1)} %collective-permute-done.12.refs_1_, bf16[2,3,9,32,128]{4,3,2,1,0:T(8,128)(2,1)S(1)} %collective-permute-done.13.refs_2_, ...), custom_call_target="tpu_custom_call" | custom-call | flops 4529848320 | bytes 2097152 | tf_op jit(solution)/shard_map/pallas_call | solution.py:147
  81.4 2.1 %collective-permute-start.19 = (bf16[10,128,128]{2,1,0:T(8,128)(2,1)S(1)}, bf16[10,128,128]{2,1,0:T(8,128)(2,1)S(1)}, u32[]{:S(2)}, u32[]{:S(2)}) collective-permute-start(bf16[10,128,128]{2,1,0:T(8,128)(2,1)S(1)} %get-tuple-element.124.refs_1_), channel_id=1, source_target_pairs={{1,4},{3,6},{5,8},{7,10},{9,12},{11,14},{13,16},{15,18},{17,20},{1... | collective-permute-start | bytes 983048 | tf_op jit(solution)/shard_map/ppermute | solution.py:23
  83.5 5.4 %shard_map.60 = (bf16[2,12,32,128]{3,2,1,0:T(8,128)(2,1)S(1)}, bf16[2,12,32,128]{3,2,1,0:T(8,128)(2,1)S(1)}, bf16[2,2,12,32,128]{4,3,2,1,0:T(8,128)(2,1)S(1)}) custom-call(bf16[12,128,128]{2,1,0:T(8,128)(2,1)S(1)} %collective-permute-done.16.refs_0_.refs_4_, bf16[12,128,128]{2,1,0:T(8,128)(2,1)S(1)} %get-tuple-element.114.refs_1_.refs_5_, ...), custom_call_target="tpu_custom_call" | custom-call | flops 5435817984 | bytes 2097152 | tf_op jit(solution)/shard_map/pallas_call | solution.py:147
  89.3 1.3 %collective-permute-start.22 = (bf16[2,2,9,32,128]{4,3,2,1,0:T(8,128)(2,1)S(1)}, bf16[2,2,9,32,128]{4,3,2,1,0:T(8,128)(2,1)S(1)}, u32[]{:S(2)}, u32[]{:S(2)}) collective-permute-start(bf16[2,2,9,32,128]{4,3,2,1,0:T(8,128)(2,1)S(1)} %pad_maximum_fusion.9), channel_id=1, source_target_pairs={{0,1},{1,0},{2,3},{3,2},{4,5},{5,4},{6,7},{7,6},{8,9},{9,8},{10,11... | collective-permute-start | bytes 884744 | tf_op jit(solution)/shard_map/ppermute | solution.py:17
  90.7 2.9 %collective-permute-done.19.refs_0_ = bf16[10,128,128]{2,1,0:T(8,128)(2,1)S(1)} collective-permute-done((bf16[10,128,128]{2,1,0:T(8,128)(2,1)S(1)}, bf16[10,128,128]{2,1,0:T(8,128)(2,1)S(1)}, u32[]{:S(2)}, u32[]{:S(2)}) %collective-permute-start.19) | collective-permute-done | bytes 327712 | tf_op jit(solution)/shard_map/ppermute | solution.py:23
  93.6 5.0 %shard_map.61 = (bf16[2,11,32,128]{3,2,1,0:T(8,128)(2,1)S(1)}, bf16[2,11,32,128]{3,2,1,0:T(8,128)(2,1)S(1)}, bf16[2,11,32,128]{3,2,1,0:T(8,128)(2,1)S(1)}, bf16[2,11,32,128]{3,2,1,0:T(8,128)(2,1)S(1)}) custom-call(bf16[10,128,128]{2,1,0:T(8,128)(2,1)S(1)} %collective-permute-done.19.refs_0_, bf16[10,128,128]{2,1,0:T(8,128)(2,1)S(1)} %get-tuple-element.124.refs_1_, ...), custom_call_target="tpu_custom_call" | custom-call | flops 4982833152 | bytes 2097152 | tf_op jit(solution)/shard_map/pallas_call | solution.py:147
  99.0 1.8 %collective-permute-start.27 = (bf16[2,11,32,128]{3,2,1,0:T(8,128)(2,1)S(1)}, bf16[2,11,32,128]{3,2,1,0:T(8,128)(2,1)S(1)}, u32[]{:S(2)}, u32[]{:S(2)}) collective-permute-start(bf16[2,11,32,128]{3,2,1,0:T(8,128)(2,1)S(1)} %get-tuple-element.138), channel_id=1, source_target_pairs={{0,3},{1,2},{2,1},{3,0},{4,7},{5,6},{6,5},{7,4},{8,11},{9,10},{10,... | collective-permute-start | bytes 540680 | tf_op jit(solution)/shard_map/ppermute | solution.py:17
  101.0 3.4 %collective-permute-done.26 = bf16[2,11,32,128]{3,2,1,0:T(8,128)(2,1)S(1)} collective-permute-done((bf16[2,11,32,128]{3,2,1,0:T(8,128)(2,1)S(1)}, bf16[2,11,32,128]{3,2,1,0:T(8,128)(2,1)S(1)}, u32[]{:S(2)}, u32[]{:S(2)}) %collective-permute-start.26) | collective-permute-done | bytes 180256 | tf_op jit(solution)/shard_map/ppermute | solution.py:17
  104.8 4.0 %collective-permute-done.27 = bf16[2,11,32,128]{3,2,1,0:T(8,128)(2,1)S(1)} collective-permute-done((bf16[2,11,32,128]{3,2,1,0:T(8,128)(2,1)S(1)}, bf16[2,11,32,128]{3,2,1,0:T(8,128)(2,1)S(1)}, u32[]{:S(2)}, u32[]{:S(2)}) %collective-permute-start.27) | collective-permute-done | bytes 180256 | tf_op jit(solution)/shard_map/ppermute | solution.py:17
  109.5 2.1 %copy.9 = bf16[2,4,32,32,128]{4,3,2,1,0:T(8,128)(2,1)} copy(bf16[2,4,32,32,128]{4,2,3,1,0:T(8,128)(2,1)S(1)} %fusion) | data formatting | bytes 4194304 | tf_op jit(solution)/shard_map/transpose | solution.py:255
  (107 shorter events, 20.6 us)
Async XLA Ops:
  1.8 9.8 %collective-permute-start = (bf16[4,11,32,128]{3,2,1,0:T(8,128)(2,1)S(1)}, bf16[4,11,32,128]{3,2,1,0:T(8,128)(2,1)S(1)}, u32[]{:S(2)}, u32[]{:S(2)}) collective-permute-start(bf16[4,11,32,128]{3,2,1,0:T(8,128)(2,1)S(1)} %slice_bitcast_fusion.1), channel_id=1, source_target_pairs={{0,2},{1,3},{2,0},{3,1},{4,6},{5,7},{6,4},{7,5},{8,10},{9,11},{10,... | collective-permute-start | bytes 1081352 | tf_op jit(solution)/shard_map/ppermute | solution.py:17
  3.1 5.6 %collective-permute-start.1 = (f32[2,32]{1,0:T(2,128)S(1)}, f32[2,32]{1,0:T(2,128)S(1)}, u32[]{:S(2)}, u32[]{:S(2)}) collective-permute-start(f32[2,32]{1,0:T(2,128)S(1)} %pad_maximum_fusion.10), channel_id=1, source_target_pairs={{0,1},{1,0},{2,3},{3,2},{4,5},{5,4},{6,7},{7,6},{8,9},{9,8},{10,11... | collective-permute-start | bytes 776 | tf_op jit(solution)/shard_map/ppermute | solution.py:17
  8.7 2.8 %collective-permute-start.2 = (f32[2,64]{1,0:T(2,128)S(1)}, f32[2,64]{1,0:T(2,128)S(1)}, u32[]{:S(2)}, u32[]{:S(2)}) collective-permute-start(f32[2,64]{1,0:T(2,128)S(1)} %pad_maximum_fusion.11), channel_id=1, source_target_pairs={{0,2},{1,3},{2,0},{3,1},{4,6},{5,7},{6,4},{7,5},{8,10},{9,11},{10,... | collective-permute-start | bytes 1544 | tf_op jit(solution)/shard_map/ppermute | solution.py:17
  11.7 3.2 %collective-permute-start.3 = (bf16[2,3,11,32,128]{4,3,2,1,0:T(8,128)(2,1)S(1)}, bf16[2,3,11,32,128]{4,3,2,1,0:T(8,128)(2,1)S(1)}, u32[]{:S(2)}, u32[]{:S(2)}) collective-permute-start(bf16[2,3,11,32,128]{4,3,2,1,0:T(8,128)(2,1)S(1)} %pad_maximum_fusion.1), channel_id=1, source_target_pairs={{0,1},{1,0},{2,3},{3,2},{4,5},{5,4},{6,7},{7,6},{8,9},{9,8},{10,11... | collective-permute-start | bytes 1622024 | tf_op jit(solution)/shard_map/ppermute | solution.py:17
  15.8 10.9 %collective-permute-start.5 = (bf16[4,12,32,128]{3,2,1,0:T(8,128)(2,1)}, bf16[4,12,32,128]{3,2,1,0:T(8,128)(2,1)S(1)}, u32[]{:S(2)}, u32[]{:S(2)}) collective-permute-start(bf16[4,12,32,128]{3,2,1,0:T(8,128)(2,1)} %slice_bitcast_fusion), channel_id=1, source_target_pairs={{0,2},{1,3},{2,0},{3,1},{4,6},{5,7},{6,4},{7,5},{8,10},{9,11},{10,... | collective-permute-start | bytes 1179656 | tf_op jit(solution)/shard_map/ppermute | solution.py:17
  18.0 16.7 %copy-start.1 = (bf16[3,3,3,128,32]{3,4,2,1,0:T(8,128)(2,1)S(1)}, bf16[3,3,3,128,32]{3,4,2,1,0:T(8,128)(2,1)}, u32[]{:S(2)}) copy-start(bf16[3,3,3,128,32]{3,4,2,1,0:T(8,128)(2,1)} %param.6) | copy-start | bytes 663556
  27.6 20.2 %copy-start = (bf16[3,3,3,32,128]{4,3,2,1,0:T(8,128)(2,1)S(1)}, bf16[3,3,3,32,128]{4,3,2,1,0:T(8,128)(2,1)}, u32[]{:S(2)}) copy-start(bf16[3,3,3,32,128]{4,3,2,1,0:T(8,128)(2,1)} %param.8) | copy-start | bytes 663556
  27.6 8.4 %collective-permute-start.6 = (bf16[2,3,12,32,128]{4,3,2,1,0:T(8,128)(2,1)}, bf16[2,3,12,32,128]{4,3,2,1,0:T(8,128)(2,1)S(1)}, u32[]{:S(2)}, u32[]{:S(2)}) collective-permute-start(bf16[2,3,12,32,128]{4,3,2,1,0:T(8,128)(2,1)} %pad_maximum_fusion), channel_id=1, source_target_pairs={{0,1},{1,0},{2,3},{3,2},{4,5},{5,4},{6,7},{7,6},{8,9},{9,8},{10,11... | collective-permute-start | bytes 1769480 | tf_op jit(solution)/shard_map/ppermute | solution.py:17
  31.5 4.7 %copy-start.4 = (bf16[4,9,32,128]{3,2,1,0:T(8,128)(2,1)S(1)}, bf16[4,9,32,128]{3,2,1,0:T(8,128)(2,1)}, u32[]{:S(2)}) copy-start(bf16[4,9,32,128]{3,2,1,0:T(8,128)(2,1)} %slice_bitcast_fusion.2) | copy-start | bytes 884740
  31.5 17.6 %copy-start.3 = (bf16[1,3,9,32,128]{4,3,2,1,0:T(8,128)(2,1)S(1)}, bf16[1,3,9,32,128]{4,3,2,1,0:T(8,128)(2,1)}, u32[]{:S(2)}) copy-start(bf16[1,3,9,32,128]{4,3,2,1,0:T(8,128)(2,1)} %dynamic-slice_bitcast_fusion.5) | copy-start | bytes 663556
  31.5 14.4 %collective-permute-start.4 = (bf16[4,11,32,128]{3,2,1,0:T(8,128)(2,1)}, bf16[4,11,32,128]{3,2,1,0:T(8,128)(2,1)S(1)}, u32[]{:S(2)}, u32[]{:S(2)}) collective-permute-start(bf16[4,11,32,128]{3,2,1,0:T(8,128)(2,1)} %pad_maximum_fusion.7), channel_id=1, source_target_pairs={{1,4},{3,6},{5,8},{7,10},{9,12},{11,14},{13,16},{15,18},{17,20},{1... | collective-permute-start | bytes 1081352 | tf_op jit(solution)/shard_map/ppermute | solution.py:23
  34.7 6.8 %collective-permute-start.7 = (bf16[27,32,128]{2,1,0:T(8,128)(2,1)S(1)}, bf16[27,32,128]{2,1,0:T(8,128)(2,1)S(1)}, u32[]{:S(2)}, u32[]{:S(2)}) collective-permute-start(bf16[27,32,128]{2,1,0:T(8,128)(2,1)S(1)} %bitcast.105), channel_id=1, source_target_pairs={{0,2},{1,3},{2,0},{3,1},{4,6},{5,7},{6,4},{7,5},{8,10},{9,11},{10,... | collective-permute-start | bytes 663560 | tf_op jit(solution)/shard_map/ppermute | solution.py:17
  36.2 11.6 %collective-permute-start.12 = (bf16[4,9,32,128]{3,2,1,0:T(8,128)(2,1)S(1)}, bf16[4,9,32,128]{3,2,1,0:T(8,128)(2,1)S(1)}, u32[]{:S(2)}, u32[]{:S(2)}) collective-permute-start(bf16[4,9,32,128]{3,2,1,0:T(8,128)(2,1)S(1)} %copy-done.4), channel_id=1, source_target_pairs={{0,2},{1,3},{2,0},{3,1},{4,6},{5,7},{6,4},{7,5},{8,10},{9,11},{10,... | collective-permute-start | bytes 884744 | tf_op jit(solution)/shard_map/ppermute | solution.py:17
  41.6 9.0 %collective-permute-start.8 = (bf16[2,27,32,128]{3,2,1,0:T(8,128)(2,1)S(1)}, bf16[2,27,32,128]{3,2,1,0:T(8,128)(2,1)S(1)}, u32[]{:S(2)}, u32[]{:S(2)}) collective-permute-start(bf16[2,27,32,128]{3,2,1,0:T(8,128)(2,1)S(1)} %pad_maximum_fusion.2), channel_id=1, source_target_pairs={{0,1},{1,0},{2,3},{3,2},{4,5},{5,4},{6,7},{7,6},{8,9},{9,8},{10,11... | collective-permute-start | bytes 1327112 | tf_op jit(solution)/shard_map/ppermute | solution.py:17
  43.6 17.5 %collective-permute-start.11 = (bf16[4,12,32,128]{3,2,1,0:T(8,128)(2,1)S(1)}, bf16[4,12,32,128]{3,2,1,0:T(8,128)(2,1)S(1)}, u32[]{:S(2)}, u32[]{:S(2)}) collective-permute-start(bf16[4,12,32,128]{3,2,1,0:T(8,128)(2,1)S(1)} %pad_maximum_fusion.5), channel_id=1, source_target_pairs={{1,4},{3,6},{5,8},{7,10},{9,12},{11,14},{13,16},{15,18},{17,20},{1... | collective-permute-start | bytes 1179656 | tf_op jit(solution)/shard_map/ppermute | solution.py:23
  47.8 10.1 %collective-permute-start.14 = (bf16[27,32,128]{2,1,0:T(8,128)(2,1)S(1)}, bf16[27,32,128]{2,1,0:T(8,128)(2,1)S(1)}, u32[]{:S(2)}, u32[]{:S(2)}) collective-permute-start(bf16[27,32,128]{2,1,0:T(8,128)(2,1)S(1)} %bitcast.102), channel_id=1, source_target_pairs={{0,2},{1,3},{2,0},{3,1},{4,6},{5,7},{6,4},{7,5},{8,10},{9,11},{10,... | collective-permute-start | bytes 663560 | tf_op jit(solution)/shard_map/ppermute | solution.py:17
  49.1 8.9 %collective-permute-start.13 = (bf16[2,3,9,32,128]{4,3,2,1,0:T(8,128)(2,1)S(1)}, bf16[2,3,9,32,128]{4,3,2,1,0:T(8,128)(2,1)S(1)}, u32[]{:S(2)}, u32[]{:S(2)}) collective-permute-start(bf16[2,3,9,32,128]{4,3,2,1,0:T(8,128)(2,1)S(1)} %pad_maximum_fusion.3), channel_id=1, source_target_pairs={{0,1},{1,0},{2,3},{3,2},{4,5},{5,4},{6,7},{7,6},{8,9},{9,8},{10,11... | collective-permute-start | bytes 1327112 | tf_op jit(solution)/shard_map/ppermute | solution.py:17
  54.7 15.1 %collective-permute-start.9 = (bf16[10,128,128]{2,1,0:T(8,128)(2,1)S(1)}, bf16[10,128,128]{2,1,0:T(8,128)(2,1)S(1)}, u32[]{:S(2)}, u32[]{:S(2)}) collective-permute-start(bf16[10,128,128]{2,1,0:T(8,128)(2,1)S(1)} %get-tuple-element.97.refs_1_.refs_5_), channel_id=1, source_target_pairs={{1,4},{3,6},{5,8},{7,10},{9,12},{11,14},{13,16},{15,18},{17,20},{1... | collective-permute-start | bytes 983048 | tf_op jit(solution)/shard_map/ppermute | solution.py:23
  56.6 13.1 %collective-permute-start.10 = (bf16[10,128,128]{2,1,0:T(8,128)(2,1)S(1)}, bf16[10,128,128]{2,1,0:T(8,128)(2,1)S(1)}, u32[]{:S(2)}, u32[]{:S(2)}) collective-permute-start(bf16[10,128,128]{2,1,0:T(8,128)(2,1)S(1)} %get-tuple-element.98.refs_2_.refs_6_), channel_id=1, source_target_pairs={{0,1},{1,0},{2,3},{3,2},{4,5},{5,4},{6,7},{7,6},{8,9},{9,8},{10,11... | collective-permute-start | bytes 983048 | tf_op jit(solution)/shard_map/ppermute | solution.py:17
  58.0 12.0 %collective-permute-start.15 = (bf16[2,27,32,128]{3,2,1,0:T(8,128)(2,1)S(1)}, bf16[2,27,32,128]{3,2,1,0:T(8,128)(2,1)S(1)}, u32[]{:S(2)}, u32[]{:S(2)}) collective-permute-start(bf16[2,27,32,128]{3,2,1,0:T(8,128)(2,1)S(1)} %pad_maximum_fusion.4), channel_id=1, source_target_pairs={{0,1},{1,0},{2,3},{3,2},{4,5},{5,4},{6,7},{7,6},{8,9},{9,8},{10,11... | collective-permute-start | bytes 1327112 | tf_op jit(solution)/shard_map/ppermute | solution.py:17
  58.2 18.9 %collective-permute-start.18 = (bf16[4,9,32,128]{3,2,1,0:T(8,128)(2,1)S(1)}, bf16[4,9,32,128]{3,2,1,0:T(8,128)(2,1)S(1)}, u32[]{:S(2)}, u32[]{:S(2)}) collective-permute-start(bf16[4,9,32,128]{3,2,1,0:T(8,128)(2,1)S(1)} %pad_maximum_fusion.8), channel_id=1, source_target_pairs={{1,4},{3,6},{5,8},{7,10},{9,12},{11,14},{13,16},{15,18},{17,20},{1... | collective-permute-start | bytes 884744 | tf_op jit(solution)/shard_map/ppermute | solution.py:23
  65.8 17.7 %collective-permute-start.16 = (bf16[12,128,128]{2,1,0:T(8,128)(2,1)S(1)}, bf16[12,128,128]{2,1,0:T(8,128)(2,1)S(1)}, u32[]{:S(2)}, u32[]{:S(2)}) collective-permute-start(bf16[12,128,128]{2,1,0:T(8,128)(2,1)S(1)} %get-tuple-element.114.refs_1_.refs_5_), channel_id=1, source_target_pairs={{1,4},{3,6},{5,8},{7,10},{9,12},{11,14},{13,16},{15,18},{17,20},{1... | collective-permute-start | bytes 1179656 | tf_op jit(solution)/shard_map/ppermute | solution.py:23
  69.7 13.7 %collective-permute-start.17 = (bf16[12,128,128]{2,1,0:T(8,128)(2,1)S(1)}, bf16[12,128,128]{2,1,0:T(8,128)(2,1)S(1)}, u32[]{:S(2)}, u32[]{:S(2)}) collective-permute-start(bf16[12,128,128]{2,1,0:T(8,128)(2,1)S(1)} %get-tuple-element.115.refs_2_.refs_6_), channel_id=1, source_target_pairs={{0,1},{1,0},{2,3},{3,2},{4,5},{5,4},{6,7},{7,6},{8,9},{9,8},{10,11... | collective-permute-start | bytes 1179656 | tf_op jit(solution)/shard_map/ppermute | solution.py:17
  74.7 14.6 %collective-permute-start.21 = (bf16[2,2,9,32,128]{4,3,2,1,0:T(8,128)(2,1)S(1)}, bf16[2,2,9,32,128]{4,3,2,1,0:T(8,128)(2,1)S(1)}, u32[]{:S(2)}, u32[]{:S(2)}) collective-permute-start(bf16[2,2,9,32,128]{4,3,2,1,0:T(8,128)(2,1)S(1)} %get-tuple-element.133), channel_id=1, source_target_pairs={{0,2},{1,3},{2,0},{3,1},{4,6},{5,7},{6,4},{7,5},{8,10},{9,11},{10,... | collective-permute-start | bytes 884744 | tf_op jit(solution)/shard_map/ppermute | solution.py:17
  81.3 9.3 %collective-permute-start.20 = (bf16[10,128,128]{2,1,0:T(8,128)(2,1)S(1)}, bf16[10,128,128]{2,1,0:T(8,128)(2,1)S(1)}, u32[]{:S(2)}, u32[]{:S(2)}) collective-permute-start(bf16[10,128,128]{2,1,0:T(8,128)(2,1)S(1)} %get-tuple-element.125.refs_2_), channel_id=1, source_target_pairs={{0,1},{1,0},{2,3},{3,2},{4,5},{5,4},{6,7},{7,6},{8,9},{9,8},{10,11... | collective-permute-start | bytes 983048 | tf_op jit(solution)/shard_map/ppermute | solution.py:17
  81.4 12.2 %collective-permute-start.19 = (bf16[10,128,128]{2,1,0:T(8,128)(2,1)S(1)}, bf16[10,128,128]{2,1,0:T(8,128)(2,1)S(1)}, u32[]{:S(2)}, u32[]{:S(2)}) collective-permute-start(bf16[10,128,128]{2,1,0:T(8,128)(2,1)S(1)} %get-tuple-element.124.refs_1_), channel_id=1, source_target_pairs={{1,4},{3,6},{5,8},{7,10},{9,12},{11,14},{13,16},{15,18},{17,20},{1... | collective-permute-start | bytes 983048 | tf_op jit(solution)/shard_map/ppermute | solution.py:23
  88.9 11.9 %collective-permute-start.23 = (bf16[2,2,12,32,128]{4,3,2,1,0:T(8,128)(2,1)S(1)}, bf16[2,2,12,32,128]{4,3,2,1,0:T(8,128)(2,1)S(1)}, u32[]{:S(2)}, u32[]{:S(2)}) collective-permute-start(bf16[2,2,12,32,128]{4,3,2,1,0:T(8,128)(2,1)S(1)} %get-tuple-element.135), channel_id=1, source_target_pairs={{0,2},{1,3},{2,0},{3,1},{4,6},{5,7},{6,4},{7,5},{8,10},{9,11},{10,... | collective-permute-start | bytes 1179656 | tf_op jit(solution)/shard_map/ppermute | solution.py:17
  89.3 15.2 %collective-permute-start.22 = (bf16[2,2,9,32,128]{4,3,2,1,0:T(8,128)(2,1)S(1)}, bf16[2,2,9,32,128]{4,3,2,1,0:T(8,128)(2,1)S(1)}, u32[]{:S(2)}, u32[]{:S(2)}) collective-permute-start(bf16[2,2,9,32,128]{4,3,2,1,0:T(8,128)(2,1)S(1)} %pad_maximum_fusion.9), channel_id=1, source_target_pairs={{0,1},{1,0},{2,3},{3,2},{4,5},{5,4},{6,7},{7,6},{8,9},{9,8},{10,11... | collective-permute-start | bytes 884744 | tf_op jit(solution)/shard_map/ppermute | solution.py:17
  98.6 6.0 %collective-permute-start.25 = (bf16[2,11,32,128]{3,2,1,0:T(8,128)(2,1)S(1)}, bf16[2,11,32,128]{3,2,1,0:T(8,128)(2,1)S(1)}, u32[]{:S(2)}, u32[]{:S(2)}) collective-permute-start(bf16[2,11,32,128]{3,2,1,0:T(8,128)(2,1)S(1)} %get-tuple-element.136), channel_id=1, source_target_pairs={{0,1},{1,0},{2,3},{3,2},{4,5},{5,4},{6,7},{7,6},{8,9},{9,8},{10,11... | collective-permute-start | bytes 540680 | tf_op jit(solution)/shard_map/ppermute | solution.py:17
  98.7 5.8 %collective-permute-start.26 = (bf16[2,11,32,128]{3,2,1,0:T(8,128)(2,1)S(1)}, bf16[2,11,32,128]{3,2,1,0:T(8,128)(2,1)S(1)}, u32[]{:S(2)}, u32[]{:S(2)}) collective-permute-start(bf16[2,11,32,128]{3,2,1,0:T(8,128)(2,1)S(1)} %get-tuple-element.137), channel_id=1, source_target_pairs={{0,2},{1,3},{2,0},{3,1},{4,6},{5,7},{6,4},{7,5},{8,10},{9,11},{10,... | collective-permute-start | bytes 540680 | tf_op jit(solution)/shard_map/ppermute | solution.py:17
  99.0 9.9 %collective-permute-start.27 = (bf16[2,11,32,128]{3,2,1,0:T(8,128)(2,1)S(1)}, bf16[2,11,32,128]{3,2,1,0:T(8,128)(2,1)S(1)}, u32[]{:S(2)}, u32[]{:S(2)}) collective-permute-start(bf16[2,11,32,128]{3,2,1,0:T(8,128)(2,1)S(1)} %get-tuple-element.138), channel_id=1, source_target_pairs={{0,3},{1,2},{2,1},{3,0},{4,7},{5,6},{6,5},{7,4},{8,11},{9,10},{10,... | collective-permute-start | bytes 540680 | tf_op jit(solution)/shard_map/ppermute | solution.py:17
  100.9 3.7 %collective-permute-start.24 = (bf16[2,2,12,32,128]{4,3,2,1,0:T(8,128)(2,1)S(1)}, bf16[2,2,12,32,128]{4,3,2,1,0:T(8,128)(2,1)S(1)}, u32[]{:S(2)}, u32[]{:S(2)}) collective-permute-start(bf16[2,2,12,32,128]{4,3,2,1,0:T(8,128)(2,1)S(1)} %pad_maximum_fusion.6), channel_id=1, source_target_pairs={{0,1},{1,0},{2,3},{3,2},{4,5},{5,4},{6,7},{7,6},{8,9},{9,8},{10,11... | collective-permute-start | bytes 1179656 | tf_op jit(solution)/shard_map/ppermute | solution.py:17
  (3 other events, 9.7 us)

commit v4 on v3

--- a/solution.py
+++ b/solution.py
@@ -9,7 +9,7 @@
 
 BF = jnp.bfloat16
 VMEM_LIMIT = 48 * 2**20
-CUTS = (9, 21, 32)
+CUTS = (11, 23, 32)
 UNROLL = 3
 
 
@@ -178,10 +178,6 @@
         edge = jnp.stack([layer(own, 3 * c), layer(sr[0], 2 * c), layer(xr, 3 * c), layer(sr[1], 2 * c)])
         return (own, xr, sr, slab_swap(edge)), edge
 
-    def weight_pieces(own, earlier):
-        across = chan_swap(after(own, earlier), 2)
-        return (own, across, chan_swap(jnp.stack([own, across]), 1))
-
     sent = cut(0, 1 - b)
     xr = chan_swap(sent, 2)
     (volume, w1, w2, biases), _ = lax.optimization_barrier(
@@ -192,35 +188,53 @@
     biases = jnp.concatenate([biases, chan_swap(biases, 2)], axis=1)
     w1 = jnp.transpose(w1, (0, 1, 2, 4, 3)).reshape(27, unit, chans)
     w2 = w2.reshape(27, unit, chans)
-    xr, biases = lax.optimization_barrier((xr, biases))
-    received, edges = [], []
-    for chunk in range(parts):
-        arrays, edge = share(cut(chunk, b), xr)
-        received.append(arrays)
-        edges.append(edge)
-        if chunk == 0:
-            first = weight_pieces(w1, edge)
-        if chunk < parts - 1:
-            xr = chan_swap(after(cut(chunk + 1, 1 - b), xr, edge), 2)
-    second = weight_pieces(w2, xr)
+    home = [cut(k, b) for k in range(parts)]
+    away = [None] + [cut(k, 1 - b) for k in range(1, parts)]
+    xr, biases, w1, home[0], away[1] = lax.optimization_barrier((xr, biases, w1, home[0], away[1]))
 
     order = [jnp.concatenate([layer(v.reshape(4, unit), me ^ q) for q in range(4)]) for v in biases[:1]] + [biases[1]]
     bias1, bias2 = (jnp.broadcast_to(v[:, None], (chans, width)) for v in order)
-    full2 = call(weights_kernel_body, [(27, chans, chans)], second, (), [(27, chans, chans)], 4, 10**9)[0]
-
-    unit_flops = 2 * 4 * width * 27 * chans * chans
-    hidden = []
-    for chunk in range(parts):
+
+    unit_flops = 4 * width * 27 * chans * chans
+    received, hidden, weights = [], [], []
+
+    def first_conv(chunk, edge):
         n = hidden_ends[chunk + 1] - hidden_ends[chunk]
         operands = received[chunk] + (received[chunk - 1] if chunk else ())
-        operands = after(operands, edges[chunk + 1 : chunk + 2])
+        if edge is not None:
+            operands = after(operands, edge)
         to_slab, to_sib = call(
             functools.partial(first_kernel_body, chunk > 0, chunk == parts - 1),
-            [(n, chans, width)] * 2, (*operands, *first), (bias1,),
+            [(n, chans, width)] * 2, (*operands, *weights[0]), (bias1,),
             [(4, n + 2, chans, width), (27, chans, chans)],
-            4 + 8 * (1 + (chunk > 0)), unit_flops * n,
+            4 + 8 * (1 + (chunk > 0)), 2 * unit_flops * n,
         )
         hidden.append((slab_swap(to_slab), to_slab, to_sib, chan_swap(to_sib, 1)))
+        return to_slab
+
+    for chunk in range(parts):
+        arrays, edge = share(home[chunk], xr)
+        side = arrays[3]
+        ready = []
+        if chunk == 0:
+            ready = [home[1:], away[2:], w2, bias1, bias2]
+        else:
+            ready = first_conv(chunk - 1, edge)
+        before = xr
+        if chunk < parts - 1:
+            xr = chan_swap(after(away[chunk + 1], before), 2)
+        if chunk < 2:
+            own = (w1, w2)[chunk]
+            across = chan_swap(after(own, before), 2)
+            (side, xr, across), ready = lax.optimization_barrier(((side, xr, across), ready))
+            weights.append((own, across, chan_swap(jnp.stack([own, across]), 1)))
+        else:
+            side, ready = lax.optimization_barrier((side, ready))
+        if chunk == 0:
+            home[1:], away[2:], w2, bias1, bias2 = ready
+        received.append((*arrays[:3], side))
+    first_conv(parts - 1, None)
+    full2 = call(weights_kernel_body, [(27, chans, chans)], weights[1], (), [(27, chans, chans)], 4, 10**9)[0]
 
     own, other, sibling, diagonal = [], [], [], []
     for chunk in range(parts):
@@ -228,30 +242,32 @@
         operands = hidden[chunk] + (hidden[chunk - 1] if chunk else ())
         operands = after(operands, [h[1] for h in hidden[chunk + 1 : chunk + 2]])
         last = chunk == parts - 1
+        if last:
+            operands = after(operands, sibling[:-1])
         block = (2, n, unit, width)
         outs = call(
             functools.partial(second_kernel_body, chunk > 0, last),
             [block] * 4 if last else [block, block, (2, *block)], operands, (full2, bias2),
-            [(4, n + 2, chans, width)], 4 * (1 + (chunk > 0)), unit_flops * n,
+            [(4, n + 2, chans, width)], 4 * (1 + (chunk > 0)), 2 * unit_flops * n,
         )
         own.append(outs[0])
         if last:
             x, s, d = (chan_swap(outs[k], k) for k in (2, 1, 3))
         else:
             got = chan_swap(outs[2], 2)
-            x = got[0]
-            s, d = chan_swap(jnp.stack([outs[1], got[1]]), 1)
+            x, passed = got[0], jnp.stack([outs[1], got[1]])
+            s, d = (None, None) if chunk == parts - 2 else chan_swap(passed, 1)
         other.append(x)
         sibling.append(s)
         diagonal.append(d)
+    sibling[-2], diagonal[-2] = chan_swap(after(passed, sibling[-1]), 1)
 
     def layers(near, far):
         near, far = jnp.concatenate(near, axis=1), jnp.concatenate(far, axis=1)
         return jnp.where(c == 0, jnp.concatenate([near, far]), jnp.concatenate([far, near]))
 
-    home = layers(own, sibling)
-    away = layers(other, diagonal)
-    out = jnp.where(b == 0, jnp.stack([home, away]), jnp.stack([away, home]))
+    near, far = layers(own, sibling), layers(other, diagonal)
+    out = jnp.where(b == 0, jnp.stack([near, far]), jnp.stack([far, near]))
     return jnp.transpose(out, (0, 1, 3, 2, 4))
 
 

time: 112 us -> 110 us (0.982)
  local copies, waits for them, and re-layouts: 16.1 us -> 7.98 us
  waiting for transfers between devices: 30.8 us -> 36.8 us
    ppermute x22, waiting for transfers between devices: 24.5 us -> 29.8 us  [chan_swap(): return lax.ppermute(value, 'chan', [(i, i ^ k) for i in range(4)])]
    dynamic_slice x5 -> x3, local copies, waits for them, and re-layouts: 5.56 us -> 2.28 us  [cut(): part = lax.dynamic_index_in_dim(volume, batch, 0, keepdims=False)]
    transpose x5 -> x6, local copies, waits for them, and re-layouts: 4.71 us -> 1.68 us  [cut(): jnp.transpose(part[:, :, in_ends[chunk]:in_ends[chunk + 1]], (0, 2, 1, 3))]
  transfers between devices with their start and end apart: 28 -> 28, of which waited for: 9 -> 11; matrix products, arithmetic and copies ran while one was open for 12% -> 5% of each run, Pallas kernels for 25% -> 25%
where the time goes in v4:
time: 110 us; the launch traced here: 109 us
  waiting for transfers between devices  36.8 us (33%)
  starting transfers between devices  33.9 us (31%)
  Pallas kernels  27.8 us (25%)
  local copies, waits for them, and re-layouts  7.98 us (7%)
  other arithmetic  2.37 us (2%)
    ppermute x22, waiting for transfers between devices, chan_swap(): return lax.ppermute(value, 'chan', [(i, i ^ k) for i in range(4)])  29.8 us
    pallas_call x7, Pallas kernels, call(): pl.pallas_call(body, out_shape=[jax.ShapeDtypeStruct(s, BF) for s in outs...  27.8 us
    ppermute x22, starting transfers between devices, chan_swap(): return lax.ppermute(value, 'chan', [(i, i ^ k) for i in range(4)])  18.8 us
    ppermute x6, starting transfers between devices, slab_swap(): lax.ppermute(value, ('slab', 'chan'), pairs + [(j, i) for i, j in pairs])  15.1 us
    ppermute x6, waiting for transfers between devices, slab_swap(): lax.ppermute(value, ('slab', 'chan'), pairs + [(j, i) for i, j in pairs])  6.97 us
    dynamic_slice x3, local copies, waits for them, and re-layouts, cut(): part = lax.dynamic_index_in_dim(volume, batch, 0, keepdims=False)  2.28 us
  transfers between devices with their start and end apart: 28, of which 11 were waited for; matrix products, arithmetic and copies ran while one was open for 5% of the time, Pallas kernels for 25%

profile of v4, /device:TPU:25, one launch (start us, length us, event | category | flops | bytes accessed | tf_op | source)
XLA Modules:
  0.0 109.4 jit_solution(10612573948251230872)
XLA Ops:
  0.0 1.5 %constant_dynamic-slice_fusion.12 = bf16[1,4,32,32,128]{4,3,2,1,0:T(8,128)(2,1)S(1)} fusion(bf16[2,4,32,32,128]{4,3,2,1,0:T(8,128)(2,1)} %param.5, s32[]{:T(128)S(6)} %select_n.103), kind=kLoop, calls=%fused_computation.57 | loop fusion | bytes 2097156 | tf_op jit(solution)/shard_map/jit(dynamic_index_in_dim)/dynamic_slice | solution.py:169
  1.9 1.3 %collective-permute-start = (bf16[4,13,32,128]{3,2,1,0:T(8,128)(2,1)S(1)}, bf16[4,13,32,128]{3,2,1,0:T(8,128)(2,1)S(1)}, u32[]{:S(2)}, u32[]{:S(2)}) collective-permute-start(bf16[4,13,32,128]{3,2,1,0:T(8,128)(2,1)S(1)} %slice_bitcast_fusion.1), channel_id=1, source_target_pairs={{0,2},{1,3},{2,0},{3,1},{4,6},{5,7},{6,4},{7,5},{8,10},{9,11},{10,... | collective-permute-start | bytes 1277960 | tf_op jit(solution)/shard_map/ppermute | solution.py:17
  7.7 5.0 %collective-permute-done.2 = f32[2,64]{1,0:T(2,128)S(1)} collective-permute-done((f32[2,64]{1,0:T(2,128)S(1)}, f32[2,64]{1,0:T(2,128)S(1)}, u32[]{:S(2)}, u32[]{:S(2)}) %collective-permute-start.2) | collective-permute-done | bytes 544 | tf_op jit(solution)/shard_map/ppermute | solution.py:17
  12.9 1.7 %collective-permute-start.3 = (bf16[2,3,13,32,128]{4,3,2,1,0:T(8,128)(2,1)S(1)}, bf16[2,3,13,32,128]{4,3,2,1,0:T(8,128)(2,1)S(1)}, u32[]{:S(2)}, u32[]{:S(2)}) collective-permute-start(bf16[2,3,13,32,128]{4,3,2,1,0:T(8,128)(2,1)S(1)} %pad_maximum_fusion), channel_id=1, source_target_pairs={{0,1},{1,0},{2,3},{3,2},{4,5},{5,4},{6,7},{7,6},{8,9},{9,8},{10,11... | collective-permute-start | bytes 1916936 | tf_op jit(solution)/shard_map/ppermute | solution.py:17
  14.6 1.3 %collective-permute-start.5 = (bf16[4,12,32,128]{3,2,1,0:T(8,128)(2,1)}, bf16[4,12,32,128]{3,2,1,0:T(8,128)(2,1)S(1)}, u32[]{:S(2)}, u32[]{:S(2)}) collective-permute-start(bf16[4,12,32,128]{3,2,1,0:T(8,128)(2,1)} %slice_bitcast_fusion.3), channel_id=1, source_target_pairs={{0,2},{1,3},{2,0},{3,1},{4,6},{5,7},{6,4},{7,5},{8,10},{9,11},{10,... | collective-permute-start | bytes 1179656 | tf_op jit(solution)/shard_map/ppermute | solution.py:17
  17.2 3.4 %collective-permute-start.4 = (bf16[4,13,32,128]{3,2,1,0:T(8,128)(2,1)}, bf16[4,13,32,128]{3,2,1,0:T(8,128)(2,1)S(1)}, u32[]{:S(2)}, u32[]{:S(2)}) collective-permute-start(bf16[4,13,32,128]{3,2,1,0:T(8,128)(2,1)} %pad_maximum_fusion.4), channel_id=1, source_target_pairs={{1,4},{3,6},{5,8},{7,10},{9,12},{11,14},{13,16},{15,18},{17,20},{1... | collective-permute-start | bytes 1277960 | tf_op jit(solution)/shard_map/ppermute | solution.py:23
  22.0 8.3 %collective-permute-done.6.refs_5_.refs_9_ = bf16[27,32,128]{2,1,0:T(8,128)(2,1)S(1)} collective-permute-done((bf16[27,32,128]{2,1,0:T(8,128)(2,1)S(1)}, bf16[27,32,128]{2,1,0:T(8,128)(2,1)S(1)}, u32[]{:S(2)}, u32[]{:S(2)}) %collective-permute-start.6) | collective-permute-done | bytes 221216 | tf_op jit(solution)/shard_map/ppermute | solution.py:17
  31.8 1.3 %collective-permute-start.13 = (bf16[27,32,128]{2,1,0:T(8,128)(2,1)S(1)}, bf16[27,32,128]{2,1,0:T(8,128)(2,1)S(1)}, u32[]{:S(2)}, u32[]{:S(2)}) collective-permute-start(bf16[27,32,128]{2,1,0:T(8,128)(2,1)S(1)} %bitcast.87), channel_id=1, source_target_pairs={{0,2},{1,3},{2,0},{3,1},{4,6},{5,7},{6,4},{7,5},{8,10},{9,11},{10,... | collective-permute-start | bytes 663560 | tf_op jit(solution)/shard_map/ppermute | solution.py:17
  34.7 2.4 %collective-permute-start.11 = (bf16[4,12,32,128]{3,2,1,0:T(8,128)(2,1)S(1)}, bf16[4,12,32,128]{3,2,1,0:T(8,128)(2,1)S(1)}, u32[]{:S(2)}, u32[]{:S(2)}) collective-permute-start(bf16[4,12,32,128]{3,2,1,0:T(8,128)(2,1)S(1)} %pad_maximum_fusion.5), channel_id=1, source_target_pairs={{1,4},{3,6},{5,8},{7,10},{9,12},{11,14},{13,16},{15,18},{17,20},{1... | collective-permute-start | bytes 1179656 | tf_op jit(solution)/shard_map/ppermute | solution.py:23
  37.1 4.6 %shard_map.55 = (bf16[12,128,128]{2,1,0:T(8,128)(2,1)S(1)}, bf16[12,128,128]{2,1,0:T(8,128)(2,1)S(1)}) custom-call(bf16[4,13,32,128]{3,2,1,0:T(8,128)(2,1)S(1)} %slice_bitcast_fusion.refs_0_.refs_4_, bf16[4,13,32,128]{3,2,1,0:T(8,128)(2,1)S(1)} %collective-permute-done.refs_1_.refs_5_, ...), custom_call_target="tpu_custom_call" | custom-call | flops 5435817984 | bytes 2097152 | tf_op jit(solution)/shard_map/pallas_call | solution.py:147
  41.7 1.7 %collective-permute-done.12.refs_1_ = bf16[4,7,32,128]{3,2,1,0:T(8,128)(2,1)S(1)} collective-permute-done((bf16[4,7,32,128]{3,2,1,0:T(8,128)(2,1)S(1)}, bf16[4,7,32,128]{3,2,1,0:T(8,128)(2,1)S(1)}, u32[]{:S(2)}, u32[]{:S(2)}) %collective-permute-start.12) | collective-permute-done | bytes 229408 | tf_op jit(solution)/shard_map/ppermute | solution.py:17
  43.4 4.6 %collective-permute-done.11.refs_3_.refs_7_ = bf16[4,12,32,128]{3,2,1,0:T(8,128)(2,1)S(1)} collective-permute-done((bf16[4,12,32,128]{3,2,1,0:T(8,128)(2,1)S(1)}, bf16[4,12,32,128]{3,2,1,0:T(8,128)(2,1)S(1)}, u32[]{:S(2)}, u32[]{:S(2)}) %collective-permute-start.11) | collective-permute-done | bytes 393248 | tf_op jit(solution)/shard_map/ppermute | solution.py:23
  48.1 1.9 %collective-permute-start.9 = (bf16[12,128,128]{2,1,0:T(8,128)(2,1)S(1)}, bf16[12,128,128]{2,1,0:T(8,128)(2,1)S(1)}, u32[]{:S(2)}, u32[]{:S(2)}) collective-permute-start(bf16[12,128,128]{2,1,0:T(8,128)(2,1)S(1)} %get-tuple-element.143.refs_1_.refs_5_), channel_id=1, source_target_pairs={{1,4},{3,6},{5,8},{7,10},{9,12},{11,14},{13,16},{15,18},{17,20},{1... | collective-permute-start | bytes 1179656 | tf_op jit(solution)/shard_map/ppermute | solution.py:23
  50.1 1.5 %collective-permute-start.10 = (bf16[12,128,128]{2,1,0:T(8,128)(2,1)S(1)}, bf16[12,128,128]{2,1,0:T(8,128)(2,1)S(1)}, u32[]{:S(2)}, u32[]{:S(2)}) collective-permute-start(bf16[12,128,128]{2,1,0:T(8,128)(2,1)S(1)} %get-tuple-element.144.refs_2_.refs_6_), channel_id=1, source_target_pairs={{0,1},{1,0},{2,3},{3,2},{4,5},{5,4},{6,7},{7,6},{8,9},{9,8},{10,11... | collective-permute-start | bytes 1179656 | tf_op jit(solution)/shard_map/ppermute | solution.py:17
  51.9 2.7 %collective-permute-start.18 = (bf16[4,7,32,128]{3,2,1,0:T(8,128)(2,1)S(1)}, bf16[4,7,32,128]{3,2,1,0:T(8,128)(2,1)S(1)}, u32[]{:S(2)}, u32[]{:S(2)}) collective-permute-start(bf16[4,7,32,128]{3,2,1,0:T(8,128)(2,1)S(1)} %pad_maximum_fusion.9), channel_id=1, source_target_pairs={{1,4},{3,6},{5,8},{7,10},{9,12},{11,14},{13,16},{15,18},{17,20},{1... | collective-permute-start | bytes 688136 | tf_op jit(solution)/shard_map/ppermute | solution.py:23
  54.5 4.7 %shard_map.56 = (bf16[12,128,128]{2,1,0:T(8,128)(2,1)S(1)}, bf16[12,128,128]{2,1,0:T(8,128)(2,1)S(1)}) custom-call(bf16[4,12,32,128]{3,2,1,0:T(8,128)(2,1)S(1)} %slice_bitcast_fusion.2.refs_0_.refs_4_, bf16[4,12,32,128]{3,2,1,0:T(8,128)(2,1)S(1)} %collective-permute-done.5.refs_1_.refs_5_, ...), custom_call_target="tpu_custom_call" | custom-call | flops 5435817984 | bytes 2097152 | tf_op jit(solution)/shard_map/pallas_call | solution.py:147
  59.2 1.4 %collective-permute-start.17 = (bf16[12,128,128]{2,1,0:T(8,128)(2,1)S(1)}, bf16[12,128,128]{2,1,0:T(8,128)(2,1)S(1)}, u32[]{:S(2)}, u32[]{:S(2)}) collective-permute-start(bf16[12,128,128]{2,1,0:T(8,128)(2,1)S(1)} %get-tuple-element.140.refs_2_.refs_6_), channel_id=1, source_target_pairs={{0,1},{1,0},{2,3},{3,2},{4,5},{5,4},{6,7},{7,6},{8,9},{9,8},{10,11... | collective-permute-start | bytes 1179656 | tf_op jit(solution)/shard_map/ppermute | solution.py:17
  60.7 1.9 %collective-permute-start.16 = (bf16[12,128,128]{2,1,0:T(8,128)(2,1)S(1)}, bf16[12,128,128]{2,1,0:T(8,128)(2,1)S(1)}, u32[]{:S(2)}, u32[]{:S(2)}) collective-permute-start(bf16[12,128,128]{2,1,0:T(8,128)(2,1)S(1)} %get-tuple-element.139.refs_1_.refs_5_), channel_id=1, source_target_pairs={{1,4},{3,6},{5,8},{7,10},{9,12},{11,14},{13,16},{15,18},{17,20},{1... | collective-permute-start | bytes 1179656 | tf_op jit(solution)/shard_map/ppermute | solution.py:23
  62.6 1.3 %collective-permute-done.9.refs_0_.refs_4_ = bf16[12,128,128]{2,1,0:T(8,128)(2,1)S(1)} collective-permute-done((bf16[12,128,128]{2,1,0:T(8,128)(2,1)S(1)}, bf16[12,128,128]{2,1,0:T(8,128)(2,1)S(1)}, u32[]{:S(2)}, u32[]{:S(2)}) %collective-permute-start.9) | collective-permute-done | bytes 393248 | tf_op jit(solution)/shard_map/ppermute | solution.py:23
  64.9 5.0 %shard_map.58 = (bf16[2,11,32,128]{3,2,1,0:T(8,128)(2,1)S(1)}, bf16[2,11,32,128]{3,2,1,0:T(8,128)(2,1)S(1)}, bf16[2,2,11,32,128]{4,3,2,1,0:T(8,128)(2,1)S(1)}) custom-call(bf16[12,128,128]{2,1,0:T(8,128)(2,1)S(1)} %collective-permute-done.9.refs_0_.refs_4_, bf16[12,128,128]{2,1,0:T(8,128)(2,1)S(1)} %get-tuple-element.143.refs_1_.refs_5_, ...), custom_call_target="tpu_custom_call" | custom-call | flops 4982833152 | bytes 2097152 | tf_op jit(solution)/shard_map/pallas_call | solution.py:147
  69.8 1.3 %collective-permute-start.21 = (bf16[2,2,11,32,128]{4,3,2,1,0:T(8,128)(2,1)S(1)}, bf16[2,2,11,32,128]{4,3,2,1,0:T(8,128)(2,1)S(1)}, u32[]{:S(2)}, u32[]{:S(2)}) collective-permute-start(bf16[2,2,11,32,128]{4,3,2,1,0:T(8,128)(2,1)S(1)} %get-tuple-element.157), channel_id=1, source_target_pairs={{0,2},{1,3},{2,0},{3,1},{4,6},{5,7},{6,4},{7,5},{8,10},{9,11},{10,... | collective-permute-start | bytes 1081352 | tf_op jit(solution)/shard_map/ppermute | solution.py:17
  71.1 3.6 %shard_map.59 = (bf16[8,128,128]{2,1,0:T(8,128)(2,1)S(1)}, bf16[8,128,128]{2,1,0:T(8,128)(2,1)S(1)}) custom-call(bf16[4,7,32,128]{3,2,1,0:T(8,128)(2,1)S(1)} %slice_bitcast_fusion.5.refs_0_, bf16[4,7,32,128]{3,2,1,0:T(8,128)(2,1)S(1)} %collective-permute-done.12.refs_1_, bf16[2,3,7,32,128]{4,3,2,1,0:T(8,128)(2,1)S(1)} %collective-permute-done.14.refs_2_, ...), custom_call_target="tpu_custom_call" | custom-call | flops 3623878656 | bytes 2097152 | tf_op jit(solution)/shard_map/pallas_call | solution.py:147
  74.8 2.8 %collective-permute-start.19 = (bf16[8,128,128]{2,1,0:T(8,128)(2,1)S(1)}, bf16[8,128,128]{2,1,0:T(8,128)(2,1)S(1)}, u32[]{:S(2)}, u32[]{:S(2)}) collective-permute-start(bf16[8,128,128]{2,1,0:T(8,128)(2,1)S(1)} %get-tuple-element.159.refs_1_), channel_id=1, source_target_pairs={{1,4},{3,6},{5,8},{7,10},{9,12},{11,14},{13,16},{15,18},{17,20},{1... | collective-permute-start | bytes 786440 | tf_op jit(solution)/shard_map/ppermute | solution.py:23
  77.7 2.4 %collective-permute-done.21 = bf16[2,2,11,32,128]{4,3,2,1,0:T(8,128)(2,1)S(1)} collective-permute-done((bf16[2,2,11,32,128]{4,3,2,1,0:T(8,128)(2,1)S(1)}, bf16[2,2,11,32,128]{4,3,2,1,0:T(8,128)(2,1)S(1)}, u32[]{:S(2)}, u32[]{:S(2)}) %collective-permute-start.21) | collective-permute-done | bytes 360480 | tf_op jit(solution)/shard_map/ppermute | solution.py:17
  80.9 5.3 %shard_map.60 = (bf16[2,12,32,128]{3,2,1,0:T(8,128)(2,1)S(1)}, bf16[2,12,32,128]{3,2,1,0:T(8,128)(2,1)S(1)}, bf16[2,2,12,32,128]{4,3,2,1,0:T(8,128)(2,1)S(1)}) custom-call(bf16[12,128,128]{2,1,0:T(8,128)(2,1)S(1)} %collective-permute-done.16.refs_0_.refs_4_, bf16[12,128,128]{2,1,0:T(8,128)(2,1)S(1)} %get-tuple-element.139.refs_1_.refs_5_, ...), custom_call_target="tpu_custom_call" | custom-call | flops 5435817984 | bytes 2097152 | tf_op jit(solution)/shard_map/pallas_call | solution.py:147
  86.2 1.3 %collective-permute-start.23 = (bf16[2,2,12,32,128]{4,3,2,1,0:T(8,128)(2,1)S(1)}, bf16[2,2,12,32,128]{4,3,2,1,0:T(8,128)(2,1)S(1)}, u32[]{:S(2)}, u32[]{:S(2)}) collective-permute-start(bf16[2,2,12,32,128]{4,3,2,1,0:T(8,128)(2,1)S(1)} %get-tuple-element.168), channel_id=1, source_target_pairs={{0,2},{1,3},{2,0},{3,1},{4,6},{5,7},{6,4},{7,5},{8,10},{9,11},{10,... | collective-permute-start | bytes 1179656 | tf_op jit(solution)/shard_map/ppermute | solution.py:17
  87.5 3.7 %shard_map.61 = (bf16[2,9,32,128]{3,2,1,0:T(8,128)(2,1)S(1)}, bf16[2,9,32,128]{3,2,1,0:T(8,128)(2,1)S(1)}, bf16[2,9,32,128]{3,2,1,0:T(8,128)(2,1)S(1)}, bf16[2,9,32,128]{3,2,1,0:T(8,128)(2,1)S(1)}) custom-call(bf16[8,128,128]{2,1,0:T(8,128)(2,1)S(1)} %collective-permute-done.19.refs_0_, bf16[8,128,128]{2,1,0:T(8,128)(2,1)S(1)} %get-tuple-element.159.refs_1_, ...), custom_call_target="tpu_custom_call" | custom-call | flops 4076863488 | bytes 2097152 | tf_op jit(solution)/shard_map/pallas_call | solution.py:147
  91.6 5.4 %collective-permute-done.23 = bf16[2,2,12,32,128]{4,3,2,1,0:T(8,128)(2,1)S(1)} collective-permute-done((bf16[2,2,12,32,128]{4,3,2,1,0:T(8,128)(2,1)S(1)}, bf16[2,2,12,32,128]{4,3,2,1,0:T(8,128)(2,1)S(1)}, u32[]{:S(2)}, u32[]{:S(2)}) %collective-permute-start.23) | collective-permute-done | bytes 393248 | tf_op jit(solution)/shard_map/ppermute | solution.py:17
  98.0 1.2 %collective-permute-start.26 = (bf16[2,9,32,128]{3,2,1,0:T(8,128)(2,1)S(1)}, bf16[2,9,32,128]{3,2,1,0:T(8,128)(2,1)S(1)}, u32[]{:S(2)}, u32[]{:S(2)}) collective-permute-start(bf16[2,9,32,128]{3,2,1,0:T(8,128)(2,1)S(1)} %get-tuple-element.171), channel_id=1, source_target_pairs={{0,2},{1,3},{2,0},{3,1},{4,6},{5,7},{6,4},{7,5},{8,10},{9,11},{10,... | collective-permute-start | bytes 442376 | tf_op jit(solution)/shard_map/ppermute | solution.py:17
  99.7 3.7 %collective-permute-done.26 = bf16[2,9,32,128]{3,2,1,0:T(8,128)(2,1)S(1)} collective-permute-done((bf16[2,9,32,128]{3,2,1,0:T(8,128)(2,1)S(1)}, bf16[2,9,32,128]{3,2,1,0:T(8,128)(2,1)S(1)}, u32[]{:S(2)}, u32[]{:S(2)}) %collective-permute-start.26) | collective-permute-done | bytes 147488 | tf_op jit(solution)/shard_map/ppermute | solution.py:17
  103.7 3.0 %collective-permute-done.27 = bf16[2,9,32,128]{3,2,1,0:T(8,128)(2,1)S(1)} collective-permute-done((bf16[2,9,32,128]{3,2,1,0:T(8,128)(2,1)S(1)}, bf16[2,9,32,128]{3,2,1,0:T(8,128)(2,1)S(1)}, u32[]{:S(2)}, u32[]{:S(2)}) %collective-permute-start.27) | collective-permute-done | bytes 147488 | tf_op jit(solution)/shard_map/ppermute | solution.py:17
  107.3 2.1 %copy.9 = bf16[2,4,32,32,128]{4,3,2,1,0:T(8,128)(2,1)} copy(bf16[2,4,32,32,128]{4,2,3,1,0:T(8,128)(2,1)S(1)} %fusion) | data formatting | bytes 4194304 | tf_op jit(solution)/shard_map/transpose | solution.py:271
  (109 shorter events, 15.7 us)
Async XLA Ops:
  1.9 10.8 %collective-permute-start = (bf16[4,13,32,128]{3,2,1,0:T(8,128)(2,1)S(1)}, bf16[4,13,32,128]{3,2,1,0:T(8,128)(2,1)S(1)}, u32[]{:S(2)}, u32[]{:S(2)}) collective-permute-start(bf16[4,13,32,128]{3,2,1,0:T(8,128)(2,1)S(1)} %slice_bitcast_fusion.1), channel_id=1, source_target_pairs={{0,2},{1,3},{2,0},{3,1},{4,6},{5,7},{6,4},{7,5},{8,10},{9,11},{10,... | collective-permute-start | bytes 1277960 | tf_op jit(solution)/shard_map/ppermute | solution.py:17
  3.2 4.1 %collective-permute-start.1 = (f32[2,32]{1,0:T(2,128)S(1)}, f32[2,32]{1,0:T(2,128)S(1)}, u32[]{:S(2)}, u32[]{:S(2)}) collective-permute-start(f32[2,32]{1,0:T(2,128)S(1)} %pad_maximum_fusion.10), channel_id=1, source_target_pairs={{0,1},{1,0},{2,3},{3,2},{4,5},{5,4},{6,7},{7,6},{8,9},{9,8},{10,11... | collective-permute-start | bytes 776 | tf_op jit(solution)/shard_map/ppermute | solution.py:17
  7.4 5.3 %collective-permute-start.2 = (f32[2,64]{1,0:T(2,128)S(1)}, f32[2,64]{1,0:T(2,128)S(1)}, u32[]{:S(2)}, u32[]{:S(2)}) collective-permute-start(f32[2,64]{1,0:T(2,128)S(1)} %pad_maximum_fusion.11), channel_id=1, source_target_pairs={{0,2},{1,3},{2,0},{3,1},{4,6},{5,7},{6,4},{7,5},{8,10},{9,11},{10,... | collective-permute-start | bytes 1544 | tf_op jit(solution)/shard_map/ppermute | solution.py:17
  7.7 6.9 %copy-start.4 = (bf16[4,32,32,128]{3,1,2,0:T(8,128)(2,1)S(1)}, bf16[4,32,32,128]{3,1,2,0:T(8,128)(2,1)}, u32[]{:S(2)}) copy-start(bf16[4,32,32,128]{3,1,2,0:T(8,128)(2,1)} %copy-done.3) | copy-start | bytes 3145732
  12.9 7.8 %copy-start.1 = (bf16[3,3,3,128,32]{3,4,2,1,0:T(8,128)(2,1)S(1)}, bf16[3,3,3,128,32]{3,4,2,1,0:T(8,128)(2,1)}, u32[]{:S(2)}) copy-start(bf16[3,3,3,128,32]{3,4,2,1,0:T(8,128)(2,1)} %param.6) | copy-start | bytes 663556
  12.9 3.4 %collective-permute-start.3 = (bf16[2,3,13,32,128]{4,3,2,1,0:T(8,128)(2,1)S(1)}, bf16[2,3,13,32,128]{4,3,2,1,0:T(8,128)(2,1)S(1)}, u32[]{:S(2)}, u32[]{:S(2)}) collective-permute-start(bf16[2,3,13,32,128]{4,3,2,1,0:T(8,128)(2,1)S(1)} %pad_maximum_fusion), channel_id=1, source_target_pairs={{0,1},{1,0},{2,3},{3,2},{4,5},{5,4},{6,7},{7,6},{8,9},{9,8},{10,11... | collective-permute-start | bytes 1916936 | tf_op jit(solution)/shard_map/ppermute | solution.py:17
  14.6 15.7 %collective-permute-start.5 = (bf16[4,12,32,128]{3,2,1,0:T(8,128)(2,1)}, bf16[4,12,32,128]{3,2,1,0:T(8,128)(2,1)S(1)}, u32[]{:S(2)}, u32[]{:S(2)}) collective-permute-start(bf16[4,12,32,128]{3,2,1,0:T(8,128)(2,1)} %slice_bitcast_fusion.3), channel_id=1, source_target_pairs={{0,2},{1,3},{2,0},{3,1},{4,6},{5,7},{6,4},{7,5},{8,10},{9,11},{10,... | collective-permute-start | bytes 1179656 | tf_op jit(solution)/shard_map/ppermute | solution.py:17
  16.3 15.5 %copy-start = (bf16[3,3,3,32,128]{4,3,2,1,0:T(8,128)(2,1)S(1)}, bf16[3,3,3,32,128]{4,3,2,1,0:T(8,128)(2,1)}, u32[]{:S(2)}) copy-start(bf16[3,3,3,32,128]{4,3,2,1,0:T(8,128)(2,1)} %param.8) | copy-start | bytes 663556
  17.2 14.2 %collective-permute-start.4 = (bf16[4,13,32,128]{3,2,1,0:T(8,128)(2,1)}, bf16[4,13,32,128]{3,2,1,0:T(8,128)(2,1)S(1)}, u32[]{:S(2)}, u32[]{:S(2)}) collective-permute-start(bf16[4,13,32,128]{3,2,1,0:T(8,128)(2,1)} %pad_maximum_fusion.4), channel_id=1, source_target_pairs={{1,4},{3,6},{5,8},{7,10},{9,12},{11,14},{13,16},{15,18},{17,20},{1... | collective-permute-start | bytes 1277960 | tf_op jit(solution)/shard_map/ppermute | solution.py:23
  20.7 12.4 %copy-start.5 = (bf16[4,7,32,128]{3,2,1,0:T(8,128)(2,1)S(1)}, bf16[4,7,32,128]{3,2,1,0:T(8,128)(2,1)}, u32[]{:S(2)}) copy-start(bf16[4,7,32,128]{3,2,1,0:T(8,128)(2,1)} %slice_bitcast_fusion.4) | copy-start | bytes 688132
  20.7 9.6 %collective-permute-start.6 = (bf16[27,32,128]{2,1,0:T(8,128)(2,1)S(1)}, bf16[27,32,128]{2,1,0:T(8,128)(2,1)S(1)}, u32[]{:S(2)}, u32[]{:S(2)}) collective-permute-start(bf16[27,32,128]{2,1,0:T(8,128)(2,1)S(1)} %bitcast.90), channel_id=1, source_target_pairs={{0,2},{1,3},{2,0},{3,1},{4,6},{5,7},{6,4},{7,5},{8,10},{9,11},{10,... | collective-permute-start | bytes 663560 | tf_op jit(solution)/shard_map/ppermute | solution.py:17
  31.7 2.8 %collective-permute-start.7 = (bf16[2,3,12,32,128]{4,3,2,1,0:T(8,128)(2,1)S(1)}, bf16[2,3,12,32,128]{4,3,2,1,0:T(8,128)(2,1)S(1)}, u32[]{:S(2)}, u32[]{:S(2)}) collective-permute-start(bf16[2,3,12,32,128]{4,3,2,1,0:T(8,128)(2,1)S(1)} %pad_maximum_fusion.1), channel_id=1, source_target_pairs={{0,1},{1,0},{2,3},{3,2},{4,5},{5,4},{6,7},{7,6},{8,9},{9,8},{10,11... | collective-permute-start | bytes 1769480 | tf_op jit(solution)/shard_map/ppermute | solution.py:17
  31.8 9.9 %collective-permute-start.13 = (bf16[27,32,128]{2,1,0:T(8,128)(2,1)S(1)}, bf16[27,32,128]{2,1,0:T(8,128)(2,1)S(1)}, u32[]{:S(2)}, u32[]{:S(2)}) collective-permute-start(bf16[27,32,128]{2,1,0:T(8,128)(2,1)S(1)} %bitcast.87), channel_id=1, source_target_pairs={{0,2},{1,3},{2,0},{3,1},{4,6},{5,7},{6,4},{7,5},{8,10},{9,11},{10,... | collective-permute-start | bytes 663560 | tf_op jit(solution)/shard_map/ppermute | solution.py:17
  33.1 10.3 %collective-permute-start.12 = (bf16[4,7,32,128]{3,2,1,0:T(8,128)(2,1)S(1)}, bf16[4,7,32,128]{3,2,1,0:T(8,128)(2,1)S(1)}, u32[]{:S(2)}, u32[]{:S(2)}) collective-permute-start(bf16[4,7,32,128]{3,2,1,0:T(8,128)(2,1)S(1)} %copy-done.5), channel_id=1, source_target_pairs={{0,2},{1,3},{2,0},{3,1},{4,6},{5,7},{6,4},{7,5},{8,10},{9,11},{10,... | collective-permute-start | bytes 688136 | tf_op jit(solution)/shard_map/ppermute | solution.py:17
  33.4 3.7 %collective-permute-start.8 = (bf16[2,27,32,128]{3,2,1,0:T(8,128)(2,1)S(1)}, bf16[2,27,32,128]{3,2,1,0:T(8,128)(2,1)S(1)}, u32[]{:S(2)}, u32[]{:S(2)}) collective-permute-start(bf16[2,27,32,128]{3,2,1,0:T(8,128)(2,1)S(1)} %pad_maximum_fusion.2), channel_id=1, source_target_pairs={{0,1},{1,0},{2,3},{3,2},{4,5},{5,4},{6,7},{7,6},{8,9},{9,8},{10,11... | collective-permute-start | bytes 1327112 | tf_op jit(solution)/shard_map/ppermute | solution.py:17
  34.7 13.3 %collective-permute-start.11 = (bf16[4,12,32,128]{3,2,1,0:T(8,128)(2,1)S(1)}, bf16[4,12,32,128]{3,2,1,0:T(8,128)(2,1)S(1)}, u32[]{:S(2)}, u32[]{:S(2)}) collective-permute-start(bf16[4,12,32,128]{3,2,1,0:T(8,128)(2,1)S(1)} %pad_maximum_fusion.5), channel_id=1, source_target_pairs={{1,4},{3,6},{5,8},{7,10},{9,12},{11,14},{13,16},{15,18},{17,20},{1... | collective-permute-start | bytes 1179656 | tf_op jit(solution)/shard_map/ppermute | solution.py:23
  48.0 3.7 %collective-permute-start.14 = (bf16[2,3,7,32,128]{4,3,2,1,0:T(8,128)(2,1)S(1)}, bf16[2,3,7,32,128]{4,3,2,1,0:T(8,128)(2,1)S(1)}, u32[]{:S(2)}, u32[]{:S(2)}) collective-permute-start(bf16[2,3,7,32,128]{4,3,2,1,0:T(8,128)(2,1)S(1)} %pad_maximum_fusion.8), channel_id=1, source_target_pairs={{0,1},{1,0},{2,3},{3,2},{4,5},{5,4},{6,7},{7,6},{8,9},{9,8},{10,11... | collective-permute-start | bytes 1032200 | tf_op jit(solution)/shard_map/ppermute | solution.py:17
  48.1 15.8 %collective-permute-start.9 = (bf16[12,128,128]{2,1,0:T(8,128)(2,1)S(1)}, bf16[12,128,128]{2,1,0:T(8,128)(2,1)S(1)}, u32[]{:S(2)}, u32[]{:S(2)}) collective-permute-start(bf16[12,128,128]{2,1,0:T(8,128)(2,1)S(1)} %get-tuple-element.143.refs_1_.refs_5_), channel_id=1, source_target_pairs={{1,4},{3,6},{5,8},{7,10},{9,12},{11,14},{13,16},{15,18},{17,20},{1... | collective-permute-start | bytes 1179656 | tf_op jit(solution)/shard_map/ppermute | solution.py:23
  50.1 10.6 %collective-permute-start.10 = (bf16[12,128,128]{2,1,0:T(8,128)(2,1)S(1)}, bf16[12,128,128]{2,1,0:T(8,128)(2,1)S(1)}, u32[]{:S(2)}, u32[]{:S(2)}) collective-permute-start(bf16[12,128,128]{2,1,0:T(8,128)(2,1)S(1)} %get-tuple-element.144.refs_2_.refs_6_), channel_id=1, source_target_pairs={{0,1},{1,0},{2,3},{3,2},{4,5},{5,4},{6,7},{7,6},{8,9},{9,8},{10,11... | collective-permute-start | bytes 1179656 | tf_op jit(solution)/shard_map/ppermute | solution.py:17
  51.6 12.3 %collective-permute-start.15 = (bf16[2,27,32,128]{3,2,1,0:T(8,128)(2,1)S(1)}, bf16[2,27,32,128]{3,2,1,0:T(8,128)(2,1)S(1)}, u32[]{:S(2)}, u32[]{:S(2)}) collective-permute-start(bf16[2,27,32,128]{3,2,1,0:T(8,128)(2,1)S(1)} %pad_maximum_fusion.3), channel_id=1, source_target_pairs={{0,1},{1,0},{2,3},{3,2},{4,5},{5,4},{6,7},{7,6},{8,9},{9,8},{10,11... | collective-permute-start | bytes 1327112 | tf_op jit(solution)/shard_map/ppermute | solution.py:17
  51.9 19.3 %collective-permute-start.18 = (bf16[4,7,32,128]{3,2,1,0:T(8,128)(2,1)S(1)}, bf16[4,7,32,128]{3,2,1,0:T(8,128)(2,1)S(1)}, u32[]{:S(2)}, u32[]{:S(2)}) collective-permute-start(bf16[4,7,32,128]{3,2,1,0:T(8,128)(2,1)S(1)} %pad_maximum_fusion.9), channel_id=1, source_target_pairs={{1,4},{3,6},{5,8},{7,10},{9,12},{11,14},{13,16},{15,18},{17,20},{1... | collective-permute-start | bytes 688136 | tf_op jit(solution)/shard_map/ppermute | solution.py:23
  59.2 18.4 %collective-permute-start.17 = (bf16[12,128,128]{2,1,0:T(8,128)(2,1)S(1)}, bf16[12,128,128]{2,1,0:T(8,128)(2,1)S(1)}, u32[]{:S(2)}, u32[]{:S(2)}) collective-permute-start(bf16[12,128,128]{2,1,0:T(8,128)(2,1)S(1)} %get-tuple-element.140.refs_2_.refs_6_), channel_id=1, source_target_pairs={{0,1},{1,0},{2,3},{3,2},{4,5},{5,4},{6,7},{7,6},{8,9},{9,8},{10,11... | collective-permute-start | bytes 1179656 | tf_op jit(solution)/shard_map/ppermute | solution.py:17
  60.7 17.0 %collective-permute-start.16 = (bf16[12,128,128]{2,1,0:T(8,128)(2,1)S(1)}, bf16[12,128,128]{2,1,0:T(8,128)(2,1)S(1)}, u32[]{:S(2)}, u32[]{:S(2)}) collective-permute-start(bf16[12,128,128]{2,1,0:T(8,128)(2,1)S(1)} %get-tuple-element.139.refs_1_.refs_5_), channel_id=1, source_target_pairs={{1,4},{3,6},{5,8},{7,10},{9,12},{11,14},{13,16},{15,18},{17,20},{1... | collective-permute-start | bytes 1179656 | tf_op jit(solution)/shard_map/ppermute | solution.py:23
  69.8 10.3 %collective-permute-start.21 = (bf16[2,2,11,32,128]{4,3,2,1,0:T(8,128)(2,1)S(1)}, bf16[2,2,11,32,128]{4,3,2,1,0:T(8,128)(2,1)S(1)}, u32[]{:S(2)}, u32[]{:S(2)}) collective-permute-start(bf16[2,2,11,32,128]{4,3,2,1,0:T(8,128)(2,1)S(1)} %get-tuple-element.157), channel_id=1, source_target_pairs={{0,2},{1,3},{2,0},{3,1},{4,6},{5,7},{6,4},{7,5},{8,10},{9,11},{10,... | collective-permute-start | bytes 1081352 | tf_op jit(solution)/shard_map/ppermute | solution.py:17
  74.7 12.8 %collective-permute-start.20 = (bf16[8,128,128]{2,1,0:T(8,128)(2,1)S(1)}, bf16[8,128,128]{2,1,0:T(8,128)(2,1)S(1)}, u32[]{:S(2)}, u32[]{:S(2)}) collective-permute-start(bf16[8,128,128]{2,1,0:T(8,128)(2,1)S(1)} %get-tuple-element.160.refs_2_), channel_id=1, source_target_pairs={{0,1},{1,0},{2,3},{3,2},{4,5},{5,4},{6,7},{7,6},{8,9},{9,8},{10,11... | collective-permute-start | bytes 786440 | tf_op jit(solution)/shard_map/ppermute | solution.py:17
  74.8 12.7 %collective-permute-start.19 = (bf16[8,128,128]{2,1,0:T(8,128)(2,1)S(1)}, bf16[8,128,128]{2,1,0:T(8,128)(2,1)S(1)}, u32[]{:S(2)}, u32[]{:S(2)}) collective-permute-start(bf16[8,128,128]{2,1,0:T(8,128)(2,1)S(1)} %get-tuple-element.159.refs_1_), channel_id=1, source_target_pairs={{1,4},{3,6},{5,8},{7,10},{9,12},{11,14},{13,16},{15,18},{17,20},{1... | collective-permute-start | bytes 786440 | tf_op jit(solution)/shard_map/ppermute | solution.py:23
  80.2 7.3 %collective-permute-start.22 = (bf16[2,2,11,32,128]{4,3,2,1,0:T(8,128)(2,1)S(1)}, bf16[2,2,11,32,128]{4,3,2,1,0:T(8,128)(2,1)S(1)}, u32[]{:S(2)}, u32[]{:S(2)}) collective-permute-start(bf16[2,2,11,32,128]{4,3,2,1,0:T(8,128)(2,1)S(1)} %pad_maximum_fusion.7), channel_id=1, source_target_pairs={{0,1},{1,0},{2,3},{3,2},{4,5},{5,4},{6,7},{7,6},{8,9},{9,8},{10,11... | collective-permute-start | bytes 1081352 | tf_op jit(solution)/shard_map/ppermute | solution.py:17
  86.2 10.8 %collective-permute-start.23 = (bf16[2,2,12,32,128]{4,3,2,1,0:T(8,128)(2,1)S(1)}, bf16[2,2,12,32,128]{4,3,2,1,0:T(8,128)(2,1)S(1)}, u32[]{:S(2)}, u32[]{:S(2)}) collective-permute-start(bf16[2,2,12,32,128]{4,3,2,1,0:T(8,128)(2,1)S(1)} %get-tuple-element.168), channel_id=1, source_target_pairs={{0,2},{1,3},{2,0},{3,1},{4,6},{5,7},{6,4},{7,5},{8,10},{9,11},{10,... | collective-permute-start | bytes 1179656 | tf_op jit(solution)/shard_map/ppermute | solution.py:17
  91.2 5.9 %collective-permute-start.24 = (bf16[2,9,32,128]{3,2,1,0:T(8,128)(2,1)S(1)}, bf16[2,9,32,128]{3,2,1,0:T(8,128)(2,1)S(1)}, u32[]{:S(2)}, u32[]{:S(2)}) collective-permute-start(bf16[2,9,32,128]{3,2,1,0:T(8,128)(2,1)S(1)} %get-tuple-element.169), channel_id=1, source_target_pairs={{0,1},{1,0},{2,3},{3,2},{4,5},{5,4},{6,7},{7,6},{8,9},{9,8},{10,11... | collective-permute-start | bytes 442376 | tf_op jit(solution)/shard_map/ppermute | solution.py:17
  97.1 6.4 %collective-permute-start.25 = (bf16[2,2,12,32,128]{4,3,2,1,0:T(8,128)(2,1)S(1)}, bf16[2,2,12,32,128]{4,3,2,1,0:T(8,128)(2,1)S(1)}, u32[]{:S(2)}, u32[]{:S(2)}) collective-permute-start(bf16[2,2,12,32,128]{4,3,2,1,0:T(8,128)(2,1)S(1)} %pad_maximum_fusion.6), channel_id=1, source_target_pairs={{0,1},{1,0},{2,3},{3,2},{4,5},{5,4},{6,7},{7,6},{8,9},{9,8},{10,11... | collective-permute-start | bytes 1179656 | tf_op jit(solution)/shard_map/ppermute | solution.py:17
  98.0 5.4 %collective-permute-start.26 = (bf16[2,9,32,128]{3,2,1,0:T(8,128)(2,1)S(1)}, bf16[2,9,32,128]{3,2,1,0:T(8,128)(2,1)S(1)}, u32[]{:S(2)}, u32[]{:S(2)}) collective-permute-start(bf16[2,9,32,128]{3,2,1,0:T(8,128)(2,1)S(1)} %get-tuple-element.171), channel_id=1, source_target_pairs={{0,2},{1,3},{2,0},{3,1},{4,6},{5,7},{6,4},{7,5},{8,10},{9,11},{10,... | collective-permute-start | bytes 442376 | tf_op jit(solution)/shard_map/ppermute | solution.py:17
  99.2 7.5 %collective-permute-start.27 = (bf16[2,9,32,128]{3,2,1,0:T(8,128)(2,1)S(1)}, bf16[2,9,32,128]{3,2,1,0:T(8,128)(2,1)S(1)}, u32[]{:S(2)}, u32[]{:S(2)}) collective-permute-start(bf16[2,9,32,128]{3,2,1,0:T(8,128)(2,1)S(1)} %get-tuple-element.172), channel_id=1, source_target_pairs={{0,3},{1,2},{2,1},{3,0},{4,7},{5,6},{6,5},{7,4},{8,11},{9,10},{10,... | collective-permute-start | bytes 442376 | tf_op jit(solution)/shard_map/ppermute | solution.py:17
  (4 other events, 11.7 us)
